TPU v7x, 32 devices: a whole 2x2x4 slice. The times are simulated.
32 devices in a mesh: grp: 4 (over z), sub: 8 (over y, x, core).
Axes of the slice: x: 2, y: 2, z: 4, core: 2. Of those that a mesh axis runs over, the one named last changes fastest.
Arguments:
- jump_data: float32 [4, 8, 256, 512], P('grp', 'sub'), as said below
- dual_block: float32 [4, 8, 512, 512], P('grp', 'sub'), as said below
- dirichlet_block: float32 [4, 8, 512, 512], P('grp', 'sub'), as said below
- coupling: float32 [4, 8, 512, 24], P('grp', 'sub'), may hold values from -0.25 to 0.25
- corner_weight: float32 [4, 8, 24], P('grp', 'sub'), may hold values from 0.2 to 2
- corner_rows: int32 [4, 8, 24], P('grp', 'sub'), may hold values from 0 to 47
- membership: int32 [4, 8], P('grp', 'sub'), may hold values from 0 to 3
- face_pairing: int32 [4, 8, 2, 128], P('grp', 'sub'), may hold values from 0 to 127, each once within a row
- block_pattern: int32 [4, 8, 4, 4], P('grp', 'sub'), may hold values from 0 to 1, as said below
Outputs:
- solution: float32 [4, 8, 256, 512], P('grp', 'sub')
- residual: float32 [4, 8, 256, 512], P('grp', 'sub')
Inputs may be any that keep to these rules, and one draw needn't show every extreme that they name: `jump_data`: the scale of one load case's data tends to grow from the first device to the last. `dual_block`: symmetric and positive definite. `dirichlet_block`: symmetric and positive definite. `block_pattern`: symmetric 0/1 masks with ones on the diagonal; the number of kept blocks differs between subdomains. `corner_rows`: corner rows of a subdomain may repeat across subdomains of the same cluster. `membership`: cluster sizes differ within a group. `face_pairing`: each row is a permutation of 0 to 127.
All inputs are finite; a program needn't handle non-finite values.
Results may differ from a plain program's by a relative error of at most 0.0003.
Values sent between devices are 32-bit elements; how exact they have to be, the bound alone decides.
No kernel may reach another device: no remote copies, remote signals or barrier semaphores. Data moves between devices by JAX's collectives and lax.ppermute only.
A program may use at most 64 MiB of HBM per device.

v0:
```python
import jax
import jax.numpy as jnp
from jax import lax
from jax.sharding import PartitionSpec as P

ITERS = 2


highest = lax.Precision.HIGHEST


def from_behind(array, axis, by):
    peers = lax.axis_size(axis)
    return lax.ppermute(array, axis, [(i, (i + by) % peers) for i in range(peers)])


def matmul(first, second):
    return jnp.dot(first, second, precision=highest, preferred_element_type=jnp.float32)


def pair_table(pairing):
    width = pairing.shape[0]
    return (pairing[:, None] == jnp.arange(width, dtype=jnp.int32)[None, :]).astype(jnp.float32)


def column_sum(first, second):
    return jnp.sum(first * second, axis=0)


def residual_product(residual, search):
    return lax.psum(column_sum(residual, search), ("grp", "sub"))


def per_device(
    jump_data,
    dual_block,
    dirichlet_block,
    coupling,
    corner_weight,
    corner_rows,
    membership,
    face_pairing,
    block_pattern,
):
    face_size = face_pairing.shape[-1]
    left_table = pair_table(face_pairing[0, 0, 0])
    lower_table = pair_table(face_pairing[0, 0, 1])
    pattern = block_pattern[0, 0]
    coupling_local = coupling[0, 0]
    rows_local = corner_rows[0, 0]
    member_local = membership[0, 0]

    def spread_field(multipliers):
        right_part = multipliers[:face_size]
        upper_part = multipliers[face_size:]
        from_left = from_behind(right_part, "sub", 1)
        from_below = from_behind(upper_part, "grp", 1)
        return jnp.concatenate(
            [
                right_part,
                -matmul(left_table, from_left),
                upper_part,
                -matmul(lower_table, from_below),
            ],
            axis=0,
        )

    block_mask = jnp.repeat(jnp.repeat(pattern, face_size, axis=0), face_size, axis=1).astype(
        jnp.float32
    )
    dual_local = dual_block[0, 0] * block_mask
    dirichlet_local = dirichlet_block[0, 0] * block_mask
    rows_every, members_every = (
        lax.all_gather(corner_rows, "sub", axis=1, tiled=True),
        lax.all_gather(membership, "sub", axis=1, tiled=True),
    )
    weights_every = lax.all_gather(corner_weight, "sub", axis=1, tiled=True)
    same_cluster = (members_every[0] == member_local).astype(jnp.float32)
    same_row = (rows_every[0][:, :, None] == rows_local[None, None, :]).astype(jnp.float32)
    link_table = same_row * same_cluster[:, None, None]
    denominator = jnp.einsum("mij,mi->j", link_table, weights_every[0], precision=highest)[:, None]

    def coarse_apply(corner_values):
        totals = jnp.einsum(
            "ons,onf->sf",
            link_table,
            lax.all_gather(corner_values[None, None], "sub", axis=1, tiled=True)[0],
            precision=highest,
        )
        return totals / denominator

    def dual_local_apply(spread):
        local = matmul(dual_local, spread)
        coarse = coarse_apply(matmul(coupling_local.T, spread))
        return local + matmul(coupling_local, coarse)

    def collect_field(local):
        send_left = matmul(left_table.T, local[face_size : 2 * face_size])
        send_down = matmul(lower_table.T, local[3 * face_size :])
        from_right = from_behind(send_left, "sub", -1)
        from_above = from_behind(send_down, "grp", -1)
        return jnp.concatenate(
            [local[:face_size] - from_right, local[2 * face_size : 3 * face_size] - from_above],
            axis=0,
        )

    def precondition(multipliers):
        return collect_field(matmul(dirichlet_local, spread_field(multipliers)))

    residual = jump_data[0, 0]
    solution = jnp.zeros_like(residual)
    search = precondition(residual)
    direction = search
    gamma = residual_product(residual, search)
    for iteration in range(ITERS):
        image = collect_field(dual_local_apply(spread_field(direction)))
        alpha = gamma / lax.psum(column_sum(direction, image), ("grp", "sub"))
        solution = solution + alpha * direction
        residual = residual - alpha * image
        if iteration + 1 < ITERS:
            search = precondition(residual)
            gamma_next = residual_product(residual, search)
            direction = search + gamma_next / gamma * direction
            gamma = gamma_next
    return (solution[None, None], residual[None, None])


def solution(mesh):
    placed = (
        P("grp", "sub", None, None),
        P("grp", "sub", None, None),
        P("grp", "sub", None, None),
        P("grp", "sub", None, None),
        P("grp", "sub", None),
        P("grp", "sub", None),
        P("grp", "sub"),
        P("grp", "sub", None, None),
        P("grp", "sub", None, None),
    )
    return jax.shard_map(
        per_device,
        mesh=mesh,
        in_specs=placed,
        out_specs=(P("grp", "sub", None, None), P("grp", "sub", None, None)),
        check_vma=False,
    )
```

profile of v0, /device:TPU:0, one launch (start us, length us, event | category | flops | bytes accessed | tf_op | source)
XLA Modules:
  0.0 260.8 jit_solution(6972299311563135541)
XLA Ops:
  0.6 1.1 slice_bitcast_fusion.1
  2.2 2.6 %collective-permute-start.1 = (f32[128,512]{1,0:T(8,128)S(1)}, f32[128,512]{1,0:T(8,128)S(1)}, u32[]{:S(2)}, u32[]{:S(2)}) collective-permute-start(f32[128,512]{1,0:T(8,128)S(1)} %get-tuple-element.19), channel_id=1, source_target_pairs={{0,8},{8,16},{16,24},{24,0},{1,9},{9,17},{17,25},{25,1},{2,10},{10... | collective-permute-start | bytes 786440 | tf_op jit(solution)/shard_map/ppermute | solution.py:14
  4.9 4.3 %collective-permute-done = f32[128,512]{1,0:T(8,128)S(1)} collective-permute-done((f32[128,512]{1,0:T(8,128)S(1)}, f32[128,512]{1,0:T(8,128)S(1)}, u32[]{:S(2)}, u32[]{:S(2)}) %collective-permute-start) | collective-permute-done | bytes 262176 | tf_op jit(solution)/shard_map/ppermute | solution.py:14
  9.5 3.8 %collective-permute-done.1 = f32[128,512]{1,0:T(8,128)S(1)} collective-permute-done((f32[128,512]{1,0:T(8,128)S(1)}, f32[128,512]{1,0:T(8,128)S(1)}, u32[]{:S(2)}, u32[]{:S(2)}) %collective-permute-start.1) | collective-permute-done | bytes 262176 | tf_op jit(solution)/shard_map/ppermute | solution.py:14
  14.5 1.9 fusion.3
  17.2 2.5 collective-permute-start.2
  19.7 1.7 collective-permute-start.3
  22.1 0.6 copy-done.15
  23.3 0.7 bitcast_dynamic-update-slice_fusion
  24.0 6.9 %all-reduce = s32[8]{0:T(128)S(1)} all-reduce(s32[8]{0:T(128)S(1)} %bitcast_dynamic-update-slice_fusion), channel_id=1, replica_groups=mesh['grp'=4,'sub'=8] {'sub'}, use_global_device_ids=true, to_apply=%add | all-reduce | flops 8 | bytes 64
  30.9 0.7 copy-done.14
  31.5 8.4 %all_gather.18 = f32[1,8,24]{2,0,1:T(1,128)S(1)} all-gather(f32[1,1,24]{2,0,1:T(1,128)S(1)} %bitcast.120), channel_id=1, replica_groups=mesh['grp'=4,'sub'=8] {'sub'}, dimensions={1}, use_global_device_ids=true | all-gather | bytes 864 | tf_op jit(solution)/shard_map/all_gather | solution.py:77
  39.9 0.7 copy-done.11
  40.6 8.2 %all_gather.15 = s32[1,8,24]{2,0,1:T(1,128)S(1)} all-gather(s32[1,1,24]{2,0,1:T(1,128)S(1)} %bitcast.116), channel_id=1, replica_groups=mesh['grp'=4,'sub'=8] {'sub'}, dimensions={1}, use_global_device_ids=true | all-gather | bytes 864 | tf_op jit(solution)/shard_map/all_gather | solution.py:74
  49.9 5.8 %collective-permute-done.4 = f32[128,512]{1,0:T(8,128)S(1)} collective-permute-done((f32[128,512]{1,0:T(8,128)S(1)}, f32[128,512]{1,0:T(8,128)S(1)}, u32[]{:S(2)}, u32[]{:S(2)}) %collective-permute-start.4) | collective-permute-done | bytes 262176 | tf_op jit(solution)/shard_map/ppermute | solution.py:14
  56.0 4.2 %collective-permute-done.5 = f32[128,512]{1,0:T(8,128)S(1)} collective-permute-done((f32[128,512]{1,0:T(8,128)S(1)}, f32[128,512]{1,0:T(8,128)S(1)}, u32[]{:S(2)}, u32[]{:S(2)}) %collective-permute-start.5) | collective-permute-done | bytes 262176 | tf_op jit(solution)/shard_map/ppermute | solution.py:14
  60.5 0.7 convolution_bitcast_fusion.3
  61.1 9.2 %all-gather = f32[192,512]{1,0:T(8,128)S(1)} all-gather(f32[24,512]{1,0:T(8,128)S(1)} %convolution_bitcast_fusion.3), channel_id=2, replica_groups=mesh['grp'=4,'sub'=8] {'sub'}, dimensions={0}, use_global_device_ids=true | all-gather | bytes 442368 | tf_op jit(solution)/shard_map/all_gather | solution.py:87
  70.7 1.0 convolution_bitcast_fusion.1
  71.7 1.9 convolution_add_fusion
  74.4 1.5 collective-permute-start.6
  75.9 3.9 %collective-permute-done.6 = f32[128,512]{1,0:T(8,128)S(1)} collective-permute-done((f32[128,512]{1,0:T(8,128)S(1)}, f32[128,512]{1,0:T(8,128)S(1)}, u32[]{:S(2)}, u32[]{:S(2)}) %collective-permute-start.6) | collective-permute-done | bytes 262176 | tf_op jit(solution)/shard_map/ppermute | solution.py:14
  79.8 3.4 %collective-permute-done.7 = f32[128,512]{1,0:T(8,128)S(1)} collective-permute-done((f32[128,512]{1,0:T(8,128)S(1)}, f32[128,512]{1,0:T(8,128)S(1)}, u32[]{:S(2)}, u32[]{:S(2)}) %collective-permute-start.7) | collective-permute-done | bytes 262176 | tf_op jit(solution)/shard_map/ppermute | solution.py:14
  84.0 37.4 %all-reduce.1 = (f32[512]{0:T(512)S(1)}, f32[512]{0:T(512)S(1)}) all-reduce(f32[512]{0:T(512)S(1)} %get-tuple-element.3, f32[512]{0:T(512)S(1)} %get-tuple-element.2), channel_id=1, replica_groups=mesh['grp'=4,'sub'=8] {'grp','sub'}, use_global_device_ids=true, to_apply=%region_1.0 | all-reduce | flops 1024 | bytes 8192 | tf_op jit(solution)/shard_map/psum | solution.py:31
  121.4 1.0 bitcast_subtract_fusion
  122.6 2.6 collective-permute-start.9
  125.1 4.1 %collective-permute-done.8 = f32[128,512]{1,0:T(8,128)S(1)} collective-permute-done((f32[128,512]{1,0:T(8,128)S(1)}, f32[128,512]{1,0:T(8,128)S(1)}, u32[]{:S(2)}, u32[]{:S(2)}) %collective-permute-start.8) | collective-permute-done | bytes 262176 | tf_op jit(solution)/shard_map/ppermute | solution.py:14
  129.6 3.0 %collective-permute-done.9 = f32[128,512]{1,0:T(8,128)S(1)} collective-permute-done((f32[128,512]{1,0:T(8,128)S(1)}, f32[128,512]{1,0:T(8,128)S(1)}, u32[]{:S(2)}, u32[]{:S(2)}) %collective-permute-start.9) | collective-permute-done | bytes 262176 | tf_op jit(solution)/shard_map/ppermute | solution.py:14
  132.9 1.9 fusion.11
  135.6 1.9 collective-permute-start.10
  137.5 1.1 collective-permute-start.11
  138.5 2.8 %collective-permute-done.10 = f32[128,512]{1,0:T(8,128)S(1)} collective-permute-done((f32[128,512]{1,0:T(8,128)S(1)}, f32[128,512]{1,0:T(8,128)S(1)}, u32[]{:S(2)}, u32[]{:S(2)}) %collective-permute-start.10) | collective-permute-done | bytes 262176 | tf_op jit(solution)/shard_map/ppermute | solution.py:14
  141.3 3.6 %collective-permute-done.11 = f32[128,512]{1,0:T(8,128)S(1)} collective-permute-done((f32[128,512]{1,0:T(8,128)S(1)}, f32[128,512]{1,0:T(8,128)S(1)}, u32[]{:S(2)}, u32[]{:S(2)}) %collective-permute-start.11) | collective-permute-done | bytes 262176 | tf_op jit(solution)/shard_map/ppermute | solution.py:14
  145.0 0.7 copy-done.7
  145.9 39.4 %psum.30 = f32[512]{0:T(512)S(1)} all-reduce(f32[512]{0:T(512)S(1)} %multiply_reduce_fusion), channel_id=1, replica_groups=mesh['grp'=4,'sub'=8] {'grp','sub'}, use_global_device_ids=true, to_apply=%region_5.0 | all-reduce | flops 512 | bytes 4096 | tf_op jit(solution)/shard_map/psum | solution.py:31
  185.3 1.1 multiply_add_fusion
  186.5 1.8 collective-permute-start.13
  188.4 4.9 %collective-permute-done.12 = f32[128,512]{1,0:T(8,128)S(1)} collective-permute-done((f32[128,512]{1,0:T(8,128)S(1)}, f32[128,512]{1,0:T(8,128)S(1)}, u32[]{:S(2)}, u32[]{:S(2)}) %collective-permute-start.12) | collective-permute-done | bytes 262176 | tf_op jit(solution)/shard_map/ppermute | solution.py:14
  193.5 2.6 %collective-permute-done.13 = f32[128,512]{1,0:T(8,128)S(1)} collective-permute-done((f32[128,512]{1,0:T(8,128)S(1)}, f32[128,512]{1,0:T(8,128)S(1)}, u32[]{:S(2)}, u32[]{:S(2)}) %collective-permute-start.13) | collective-permute-done | bytes 262176 | tf_op jit(solution)/shard_map/ppermute | solution.py:14
  196.5 1.9 fusion.19
  198.4 0.7 convolution_bitcast_fusion.2
  199.0 11.3 %all-gather.1 = f32[192,512]{1,0:T(8,128)S(1)} all-gather(f32[24,512]{1,0:T(8,128)S(1)} %convolution_bitcast_fusion.2), channel_id=3, replica_groups=mesh['grp'=4,'sub'=8] {'sub'}, dimensions={0}, use_global_device_ids=true | all-gather | bytes 442368 | tf_op jit(solution)/shard_map/all_gather | solution.py:87
  210.7 1.1 fusion
  212.6 1.5 collective-permute-start.14
  214.0 3.9 %collective-permute-done.14 = f32[128,512]{1,0:T(8,128)S(1)} collective-permute-done((f32[128,512]{1,0:T(8,128)S(1)}, f32[128,512]{1,0:T(8,128)S(1)}, u32[]{:S(2)}, u32[]{:S(2)}) %collective-permute-start.14) | collective-permute-done | bytes 262176 | tf_op jit(solution)/shard_map/ppermute | solution.py:14
  217.9 3.4 %collective-permute-done.15 = f32[128,512]{1,0:T(8,128)S(1)} collective-permute-done((f32[128,512]{1,0:T(8,128)S(1)}, f32[128,512]{1,0:T(8,128)S(1)}, u32[]{:S(2)}, u32[]{:S(2)}) %collective-permute-start.15) | collective-permute-done | bytes 262176 | tf_op jit(solution)/shard_map/ppermute | solution.py:14
  221.6 37.9 %psum.31 = f32[512]{0:T(512)S(1)} all-reduce(f32[512]{0:T(512)S(1)} %fusion.20), channel_id=1, replica_groups=mesh['grp'=4,'sub'=8] {'grp','sub'}, use_global_device_ids=true, to_apply=%region_7.0 | all-reduce | flops 512 | bytes 4096 | tf_op jit(solution)/shard_map/psum | solution.py:117
  259.5 1.3 fusion.24
  (75 shorter events, 11.0 us)
Async XLA Ops:
  0.6 59.8 %copy-start = (f32[1,1,512,24]{2,3,1,0:T(8,128)S(1)}, f32[1,1,512,24]{2,3,1,0:T(8,128)}, u32[]{:S(2)}) copy-start(f32[1,1,512,24]{2,3,1,0:T(8,128)} %param.12) | copy-start | bytes 147460
  1.7 3.2 %copy-start.12 = (s32[1,1,4,4]{3,2,1,0:T(4,128)S(1)}, s32[1,1,4,4]{3,2,1,0:T(4,128)}, u32[]{:S(2)}) copy-start(s32[1,1,4,4]{3,2,1,0:T(4,128)} %param.17) | copy-start | bytes 196
  1.7 7.4 %collective-permute-start = (f32[128,512]{1,0:T(8,128)S(1)}, f32[128,512]{1,0:T(8,128)S(1)}, u32[]{:S(2)}, u32[]{:S(2)}) collective-permute-start(f32[128,512]{1,0:T(8,128)S(1)} %get-tuple-element.18), channel_id=1, source_target_pairs={{0,1},{1,2},{2,3},{3,4},{4,5},{5,6},{6,7},{7,0},{8,9},{9,10},{10,1... | collective-permute-start | bytes 786440 | tf_op jit(solution)/shard_map/ppermute | solution.py:14
  2.2 2.7 %copy-start.13 = (s32[1,1,2,128]{3,2,1,0:T(2,128)S(1)}, s32[1,1,2,128]{3,2,1,0:T(2,128)}, u32[]{:S(2)}) copy-start(s32[1,1,2,128]{3,2,1,0:T(2,128)} %param.16) | copy-start | bytes 3076
  2.2 11.0 %collective-permute-start.1 = (f32[128,512]{1,0:T(8,128)S(1)}, f32[128,512]{1,0:T(8,128)S(1)}, u32[]{:S(2)}, u32[]{:S(2)}) collective-permute-start(f32[128,512]{1,0:T(8,128)S(1)} %get-tuple-element.19), channel_id=1, source_target_pairs={{0,8},{8,16},{16,24},{24,0},{1,9},{9,17},{17,25},{25,1},{2,10},{10... | collective-permute-start | bytes 786440 | tf_op jit(solution)/shard_map/ppermute | solution.py:14
  13.3 1.2 copy-start.3
  17.2 31.6 %collective-permute-start.2 = (f32[128,512]{1,0:T(8,128)S(1)}, f32[128,512]{1,0:T(8,128)S(1)}, u32[]{:S(2)}, u32[]{:S(2)}) collective-permute-start(f32[128,512]{1,0:T(8,128)S(1)} %fusion.40), channel_id=1, source_target_pairs={{0,7},{1,0},{2,1},{3,2},{4,3},{5,4},{6,5},{7,6},{8,15},{9,8},{10,9... | collective-permute-start | bytes 786440 | tf_op jit(solution)/shard_map/ppermute | solution.py:14
  19.7 29.1 %collective-permute-start.3 = (f32[128,512]{1,0:T(8,128)S(1)}, f32[128,512]{1,0:T(8,128)S(1)}, u32[]{:S(2)}, u32[]{:S(2)}) collective-permute-start(f32[128,512]{1,0:T(8,128)S(1)} %fusion.38), channel_id=1, source_target_pairs={{0,24},{8,0},{16,8},{24,16},{1,25},{9,1},{17,9},{25,17},{2,26},{10... | collective-permute-start | bytes 786440 | tf_op jit(solution)/shard_map/ppermute | solution.py:14
  22.0 0.7 copy-start.15
  30.9 0.7 copy-start.14
  39.9 0.7 copy-start.11
  48.9 6.7 %collective-permute-start.4 = (f32[128,512]{1,0:T(8,128)S(1)}, f32[128,512]{1,0:T(8,128)S(1)}, u32[]{:S(2)}, u32[]{:S(2)}) collective-permute-start(f32[128,512]{1,0:T(8,128)S(1)} %get-tuple-element.12), channel_id=1, source_target_pairs={{0,1},{1,2},{2,3},{3,4},{4,5},{5,6},{6,7},{7,0},{8,9},{9,10},{10,1... | collective-permute-start | bytes 786440 | tf_op jit(solution)/shard_map/ppermute | solution.py:14
  49.3 10.9 %collective-permute-start.5 = (f32[128,512]{1,0:T(8,128)S(1)}, f32[128,512]{1,0:T(8,128)S(1)}, u32[]{:S(2)}, u32[]{:S(2)}) collective-permute-start(f32[128,512]{1,0:T(8,128)S(1)} %get-tuple-element.13), channel_id=1, source_target_pairs={{0,8},{8,16},{16,24},{24,0},{1,9},{9,17},{17,25},{25,1},{2,10},{10... | collective-permute-start | bytes 786440 | tf_op jit(solution)/shard_map/ppermute | solution.py:14
  61.1 10.6 %copy-start.2 = (f32[1,1,512,512]{3,2,1,0:T(8,128)S(1)}, f32[1,1,512,512]{3,2,1,0:T(8,128)}, u32[]{:S(2)}) copy-start(f32[1,1,512,512]{3,2,1,0:T(8,128)} %param.10) | copy-start | bytes 3145732
  74.4 8.9 %copy-start.1 = (f32[1,1,256,512]{3,2,1,0:T(8,128)S(1)}, f32[1,1,256,512]{3,2,1,0:T(8,128)}, u32[]{:S(2)}) copy-start(f32[1,1,256,512]{3,2,1,0:T(8,128)} %param.9) | copy-start | bytes 1572868
  74.4 5.4 %collective-permute-start.6 = (f32[128,512]{1,0:T(8,128)S(1)}, f32[128,512]{1,0:T(8,128)S(1)}, u32[]{:S(2)}, u32[]{:S(2)}) collective-permute-start(f32[128,512]{1,0:T(8,128)S(1)} %fusion.36), channel_id=1, source_target_pairs={{0,7},{1,0},{2,1},{3,2},{4,3},{5,4},{6,5},{7,6},{8,15},{9,8},{10,9... | collective-permute-start | bytes 786440 | tf_op jit(solution)/shard_map/ppermute | solution.py:14
  75.9 7.3 %collective-permute-start.7 = (f32[128,512]{1,0:T(8,128)S(1)}, f32[128,512]{1,0:T(8,128)S(1)}, u32[]{:S(2)}, u32[]{:S(2)}) collective-permute-start(f32[128,512]{1,0:T(8,128)S(1)} %fusion.34), channel_id=1, source_target_pairs={{0,24},{8,0},{16,8},{24,16},{1,25},{9,1},{17,9},{25,17},{2,26},{10... | collective-permute-start | bytes 786440 | tf_op jit(solution)/shard_map/ppermute | solution.py:14
  83.3 0.7 copy-start.5
  122.4 10.5 %copy-start.4 = (f32[1,1,512,512]{3,2,1,0:T(8,128)S(1)}, f32[1,1,512,512]{3,2,1,0:T(8,128)}, u32[]{:S(2)}) copy-start(f32[1,1,512,512]{3,2,1,0:T(8,128)} %param.11) | copy-start | bytes 3145732
  122.5 6.7 %collective-permute-start.8 = (f32[128,512]{1,0:T(8,128)S(1)}, f32[128,512]{1,0:T(8,128)S(1)}, u32[]{:S(2)}, u32[]{:S(2)}) collective-permute-start(f32[128,512]{1,0:T(8,128)S(1)} %get-tuple-element.16), channel_id=1, source_target_pairs={{0,1},{1,2},{2,3},{3,4},{4,5},{5,6},{6,7},{7,0},{8,9},{9,10},{10,1... | collective-permute-start | bytes 786440 | tf_op jit(solution)/shard_map/ppermute | solution.py:14
  122.6 10.0 %collective-permute-start.9 = (f32[128,512]{1,0:T(8,128)S(1)}, f32[128,512]{1,0:T(8,128)S(1)}, u32[]{:S(2)}, u32[]{:S(2)}) collective-permute-start(f32[128,512]{1,0:T(8,128)S(1)} %get-tuple-element.17), channel_id=1, source_target_pairs={{0,8},{8,16},{16,24},{24,0},{1,9},{9,17},{17,25},{25,1},{2,10},{10... | collective-permute-start | bytes 786440 | tf_op jit(solution)/shard_map/ppermute | solution.py:14
  135.6 5.8 %collective-permute-start.10 = (f32[128,512]{1,0:T(8,128)S(1)}, f32[128,512]{1,0:T(8,128)S(1)}, u32[]{:S(2)}, u32[]{:S(2)}) collective-permute-start(f32[128,512]{1,0:T(8,128)S(1)} %fusion.32), channel_id=1, source_target_pairs={{0,7},{1,0},{2,1},{3,2},{4,3},{5,4},{6,5},{7,6},{8,15},{9,8},{10,9... | collective-permute-start | bytes 786440 | tf_op jit(solution)/shard_map/ppermute | solution.py:14
  137.5 7.5 %collective-permute-start.11 = (f32[128,512]{1,0:T(8,128)S(1)}, f32[128,512]{1,0:T(8,128)S(1)}, u32[]{:S(2)}, u32[]{:S(2)}) collective-permute-start(f32[128,512]{1,0:T(8,128)S(1)} %fusion.30), channel_id=1, source_target_pairs={{0,24},{8,0},{16,8},{24,16},{1,25},{9,1},{17,9},{25,17},{2,26},{10... | collective-permute-start | bytes 786440 | tf_op jit(solution)/shard_map/ppermute | solution.py:14
  145.0 0.7 copy-start.7
  145.0 0.8 copy-start.9
  186.5 6.7 %collective-permute-start.12 = (f32[128,512]{1,0:T(8,128)S(1)}, f32[128,512]{1,0:T(8,128)S(1)}, u32[]{:S(2)}, u32[]{:S(2)}) collective-permute-start(f32[128,512]{1,0:T(8,128)S(1)} %get-tuple-element.14), channel_id=1, source_target_pairs={{0,1},{1,2},{2,3},{3,4},{4,5},{5,6},{6,7},{7,0},{8,9},{9,10},{10,1... | collective-permute-start | bytes 786440 | tf_op jit(solution)/shard_map/ppermute | solution.py:14
  186.5 9.6 %collective-permute-start.13 = (f32[128,512]{1,0:T(8,128)S(1)}, f32[128,512]{1,0:T(8,128)S(1)}, u32[]{:S(2)}, u32[]{:S(2)}) collective-permute-start(f32[128,512]{1,0:T(8,128)S(1)} %get-tuple-element.15), channel_id=1, source_target_pairs={{0,8},{8,16},{16,24},{24,0},{1,9},{9,17},{17,25},{25,1},{2,10},{10... | collective-permute-start | bytes 786440 | tf_op jit(solution)/shard_map/ppermute | solution.py:14
  212.6 5.4 %collective-permute-start.14 = (f32[128,512]{1,0:T(8,128)S(1)}, f32[128,512]{1,0:T(8,128)S(1)}, u32[]{:S(2)}, u32[]{:S(2)}) collective-permute-start(f32[128,512]{1,0:T(8,128)S(1)} %fusion.28), channel_id=1, source_target_pairs={{0,7},{1,0},{2,1},{3,2},{4,3},{5,4},{6,5},{7,6},{8,15},{9,8},{10,9... | collective-permute-start | bytes 786440 | tf_op jit(solution)/shard_map/ppermute | solution.py:14
  214.0 7.3 %collective-permute-start.15 = (f32[128,512]{1,0:T(8,128)S(1)}, f32[128,512]{1,0:T(8,128)S(1)}, u32[]{:S(2)}, u32[]{:S(2)}) collective-permute-start(f32[128,512]{1,0:T(8,128)S(1)} %fusion.26), channel_id=1, source_target_pairs={{0,24},{8,0},{16,8},{24,16},{1,25},{9,1},{17,9},{25,17},{2,26},{10... | collective-permute-start | bytes 786440 | tf_op jit(solution)/shard_map/ppermute | solution.py:14
  221.4 38.0 %copy-start.6 = (f32[128,512]{1,0:T(8,128)S(1)}, f32[128,512]{1,0:T(8,128)}, u32[]{:S(2)}) copy-start(f32[128,512]{1,0:T(8,128)} %copy-done.5) | copy-start | bytes 786436
  221.4 38.0 %copy-start.8 = (f32[128,512]{1,0:T(8,128)S(1)}, f32[128,512]{1,0:T(8,128)}, u32[]{:S(2)}) copy-start(f32[128,512]{1,0:T(8,128)} %copy-done.7) | copy-start | bytes 786436
  221.5 38.0 %copy-start.10 = (f32[128,512]{1,0:T(8,128)S(1)}, f32[128,512]{1,0:T(8,128)}, u32[]{:S(2)}) copy-start(f32[128,512]{1,0:T(8,128)} %copy-done.9) | copy-start | bytes 786436
where the time goes:
time: 261 us
  blocking collectives  159 us (61%)
  waiting for transfers between devices  53.6 us (21%)
  starting transfers between devices  18.5 us (7%)
  matrix products  17.6 us (7%)
  local copies, waits for them, and re-layouts  6.6 us (3%)
  other arithmetic  4.21 us (2%)
    psum x2, blocking collectives, residual_product(): return lax.psum(column_sum(residual, search), ('grp', 'sub'))  76.7 us
    ppermute x16, waiting for transfers between devices, from_behind(): lax.ppermute(array, axis, [(i, (i + by) % peers) for i in range(peers)])  53.6 us
    psum x1, blocking collectives, per_device(): alpha = gamma / lax.psum(column_sum(direction, image), ('grp', 'sub'))  37.9 us
    all_gather x2, blocking collectives, coarse_apply(): lax.all_gather(corner_values[None, None], 'sub', axis=1, tiled=True)[0]  20.5 us
    ppermute x16, starting transfers between devices, from_behind(): lax.ppermute(array, axis, [(i, (i + by) % peers) for i in range(peers)])  18.5 us
    dot_general x24, matrix products, matmul(): jnp.dot(first, second, precision=highest, preferred_element_type=jnp.floa...  16.5 us
    all_gather x1, blocking collectives, per_device(): weights_every = lax.all_gather(corner_weight, 'sub', axis=1, tiled=True)  8.4 us
    all_gather x1, blocking collectives, per_device(): lax.all_gather(corner_rows, 'sub', axis=1, tiled=True)  8.2 us
  transfers between devices with their start and end apart: 16, of which 14 were waited for; matrix products, arithmetic and copies ran while one was open for 1% of the time, Pallas kernels for 0%

commit v1 on v0

v1 whole, which is shorter than its diff:
```python
import jax
import jax.numpy as jnp
from jax import lax
from jax.sharding import PartitionSpec as P

ITERS = 2

high = lax.Precision.HIGH
highest = lax.Precision.HIGHEST


def matmul(first, second, precision=high):
    return jnp.dot(first, second, precision=precision, preferred_element_type=jnp.float32)


def move(array, axis, target):
    peers = lax.axis_size(axis)
    return lax.ppermute(array, axis, [(i, target(i) % peers) for i in range(peers)])


def near(i):
    return i ^ 1


def far(i):
    return i - 1 if i % 2 == 0 else i + 1


def swap_edges(parts):
    return (
        move(parts[0], "sub", near),
        move(parts[1], "sub", far),
        move(parts[2], "grp", near),
        move(parts[3], "grp", far),
    )


def gather_members(array):
    peers = lax.axis_size("sub")
    same = [array] + [move(array, "sub", lambda i, k=k: i ^ k) for k in range(2, peers, 2)]
    same = jnp.concatenate(same, axis=0)
    return jnp.concatenate([same, move(same, "sub", near)], axis=0)


def sum_everywhere(array):
    for axis in ("sub", "grp"):
        step = 1
        while step < lax.axis_size(axis):
            array = array + move(array, axis, lambda i, k=step: i ^ k)
            step *= 2
    return array


def column_sum(first, second):
    return jnp.sum(first * second, axis=0)


def per_device(
    jump_data,
    dual_block,
    dirichlet_block,
    coupling,
    corner_weight,
    corner_rows,
    membership,
    face_pairing,
    block_pattern,
):
    face = face_pairing.shape[-1]
    corners = corner_rows.shape[-1]
    pattern = block_pattern[0, 0]
    odd_sub = lax.axis_index("sub") % 2 == 1
    odd_grp = lax.axis_index("grp") % 2 == 1

    identity = jnp.eye(face, dtype=jnp.float32)
    nothing = jnp.zeros((face, face), jnp.float32)

    def pair_table(pairing):
        return (pairing[:, None] == jnp.arange(face, dtype=jnp.int32)[None, :]).astype(jnp.float32)

    def turn(pairing, odd):
        table = -pair_table(pairing)
        first = jnp.concatenate([jnp.where(odd, nothing, identity), jnp.where(odd, identity, nothing)], 1)
        second = jnp.concatenate([jnp.where(odd, table, nothing), jnp.where(odd, nothing, table)], 1)
        return jnp.concatenate([first, second], 0)

    turn_sub = turn(face_pairing[0, 0, 0], odd_sub)
    turn_grp = turn(face_pairing[0, 0, 1], odd_grp)
    blank = jnp.zeros_like(turn_sub)
    turning = jnp.concatenate(
        [jnp.concatenate([turn_sub, blank], 1), jnp.concatenate([blank, turn_grp], 1)], 0
    )

    jump = jump_data[0, 0]
    right, upper = jump[:face], jump[face:]
    from_left = move(right, "sub", lambda i: i + 1)
    from_below = move(upper, "grp", lambda i: i + 1)

    block_mask = jnp.repeat(jnp.repeat(pattern, face, axis=0), face, axis=1).astype(jnp.float32)

    def turned(block):
        return matmul(turning.T, matmul(block * block_mask, turning))

    dirichlet_local = turned(dirichlet_block[0, 0])
    dual_local = turned(dual_block[0, 0])
    coupling_local = matmul(turning.T, coupling[0, 0])

    label = jnp.concatenate(
        [
            corner_weight[0, 0],
            corner_rows[0, 0].astype(jnp.float32),
            jnp.broadcast_to(membership[0, 0].astype(jnp.float32), (corners,)),
        ]
    ).reshape(1, 3, corners)
    labels = gather_members(label)
    weights_every, rows_every, members_every = (labels[:, i].reshape(-1) for i in range(3))
    link_table = (
        (rows_every[None, :] == rows_every[:corners, None])
        & (members_every[None, :] == members_every[:corners, None])
    ).astype(jnp.float32)
    denominator = matmul(link_table, weights_every[:, None], highest)
    coarse_table = matmul(coupling_local, link_table / denominator)

    def slots(array):
        return tuple(array[i * face : (i + 1) * face] for i in range(4))

    def assemble(local):
        return jnp.concatenate([a + b for a, b in zip(slots(local), swap_edges(slots(local)))], 0)

    def dual_apply(field):
        every = gather_members(matmul(coupling_local.T, field))
        return matmul(dual_local, field) + matmul(coarse_table, every)

    residual = jnp.concatenate(
        [
            jnp.where(odd_sub, from_left, right),
            jnp.where(odd_sub, right, from_left),
            jnp.where(odd_grp, from_below, upper),
            jnp.where(odd_grp, upper, from_below),
        ],
        0,
    )
    search_local = matmul(dirichlet_local, residual)
    gamma_part = column_sum(residual, search_local)
    search = assemble(search_local)
    image_local = dual_apply(search)
    sums = sum_everywhere(jnp.stack([gamma_part, column_sum(search, image_local)]))
    gamma, alpha = sums[0], sums[0] / sums[1]
    image = assemble(image_local)

    later = assemble(matmul(dirichlet_local, image))
    residual_next = residual - alpha * image
    search_next = search - alpha * later
    later_local = dual_apply(search_next)
    parts = jnp.stack(
        [
            0.5 * column_sum(residual_next, search_next),
            column_sum(search_next, later_local),
            0.5 * column_sum(search_next, image),
            column_sum(search, later_local),
        ]
    )
    gamma_next, steep, cross, cross_other = sum_everywhere(parts)
    beta = gamma_next / gamma
    alpha_next = gamma_next / (steep + beta * (cross + cross_other + beta * sums[1]))

    def owned(array):
        a, b, c, d = slots(array)
        return jnp.concatenate([jnp.where(odd_sub, b, a), jnp.where(odd_grp, d, c)], 0)

    a, b, c, d = slots(later_local)
    back = jnp.concatenate(
        [
            move(jnp.where(odd_sub, a, b), "sub", lambda i: i - 1),
            move(jnp.where(odd_grp, c, d), "grp", lambda i: i - 1),
        ],
        0,
    )
    later_image = owned(later_local) + back
    search_own = owned(search)
    solution = alpha * search_own + alpha_next * (owned(search_next) + beta * search_own)
    final = owned(residual_next) - alpha_next * (later_image + beta * owned(image))
    return (solution[None, None], final[None, None])


def solution(mesh):
    placed = (
        P("grp", "sub", None, None),
        P("grp", "sub", None, None),
        P("grp", "sub", None, None),
        P("grp", "sub", None, None),
        P("grp", "sub", None),
        P("grp", "sub", None),
        P("grp", "sub"),
        P("grp", "sub", None, None),
        P("grp", "sub", None, None),
    )
    return jax.shard_map(
        per_device,
        mesh=mesh,
        in_specs=placed,
        out_specs=(P("grp", "sub", None, None), P("grp", "sub", None, None)),
        check_vma=False,
    )
```

time: 261 us -> 121 us (0.46)
  blocking collectives: 159 us -> 0 us
  starting transfers between devices: 18.5 us -> 43.7 us
  matrix products: 17.6 us -> 12.6 us
  waiting for transfers between devices: 53.6 us -> 50 us
    psum x3 -> x0, blocking collectives: 115 us -> none  [the longest x2 76.7 us: residual_product(): return lax.psum(column_sum(residual, search), ('grp', 'sub'))]
    all_gather x4 -> x0, blocking collectives: 37.1 us -> none  [the longest x2 20.5 us: coarse_apply(): lax.all_gather(corner_values[None, None], 'sub', axis=1, tiled=True)[0]]
    ppermute x16 -> x38, starting transfers between devices: 18.5 us -> 43.7 us  [move(): lax.ppermute(array, axis, [(i, target(i) % peers) for i in range(peers)])]
    unnamed x1 -> x0, blocking collectives: 6.92 us -> none
    dot_general x27 -> x15, matrix products: 17.6 us -> 12.6 us  [matmul(): jnp.dot(first, second, precision=precision, preferred_element_type=jnp.fl...]
    ppermute x16 -> x38, waiting for transfers between devices: 53.6 us -> 50 us  [move(): lax.ppermute(array, axis, [(i, target(i) % peers) for i in range(peers)])]
  transfers between devices with their start and end apart: 16 -> 38, of which waited for: 14 -> 24; matrix products, arithmetic and copies ran while one was open for 1% -> 9% of each run, Pallas kernels for 0% -> 0%
where the time goes in v1:
time: 121 us; the launch traced here: 120 us
  waiting for transfers between devices  50 us (41%)
  starting transfers between devices  43.7 us (36%)
  matrix products  12.6 us (10%)
  local copies, waits for them, and re-layouts  7.78 us (6%)
  other arithmetic  4.47 us (4%)
  between operations  1.87 us (2%)
    ppermute x38, waiting for transfers between devices, move(): lax.ppermute(array, axis, [(i, target(i) % peers) for i in range(peers)])  50 us
    ppermute x38, starting transfers between devices, move(): lax.ppermute(array, axis, [(i, target(i) % peers) for i in range(peers)])  43.7 us
    dot_general x15, matrix products, matmul(): jnp.dot(first, second, precision=precision, preferred_element_type=jnp.fl...  12.6 us
    unnamed x38, local copies, waits for them, and re-layouts  4.55 us
  transfers between devices with their start and end apart: 38, of which 24 were waited for; matrix products, arithmetic and copies ran while one was open for 9% of the time, Pallas kernels for 0%

profile of v1, /device:TPU:0, one launch (start us, length us, event | category | flops | bytes accessed | tf_op | source)
XLA Modules:
  0.0 120.3 jit_solution(17661823475373193080)
XLA Ops:
  2.8 2.9 %collective-permute-start.6 = (f32[1,3,24]{2,1,0:T(4,128)S(1)}, f32[1,3,24]{2,1,0:T(4,128)S(1)}, u32[]{:S(2)}, u32[]{:S(2)}) collective-permute-start(f32[1,3,24]{2,1,0:T(4,128)S(1)} %reshape.380), channel_id=1, source_target_pairs={{0,2},{1,3},{2,0},{3,1},{4,6},{5,7},{6,4},{7,5},{8,10},{9,11},{10,... | collective-permute-start | bytes 872 | tf_op jit(solution)/shard_map/ppermute | solution.py:18
  5.7 1.5 %collective-permute-start.7 = (f32[1,3,24]{2,1,0:T(4,128)S(1)}, f32[1,3,24]{2,1,0:T(4,128)S(1)}, u32[]{:S(2)}, u32[]{:S(2)}) collective-permute-start(f32[1,3,24]{2,1,0:T(4,128)S(1)} %reshape.380), channel_id=1, source_target_pairs={{0,4},{1,5},{2,6},{3,7},{4,0},{5,1},{6,2},{7,3},{8,12},{9,13},{10,... | collective-permute-start | bytes 872 | tf_op jit(solution)/shard_map/ppermute | solution.py:18
  7.2 1.1 slice_bitcast_fusion.1
  8.4 2.1 %collective-permute-start.1 = (f32[128,512]{1,0:T(8,128)S(1)}, f32[128,512]{1,0:T(8,128)S(1)}, u32[]{:S(2)}, u32[]{:S(2)}) collective-permute-start(f32[128,512]{1,0:T(8,128)S(1)} %get-tuple-element.61), channel_id=1, source_target_pairs={{0,8},{8,16},{16,24},{24,0},{1,9},{9,17},{17,25},{25,1},{2,10},{10... | collective-permute-start | bytes 786440 | tf_op jit(solution)/shard_map/ppermute | solution.py:18
  14.3 1.1 fusion.15
  16.6 1.1 fusion.1
  17.7 1.1 fusion.14
  18.8 1.3 %collective-permute-start.9 = (f32[4,3,24]{2,1,0:T(4,128)S(1)}, f32[4,3,24]{2,1,0:T(4,128)S(1)}, u32[]{:S(2)}, u32[]{:S(2)}) collective-permute-start(f32[4,3,24]{2,1,0:T(4,128)S(1)} %pad_maximum_fusion.14), channel_id=1, source_target_pairs={{0,1},{1,0},{2,3},{3,2},{4,5},{5,4},{6,7},{7,6},{8,9},{9,8},{10,11... | collective-permute-start | bytes 3464 | tf_op jit(solution)/shard_map/ppermute | solution.py:18
  20.4 1.1 multiply_reduce_fusion.5
  22.5 1.8 %collective-permute-start.3 = (f32[128,512]{1,0:T(8,128)}, f32[128,512]{1,0:T(8,128)}, u32[]{:S(2)}, u32[]{:S(2)}) collective-permute-start(f32[128,512]{1,0:T(8,128)} %get-tuple-element.50), channel_id=1, source_target_pairs={{0,7},{1,2},{2,1},{3,4},{4,3},{5,6},{6,5},{7,0},{8,15},{9,10},{10,... | collective-permute-start | bytes 786440 | tf_op jit(solution)/shard_map/ppermute | solution.py:18
  24.3 1.3 %collective-permute-start.4 = (f32[128,512]{1,0:T(8,128)}, f32[128,512]{1,0:T(8,128)}, u32[]{:S(2)}, u32[]{:S(2)}) collective-permute-start(f32[128,512]{1,0:T(8,128)} %get-tuple-element.52), channel_id=1, source_target_pairs={{0,8},{8,0},{16,24},{24,16},{1,9},{9,1},{17,25},{25,17},{2,10},{10... | collective-permute-start | bytes 786440 | tf_op jit(solution)/shard_map/ppermute | solution.py:18
  25.6 2.5 %collective-permute-start.5 = (f32[128,512]{1,0:T(8,128)}, f32[128,512]{1,0:T(8,128)}, u32[]{:S(2)}, u32[]{:S(2)}) collective-permute-start(f32[128,512]{1,0:T(8,128)} %get-tuple-element.51), channel_id=1, source_target_pairs={{0,24},{8,16},{16,8},{24,0},{1,25},{9,17},{17,9},{25,1},{2,26},{10... | collective-permute-start | bytes 786440 | tf_op jit(solution)/shard_map/ppermute | solution.py:18
  28.5 3.1 %collective-permute-done.3 = f32[128,512]{1,0:T(8,128)} collective-permute-done((f32[128,512]{1,0:T(8,128)}, f32[128,512]{1,0:T(8,128)}, u32[]{:S(2)}, u32[]{:S(2)}) %collective-permute-start.3) | collective-permute-done | bytes 262176 | tf_op jit(solution)/shard_map/ppermute | solution.py:18
  32.6 7.6 %collective-permute-done.5 = f32[128,512]{1,0:T(8,128)} collective-permute-done((f32[128,512]{1,0:T(8,128)}, f32[128,512]{1,0:T(8,128)}, u32[]{:S(2)}, u32[]{:S(2)}) %collective-permute-start.5) | collective-permute-done | bytes 262176 | tf_op jit(solution)/shard_map/ppermute | solution.py:18
  40.3 1.4 %select_bitcast_fusion.5 = (f32[1,1,128,512]{3,2,1,0:T(8,128)S(1)}, f32[128,512]{1,0:T(8,128)S(1)}, f32[128,512]{1,0:T(8,128)S(1)}, f32[1,1,128,512]{3,2,1,0:T(8...) fusion(pred[]{:T(512)S(6)} %eq.82, f32[128,512]{1,0:T(8,128)} %collective-permute-done.2, ...), kind=kLoop, calls=%fused_computation.57 | loop fusion | flops 393216 | bytes 3670018 | tf_op jit(solution)/shard_map/concatenate | solution.py:169
  42.1 1.5 %collective-permute-start.10 = (f32[24,512]{1,0:T(8,128)S(1)}, f32[24,512]{1,0:T(8,128)S(1)}, u32[]{:S(2)}, u32[]{:S(2)}) collective-permute-start(f32[24,512]{1,0:T(8,128)S(1)} %get-tuple-element.73), channel_id=1, source_target_pairs={{0,2},{1,3},{2,0},{3,1},{4,6},{5,7},{6,4},{7,5},{8,10},{9,11},{10,... | collective-permute-start | bytes 147464 | tf_op jit(solution)/shard_map/ppermute | solution.py:18
  44.1 1.5 %collective-permute-start.12 = (f32[24,512]{1,0:T(8,128)S(1)}, f32[24,512]{1,0:T(8,128)S(1)}, u32[]{:S(2)}, u32[]{:S(2)}) collective-permute-start(f32[24,512]{1,0:T(8,128)S(1)} %get-tuple-element.73), channel_id=1, source_target_pairs={{0,6},{1,7},{2,4},{3,5},{4,2},{5,3},{6,0},{7,1},{8,14},{9,15},{10,... | collective-permute-start | bytes 147464 | tf_op jit(solution)/shard_map/ppermute | solution.py:18
  46.2 1.7 %collective-permute-done.11 = f32[24,512]{1,0:T(8,128)S(1)} collective-permute-done((f32[24,512]{1,0:T(8,128)S(1)}, f32[24,512]{1,0:T(8,128)S(1)}, u32[]{:S(2)}, u32[]{:S(2)}) %collective-permute-start.11) | collective-permute-done | bytes 49184 | tf_op jit(solution)/shard_map/ppermute | solution.py:18
  47.9 1.2 collective-permute-done.12
  49.2 1.4 %collective-permute-done.13 = f32[96,512]{1,0:T(8,128)S(1)} collective-permute-done((f32[96,512]{1,0:T(8,128)S(1)}, f32[96,512]{1,0:T(8,128)S(1)}, u32[]{:S(2)}, u32[]{:S(2)}) %collective-permute-start.13) | collective-permute-done | bytes 196640 | tf_op jit(solution)/shard_map/ppermute | solution.py:18
  51.3 1.1 multiply_reduce_fusion.4
  52.6 1.5 %collective-permute-start.20 = (f32[128,512]{1,0:T(8,128)S(1)}, f32[128,512]{1,0:T(8,128)S(1)}, u32[]{:S(2)}, u32[]{:S(2)}) collective-permute-start(f32[128,512]{1,0:T(8,128)S(1)} %get-tuple-element.43), channel_id=1, source_target_pairs={{0,7},{1,2},{2,1},{3,4},{4,3},{5,6},{6,5},{7,0},{8,15},{9,10},{10,... | collective-permute-start | bytes 786440 | tf_op jit(solution)/shard_map/ppermute | solution.py:18
  54.1 2.0 %collective-permute-start.22 = (f32[128,512]{1,0:T(8,128)S(1)}, f32[128,512]{1,0:T(8,128)S(1)}, u32[]{:S(2)}, u32[]{:S(2)}) collective-permute-start(f32[128,512]{1,0:T(8,128)S(1)} %get-tuple-element.44), channel_id=1, source_target_pairs={{0,24},{8,16},{16,8},{24,0},{1,25},{9,17},{17,9},{25,1},{2,26},{10... | collective-permute-start | bytes 786440 | tf_op jit(solution)/shard_map/ppermute | solution.py:18
  56.2 1.2 collective-permute-done.14
  58.2 3.5 %collective-permute-done.20 = f32[128,512]{1,0:T(8,128)S(1)} collective-permute-done((f32[128,512]{1,0:T(8,128)S(1)}, f32[128,512]{1,0:T(8,128)S(1)}, u32[]{:S(2)}, u32[]{:S(2)}) %collective-permute-start.20) | collective-permute-done | bytes 262176 | tf_op jit(solution)/shard_map/ppermute | solution.py:18
  61.7 1.7 %collective-permute-done.21 = f32[128,512]{1,0:T(8,128)S(1)} collective-permute-done((f32[128,512]{1,0:T(8,128)S(1)}, f32[128,512]{1,0:T(8,128)S(1)}, u32[]{:S(2)}, u32[]{:S(2)}) %collective-permute-start.21) | collective-permute-done | bytes 262176 | tf_op jit(solution)/shard_map/ppermute | solution.py:18
  63.4 4.1 %collective-permute-done.22 = f32[128,512]{1,0:T(8,128)S(1)} collective-permute-done((f32[128,512]{1,0:T(8,128)S(1)}, f32[128,512]{1,0:T(8,128)S(1)}, u32[]{:S(2)}, u32[]{:S(2)}) %collective-permute-start.22) | collective-permute-done | bytes 262176 | tf_op jit(solution)/shard_map/ppermute | solution.py:18
  68.9 2.3 %collective-permute-start.24 = (f32[128,512]{1,0:T(8,128)S(1)}, f32[128,512]{1,0:T(8,128)S(1)}, u32[]{:S(2)}, u32[]{:S(2)}) collective-permute-start(f32[128,512]{1,0:T(8,128)S(1)} %get-tuple-element.39), channel_id=1, source_target_pairs={{0,7},{1,2},{2,1},{3,4},{4,3},{5,6},{6,5},{7,0},{8,15},{9,10},{10,... | collective-permute-start | bytes 786440 | tf_op jit(solution)/shard_map/ppermute | solution.py:18
  71.2 1.6 %collective-permute-start.25 = (f32[128,512]{1,0:T(8,128)S(1)}, f32[128,512]{1,0:T(8,128)S(1)}, u32[]{:S(2)}, u32[]{:S(2)}) collective-permute-start(f32[128,512]{1,0:T(8,128)S(1)} %get-tuple-element.38), channel_id=1, source_target_pairs={{0,8},{8,0},{16,24},{24,16},{1,9},{9,1},{17,25},{25,17},{2,10},{10... | collective-permute-start | bytes 786440 | tf_op jit(solution)/shard_map/ppermute | solution.py:18
  72.8 1.4 %collective-permute-start.26 = (f32[128,512]{1,0:T(8,128)S(1)}, f32[128,512]{1,0:T(8,128)S(1)}, u32[]{:S(2)}, u32[]{:S(2)}) collective-permute-start(f32[128,512]{1,0:T(8,128)S(1)} %get-tuple-element.37), channel_id=1, source_target_pairs={{0,24},{8,16},{16,8},{24,0},{1,25},{9,17},{17,9},{25,1},{2,26},{10... | collective-permute-start | bytes 786440 | tf_op jit(solution)/shard_map/ppermute | solution.py:18
  74.2 1.5 %collective-permute-start.16 = (f32[2,512]{1,0:T(2,128)S(1)}, f32[2,512]{1,0:T(2,128)S(1)}, u32[]{:S(2)}, u32[]{:S(2)}) collective-permute-start(f32[2,512]{1,0:T(2,128)S(1)} %fusion.74), channel_id=1, source_target_pairs={{0,4},{1,5},{2,6},{3,7},{4,0},{5,1},{6,2},{7,3},{8,12},{9,13},{10,... | collective-permute-start | bytes 12296 | tf_op jit(solution)/shard_map/ppermute | solution.py:18
  75.8 2.2 %collective-permute-done.16 = f32[2,512]{1,0:T(2,128)S(1)} collective-permute-done((f32[2,512]{1,0:T(2,128)S(1)}, f32[2,512]{1,0:T(2,128)S(1)}, u32[]{:S(2)}, u32[]{:S(2)}) %collective-permute-start.16) | collective-permute-done | bytes 4128 | tf_op jit(solution)/shard_map/ppermute | solution.py:18
  78.1 6.2 %collective-permute-done.17 = f32[2,512]{1,0:T(2,128)S(1)} collective-permute-done((f32[2,512]{1,0:T(2,128)S(1)}, f32[2,512]{1,0:T(2,128)S(1)}, u32[]{:S(2)}, u32[]{:S(2)}) %collective-permute-start.17) | collective-permute-done | bytes 4128 | tf_op jit(solution)/shard_map/ppermute | solution.py:18
  84.3 2.5 %collective-permute-start.18 = (f32[2,512]{1,0:T(2,128)S(1)}, f32[2,512]{1,0:T(2,128)S(1)}, u32[]{:S(2)}, u32[]{:S(2)}) collective-permute-start(f32[2,512]{1,0:T(2,128)S(1)} %add.145), channel_id=1, source_target_pairs={{0,16},{8,24},{16,0},{24,8},{1,17},{9,25},{17,1},{25,9},{2,18},{10... | collective-permute-start | bytes 12296 | tf_op jit(solution)/shard_map/ppermute | solution.py:18
  86.8 2.0 %collective-permute-done.18 = f32[2,512]{1,0:T(2,128)S(1)} collective-permute-done((f32[2,512]{1,0:T(2,128)S(1)}, f32[2,512]{1,0:T(2,128)S(1)}, u32[]{:S(2)}, u32[]{:S(2)}) %collective-permute-start.18) | collective-permute-done | bytes 4128 | tf_op jit(solution)/shard_map/ppermute | solution.py:18
  91.2 2.2 %collective-permute-start.29 = (f32[24,512]{1,0:T(8,128)S(1)}, f32[24,512]{1,0:T(8,128)S(1)}, u32[]{:S(2)}, u32[]{:S(2)}) collective-permute-start(f32[24,512]{1,0:T(8,128)S(1)} %get-tuple-element.79), channel_id=1, source_target_pairs={{0,6},{1,7},{2,4},{3,5},{4,2},{5,3},{6,0},{7,1},{8,14},{9,15},{10,... | collective-permute-start | bytes 147464 | tf_op jit(solution)/shard_map/ppermute | solution.py:18
  94.6 1.6 %collective-permute-done.29 = f32[24,512]{1,0:T(8,128)S(1)} collective-permute-done((f32[24,512]{1,0:T(8,128)S(1)}, f32[24,512]{1,0:T(8,128)S(1)}, u32[]{:S(2)}, u32[]{:S(2)}) %collective-permute-start.29) | collective-permute-done | bytes 49184 | tf_op jit(solution)/shard_map/ppermute | solution.py:18
  96.3 1.4 %collective-permute-done.30 = f32[96,512]{1,0:T(8,128)S(1)} collective-permute-done((f32[96,512]{1,0:T(8,128)S(1)}, f32[96,512]{1,0:T(8,128)S(1)}, u32[]{:S(2)}, u32[]{:S(2)}) %collective-permute-start.30) | collective-permute-done | bytes 196640 | tf_op jit(solution)/shard_map/ppermute | solution.py:18
  98.9 2.1 %multiply_reduce_fusion.3 = (f32[512]{0:T(512)S(1)}, f32[512]{0:T(512)S(1)}, f32[512]{0:T(512)S(1)}, f32[512]{0:T(512)S(1)}, f32[512,512]{1,0:T(8,128)S(1)}, /*index=5*/f32[512,512]{1,0:T(8,128)S(1)}) fusion(f32[512,512]{1,0:T(8,128)S(1)} %fusion.2, f32[128,512]{1,0:T(8,128)S(1)} %get-tuple-element.42, f32[128,512]{1,0:T(8,128)S(1)} %get-tuple-element.41, ...), kind=kOutput, calls=%fused_computation.18 | convolution fusion | flops 810547200 | bytes 8398848 | tf_op jit(solution)/shard_map/dot_general | solution.py:13
  102.3 1.3 %collective-permute-start.32 = (f32[4,512]{1,0:T(4,128)S(1)}, f32[4,512]{1,0:T(4,128)S(1)}, u32[]{:S(2)}, u32[]{:S(2)}) collective-permute-start(f32[4,512]{1,0:T(4,128)S(1)} %fusion.50), channel_id=1, source_target_pairs={{0,2},{1,3},{2,0},{3,1},{4,6},{5,7},{6,4},{7,5},{8,10},{9,11},{10,... | collective-permute-start | bytes 24584 | tf_op jit(solution)/shard_map/ppermute | solution.py:18
  103.6 2.4 %collective-permute-done.32 = f32[4,512]{1,0:T(4,128)S(1)} collective-permute-done((f32[4,512]{1,0:T(4,128)S(1)}, f32[4,512]{1,0:T(4,128)S(1)}, u32[]{:S(2)}, u32[]{:S(2)}) %collective-permute-start.32) | collective-permute-done | bytes 8224 | tf_op jit(solution)/shard_map/ppermute | solution.py:18
  106.1 1.4 %collective-permute-start.33 = (f32[4,512]{1,0:T(4,128)S(1)}, f32[4,512]{1,0:T(4,128)S(1)}, u32[]{:S(2)}, u32[]{:S(2)}) collective-permute-start(f32[4,512]{1,0:T(4,128)S(1)} %fusion.73), channel_id=1, source_target_pairs={{0,4},{1,5},{2,6},{3,7},{4,0},{5,1},{6,2},{7,3},{8,12},{9,13},{10,... | collective-permute-start | bytes 24584 | tf_op jit(solution)/shard_map/ppermute | solution.py:18
  107.5 2.3 %collective-permute-done.33 = f32[4,512]{1,0:T(4,128)S(1)} collective-permute-done((f32[4,512]{1,0:T(4,128)S(1)}, f32[4,512]{1,0:T(4,128)S(1)}, u32[]{:S(2)}, u32[]{:S(2)}) %collective-permute-start.33) | collective-permute-done | bytes 8224 | tf_op jit(solution)/shard_map/ppermute | solution.py:18
  109.8 2.5 %collective-permute-start.34 = (f32[4,512]{1,0:T(4,128)S(1)}, f32[4,512]{1,0:T(4,128)S(1)}, u32[]{:S(2)}, u32[]{:S(2)}) collective-permute-start(f32[4,512]{1,0:T(4,128)S(1)} %add.158), channel_id=1, source_target_pairs={{0,8},{8,0},{16,24},{24,16},{1,9},{9,1},{17,25},{25,17},{2,10},{10... | collective-permute-start | bytes 24584 | tf_op jit(solution)/shard_map/ppermute | solution.py:18
  112.4 1.5 %collective-permute-start.37 = (f32[128,512]{1,0:T(8,128)S(1)}, f32[128,512]{1,0:T(8,128)S(1)}, u32[]{:S(2)}, u32[]{:S(2)}) collective-permute-start(f32[128,512]{1,0:T(8,128)S(1)} %get-tuple-element.25), channel_id=1, source_target_pairs={{0,24},{8,0},{16,8},{24,16},{1,25},{9,1},{17,9},{25,17},{2,26},{10... | collective-permute-start | bytes 786440 | tf_op jit(solution)/shard_map/ppermute | solution.py:18
  114.0 1.9 %collective-permute-start.35 = (f32[4,512]{1,0:T(4,128)S(1)}, f32[4,512]{1,0:T(4,128)S(1)}, u32[]{:S(2)}, u32[]{:S(2)}) collective-permute-start(f32[4,512]{1,0:T(4,128)S(1)} %add.159), channel_id=1, source_target_pairs={{0,16},{8,24},{16,0},{24,8},{1,17},{9,25},{17,1},{25,9},{2,18},{10... | collective-permute-start | bytes 24584 | tf_op jit(solution)/shard_map/ppermute | solution.py:18
  116.0 2.6 %collective-permute-done.35 = f32[4,512]{1,0:T(4,128)S(1)} collective-permute-done((f32[4,512]{1,0:T(4,128)S(1)}, f32[4,512]{1,0:T(4,128)S(1)}, u32[]{:S(2)}, u32[]{:S(2)}) %collective-permute-start.35) | collective-permute-done | bytes 8224 | tf_op jit(solution)/shard_map/ppermute | solution.py:18
  119.0 1.3 %maximum_subtract_fusion = (f32[1,1,256,512]{3,2,1,0:T(8,128)}, f32[1,1,256,512]{3,2,1,0:T(8,128)}) fusion(f32[1,1,128,512]{3,2,1,0:T(8,128)S(1)} %get-tuple-element.29, f32[1,1,128,512]{3,2,1,0:T(8,128)S(1)} %get-tuple-element.28, f32[1,1,128,512]{3,2,1,0:T(8,128)S(1)} %get-tuple-element.27, f32[1,1,128,512]{3,2,1,0:T(8,128)S(1)} %get-tuple-element.26, ...), kind=kLoop, calls=%fused_computation.36 | loop fusion | flops 2097152 | bytes 4200448 | tf_op jit(solution)/shard_map/sub | solution.py:182
  (134 shorter events, 20.8 us)
Async XLA Ops:
  0.6 14.8 %copy-start = (f32[1,1,512,24]{2,3,1,0:T(8,128)S(1)}, f32[1,1,512,24]{2,3,1,0:T(8,128)}, u32[]{:S(2)}) copy-start(f32[1,1,512,24]{2,3,1,0:T(8,128)} %param.12) | copy-start | bytes 147460
  2.8 16.0 %collective-permute-start.6 = (f32[1,3,24]{2,1,0:T(4,128)S(1)}, f32[1,3,24]{2,1,0:T(4,128)S(1)}, u32[]{:S(2)}, u32[]{:S(2)}) collective-permute-start(f32[1,3,24]{2,1,0:T(4,128)S(1)} %reshape.380), channel_id=1, source_target_pairs={{0,2},{1,3},{2,0},{3,1},{4,6},{5,7},{6,4},{7,5},{8,10},{9,11},{10,... | collective-permute-start | bytes 872 | tf_op jit(solution)/shard_map/ppermute | solution.py:18
  5.7 13.1 %collective-permute-start.7 = (f32[1,3,24]{2,1,0:T(4,128)S(1)}, f32[1,3,24]{2,1,0:T(4,128)S(1)}, u32[]{:S(2)}, u32[]{:S(2)}) collective-permute-start(f32[1,3,24]{2,1,0:T(4,128)S(1)} %reshape.380), channel_id=1, source_target_pairs={{0,4},{1,5},{2,6},{3,7},{4,0},{5,1},{6,2},{7,3},{8,12},{9,13},{10,... | collective-permute-start | bytes 872 | tf_op jit(solution)/shard_map/ppermute | solution.py:18
  7.2 11.6 %collective-permute-start.8 = (f32[1,3,24]{2,1,0:T(4,128)S(1)}, f32[1,3,24]{2,1,0:T(4,128)S(1)}, u32[]{:S(2)}, u32[]{:S(2)}) collective-permute-start(f32[1,3,24]{2,1,0:T(4,128)S(1)} %reshape.380), channel_id=1, source_target_pairs={{0,6},{1,7},{2,4},{3,5},{4,2},{5,3},{6,0},{7,1},{8,14},{9,15},{10,... | collective-permute-start | bytes 872 | tf_op jit(solution)/shard_map/ppermute | solution.py:18
  8.3 11.9 %collective-permute-start = (f32[128,512]{1,0:T(8,128)S(1)}, f32[128,512]{1,0:T(8,128)S(1)}, u32[]{:S(2)}, u32[]{:S(2)}) collective-permute-start(f32[128,512]{1,0:T(8,128)S(1)} %get-tuple-element.60), channel_id=1, source_target_pairs={{0,1},{1,2},{2,3},{3,4},{4,5},{5,6},{6,7},{7,0},{8,9},{9,10},{10,1... | collective-permute-start | bytes 786440 | tf_op jit(solution)/shard_map/ppermute | solution.py:18
  8.4 11.8 %collective-permute-start.1 = (f32[128,512]{1,0:T(8,128)S(1)}, f32[128,512]{1,0:T(8,128)S(1)}, u32[]{:S(2)}, u32[]{:S(2)}) collective-permute-start(f32[128,512]{1,0:T(8,128)S(1)} %get-tuple-element.61), channel_id=1, source_target_pairs={{0,8},{8,16},{16,24},{24,0},{1,9},{9,17},{17,25},{25,1},{2,10},{10... | collective-permute-start | bytes 786440 | tf_op jit(solution)/shard_map/ppermute | solution.py:18
  12.1 1.2 %copy-start.2 = (f32[1,1,512,512]{3,2,1,0:T(8,128)S(1)}, f32[1,1,512,512]{3,2,1,0:T(8,128)}, u32[]{:S(2)}) copy-start(f32[1,1,512,512]{3,2,1,0:T(8,128)} %param.11) | copy-start | bytes 3145732
  15.4 1.2 %copy-start.3 = (f32[1,1,512,512]{3,2,1,0:T(8,128)S(1)}, f32[1,1,512,512]{3,2,1,0:T(8,128)}, u32[]{:S(2)}) copy-start(f32[1,1,512,512]{3,2,1,0:T(8,128)} %param.10) | copy-start | bytes 3145732
  17.7 2.5 %copy-start.1 = (f32[1,1,256,512]{3,2,1,0:T(8,128)S(1)}, f32[1,1,256,512]{3,2,1,0:T(8,128)}, u32[]{:S(2)}) copy-start(f32[1,1,256,512]{3,2,1,0:T(8,128)} %param.9) | copy-start | bytes 1572868
  18.8 9.2 %collective-permute-start.9 = (f32[4,3,24]{2,1,0:T(4,128)S(1)}, f32[4,3,24]{2,1,0:T(4,128)S(1)}, u32[]{:S(2)}, u32[]{:S(2)}) collective-permute-start(f32[4,3,24]{2,1,0:T(4,128)S(1)} %pad_maximum_fusion.14), channel_id=1, source_target_pairs={{0,1},{1,0},{2,3},{3,2},{4,5},{5,4},{6,7},{7,6},{8,9},{9,8},{10,11... | collective-permute-start | bytes 3464 | tf_op jit(solution)/shard_map/ppermute | solution.py:18
  20.3 1.1 copy-start.4
  20.3 1.1 copy-start.6
  20.3 1.1 copy-start.8
  22.4 6.1 %collective-permute-start.2 = (f32[128,512]{1,0:T(8,128)}, f32[128,512]{1,0:T(8,128)}, u32[]{:S(2)}, u32[]{:S(2)}) collective-permute-start(f32[128,512]{1,0:T(8,128)} %get-tuple-element.53), channel_id=1, source_target_pairs={{0,1},{1,0},{2,3},{3,2},{4,5},{5,4},{6,7},{7,6},{8,9},{9,8},{10,11... | collective-permute-start | bytes 786440 | tf_op jit(solution)/shard_map/ppermute | solution.py:18
  22.5 9.2 %collective-permute-start.3 = (f32[128,512]{1,0:T(8,128)}, f32[128,512]{1,0:T(8,128)}, u32[]{:S(2)}, u32[]{:S(2)}) collective-permute-start(f32[128,512]{1,0:T(8,128)} %get-tuple-element.50), channel_id=1, source_target_pairs={{0,7},{1,2},{2,1},{3,4},{4,3},{5,6},{6,5},{7,0},{8,15},{9,10},{10,... | collective-permute-start | bytes 786440 | tf_op jit(solution)/shard_map/ppermute | solution.py:18
  24.3 8.3 %collective-permute-start.4 = (f32[128,512]{1,0:T(8,128)}, f32[128,512]{1,0:T(8,128)}, u32[]{:S(2)}, u32[]{:S(2)}) collective-permute-start(f32[128,512]{1,0:T(8,128)} %get-tuple-element.52), channel_id=1, source_target_pairs={{0,8},{8,0},{16,24},{24,16},{1,9},{9,1},{17,25},{25,17},{2,10},{10... | collective-permute-start | bytes 786440 | tf_op jit(solution)/shard_map/ppermute | solution.py:18
  25.6 14.7 %collective-permute-start.5 = (f32[128,512]{1,0:T(8,128)}, f32[128,512]{1,0:T(8,128)}, u32[]{:S(2)}, u32[]{:S(2)}) collective-permute-start(f32[128,512]{1,0:T(8,128)} %get-tuple-element.51), channel_id=1, source_target_pairs={{0,24},{8,16},{16,8},{24,0},{1,25},{9,17},{17,9},{25,1},{2,26},{10... | collective-permute-start | bytes 786440 | tf_op jit(solution)/shard_map/ppermute | solution.py:18
  42.1 4.1 %collective-permute-start.10 = (f32[24,512]{1,0:T(8,128)S(1)}, f32[24,512]{1,0:T(8,128)S(1)}, u32[]{:S(2)}, u32[]{:S(2)}) collective-permute-start(f32[24,512]{1,0:T(8,128)S(1)} %get-tuple-element.73), channel_id=1, source_target_pairs={{0,2},{1,3},{2,0},{3,1},{4,6},{5,7},{6,4},{7,5},{8,10},{9,11},{10,... | collective-permute-start | bytes 147464 | tf_op jit(solution)/shard_map/ppermute | solution.py:18
  43.5 4.4 %collective-permute-start.11 = (f32[24,512]{1,0:T(8,128)S(1)}, f32[24,512]{1,0:T(8,128)S(1)}, u32[]{:S(2)}, u32[]{:S(2)}) collective-permute-start(f32[24,512]{1,0:T(8,128)S(1)} %get-tuple-element.73), channel_id=1, source_target_pairs={{0,4},{1,5},{2,6},{3,7},{4,0},{5,1},{6,2},{7,3},{8,12},{9,13},{10,... | collective-permute-start | bytes 147464 | tf_op jit(solution)/shard_map/ppermute | solution.py:18
  44.1 5.0 %collective-permute-start.12 = (f32[24,512]{1,0:T(8,128)S(1)}, f32[24,512]{1,0:T(8,128)S(1)}, u32[]{:S(2)}, u32[]{:S(2)}) collective-permute-start(f32[24,512]{1,0:T(8,128)S(1)} %get-tuple-element.73), channel_id=1, source_target_pairs={{0,6},{1,7},{2,4},{3,5},{4,2},{5,3},{6,0},{7,1},{8,14},{9,15},{10,... | collective-permute-start | bytes 147464 | tf_op jit(solution)/shard_map/ppermute | solution.py:18
  49.1 1.5 %collective-permute-start.13 = (f32[96,512]{1,0:T(8,128)S(1)}, f32[96,512]{1,0:T(8,128)S(1)}, u32[]{:S(2)}, u32[]{:S(2)}) collective-permute-start(f32[96,512]{1,0:T(8,128)S(1)} %pad_maximum_fusion.10), channel_id=1, source_target_pairs={{0,1},{1,0},{2,3},{3,2},{4,5},{5,4},{6,7},{7,6},{8,9},{9,8},{10,11... | collective-permute-start | bytes 589832 | tf_op jit(solution)/shard_map/ppermute | solution.py:18
  52.4 5.7 %collective-permute-start.19 = (f32[128,512]{1,0:T(8,128)S(1)}, f32[128,512]{1,0:T(8,128)S(1)}, u32[]{:S(2)}, u32[]{:S(2)}) collective-permute-start(f32[128,512]{1,0:T(8,128)S(1)} %get-tuple-element.46), channel_id=1, source_target_pairs={{0,1},{1,0},{2,3},{3,2},{4,5},{5,4},{6,7},{7,6},{8,9},{9,8},{10,11... | collective-permute-start | bytes 786440 | tf_op jit(solution)/shard_map/ppermute | solution.py:18
  52.6 9.0 %collective-permute-start.20 = (f32[128,512]{1,0:T(8,128)S(1)}, f32[128,512]{1,0:T(8,128)S(1)}, u32[]{:S(2)}, u32[]{:S(2)}) collective-permute-start(f32[128,512]{1,0:T(8,128)S(1)} %get-tuple-element.43), channel_id=1, source_target_pairs={{0,7},{1,2},{2,1},{3,4},{4,3},{5,6},{6,5},{7,0},{8,15},{9,10},{10,... | collective-permute-start | bytes 786440 | tf_op jit(solution)/shard_map/ppermute | solution.py:18
  54.1 9.3 %collective-permute-start.21 = (f32[128,512]{1,0:T(8,128)S(1)}, f32[128,512]{1,0:T(8,128)S(1)}, u32[]{:S(2)}, u32[]{:S(2)}) collective-permute-start(f32[128,512]{1,0:T(8,128)S(1)} %get-tuple-element.45), channel_id=1, source_target_pairs={{0,8},{8,0},{16,24},{24,16},{1,9},{9,1},{17,25},{25,17},{2,10},{10... | collective-permute-start | bytes 786440 | tf_op jit(solution)/shard_map/ppermute | solution.py:18
  54.1 13.3 %collective-permute-start.22 = (f32[128,512]{1,0:T(8,128)S(1)}, f32[128,512]{1,0:T(8,128)S(1)}, u32[]{:S(2)}, u32[]{:S(2)}) collective-permute-start(f32[128,512]{1,0:T(8,128)S(1)} %get-tuple-element.44), channel_id=1, source_target_pairs={{0,24},{8,16},{16,8},{24,0},{1,25},{9,17},{17,9},{25,1},{2,26},{10... | collective-permute-start | bytes 786440 | tf_op jit(solution)/shard_map/ppermute | solution.py:18
  56.2 1.2 %collective-permute-start.14 = (f32[2,512]{1,0:T(2,128)S(1)}, f32[2,512]{1,0:T(2,128)S(1)}, u32[]{:S(2)}, u32[]{:S(2)}) collective-permute-start(f32[2,512]{1,0:T(2,128)S(1)} %pad_maximum_fusion.16), channel_id=1, source_target_pairs={{0,1},{1,0},{2,3},{3,2},{4,5},{5,4},{6,7},{7,6},{8,9},{9,8},{10,11... | collective-permute-start | bytes 12296 | tf_op jit(solution)/shard_map/ppermute | solution.py:18
  57.4 16.8 %collective-permute-start.15 = (f32[2,512]{1,0:T(2,128)S(1)}, f32[2,512]{1,0:T(2,128)S(1)}, u32[]{:S(2)}, u32[]{:S(2)}) collective-permute-start(f32[2,512]{1,0:T(2,128)S(1)} %fusion.49), channel_id=1, source_target_pairs={{0,2},{1,3},{2,0},{3,1},{4,6},{5,7},{6,4},{7,5},{8,10},{9,11},{10,... | collective-permute-start | bytes 12296 | tf_op jit(solution)/shard_map/ppermute | solution.py:18
  68.8 20.0 %collective-permute-start.23 = (f32[128,512]{1,0:T(8,128)S(1)}, f32[128,512]{1,0:T(8,128)S(1)}, u32[]{:S(2)}, u32[]{:S(2)}) collective-permute-start(f32[128,512]{1,0:T(8,128)S(1)} %get-tuple-element.36), channel_id=1, source_target_pairs={{0,1},{1,0},{2,3},{3,2},{4,5},{5,4},{6,7},{7,6},{8,9},{9,8},{10,11... | collective-permute-start | bytes 786440 | tf_op jit(solution)/shard_map/ppermute | solution.py:18
  68.9 20.0 %collective-permute-start.24 = (f32[128,512]{1,0:T(8,128)S(1)}, f32[128,512]{1,0:T(8,128)S(1)}, u32[]{:S(2)}, u32[]{:S(2)}) collective-permute-start(f32[128,512]{1,0:T(8,128)S(1)} %get-tuple-element.39), channel_id=1, source_target_pairs={{0,7},{1,2},{2,1},{3,4},{4,3},{5,6},{6,5},{7,0},{8,15},{9,10},{10,... | collective-permute-start | bytes 786440 | tf_op jit(solution)/shard_map/ppermute | solution.py:18
  71.2 17.7 %collective-permute-start.25 = (f32[128,512]{1,0:T(8,128)S(1)}, f32[128,512]{1,0:T(8,128)S(1)}, u32[]{:S(2)}, u32[]{:S(2)}) collective-permute-start(f32[128,512]{1,0:T(8,128)S(1)} %get-tuple-element.38), channel_id=1, source_target_pairs={{0,8},{8,0},{16,24},{24,16},{1,9},{9,1},{17,25},{25,17},{2,10},{10... | collective-permute-start | bytes 786440 | tf_op jit(solution)/shard_map/ppermute | solution.py:18
  72.8 16.1 %collective-permute-start.26 = (f32[128,512]{1,0:T(8,128)S(1)}, f32[128,512]{1,0:T(8,128)S(1)}, u32[]{:S(2)}, u32[]{:S(2)}) collective-permute-start(f32[128,512]{1,0:T(8,128)S(1)} %get-tuple-element.37), channel_id=1, source_target_pairs={{0,24},{8,16},{16,8},{24,0},{1,25},{9,17},{17,9},{25,1},{2,26},{10... | collective-permute-start | bytes 786440 | tf_op jit(solution)/shard_map/ppermute | solution.py:18
  74.2 3.7 %collective-permute-start.16 = (f32[2,512]{1,0:T(2,128)S(1)}, f32[2,512]{1,0:T(2,128)S(1)}, u32[]{:S(2)}, u32[]{:S(2)}) collective-permute-start(f32[2,512]{1,0:T(2,128)S(1)} %fusion.74), channel_id=1, source_target_pairs={{0,4},{1,5},{2,6},{3,7},{4,0},{5,1},{6,2},{7,3},{8,12},{9,13},{10,... | collective-permute-start | bytes 12296 | tf_op jit(solution)/shard_map/ppermute | solution.py:18
  78.0 6.3 %collective-permute-start.17 = (f32[2,512]{1,0:T(2,128)S(1)}, f32[2,512]{1,0:T(2,128)S(1)}, u32[]{:S(2)}, u32[]{:S(2)}) collective-permute-start(f32[2,512]{1,0:T(2,128)S(1)} %add.144), channel_id=1, source_target_pairs={{0,8},{8,0},{16,24},{24,16},{1,9},{9,1},{17,25},{25,17},{2,10},{10... | collective-permute-start | bytes 12296 | tf_op jit(solution)/shard_map/ppermute | solution.py:18
  84.3 4.5 %collective-permute-start.18 = (f32[2,512]{1,0:T(2,128)S(1)}, f32[2,512]{1,0:T(2,128)S(1)}, u32[]{:S(2)}, u32[]{:S(2)}) collective-permute-start(f32[2,512]{1,0:T(2,128)S(1)} %add.145), channel_id=1, source_target_pairs={{0,16},{8,24},{16,0},{24,8},{1,17},{9,25},{17,1},{25,9},{2,18},{10... | collective-permute-start | bytes 12296 | tf_op jit(solution)/shard_map/ppermute | solution.py:18
  89.9 4.1 %collective-permute-start.27 = (f32[24,512]{1,0:T(8,128)S(1)}, f32[24,512]{1,0:T(8,128)S(1)}, u32[]{:S(2)}, u32[]{:S(2)}) collective-permute-start(f32[24,512]{1,0:T(8,128)S(1)} %get-tuple-element.79), channel_id=1, source_target_pairs={{0,2},{1,3},{2,0},{3,1},{4,6},{5,7},{6,4},{7,5},{8,10},{9,11},{10,... | collective-permute-start | bytes 147464 | tf_op jit(solution)/shard_map/ppermute | solution.py:18
  90.5 4.1 %collective-permute-start.28 = (f32[24,512]{1,0:T(8,128)S(1)}, f32[24,512]{1,0:T(8,128)S(1)}, u32[]{:S(2)}, u32[]{:S(2)}) collective-permute-start(f32[24,512]{1,0:T(8,128)S(1)} %get-tuple-element.79), channel_id=1, source_target_pairs={{0,4},{1,5},{2,6},{3,7},{4,0},{5,1},{6,2},{7,3},{8,12},{9,13},{10,... | collective-permute-start | bytes 147464 | tf_op jit(solution)/shard_map/ppermute | solution.py:18
  91.2 5.0 %collective-permute-start.29 = (f32[24,512]{1,0:T(8,128)S(1)}, f32[24,512]{1,0:T(8,128)S(1)}, u32[]{:S(2)}, u32[]{:S(2)}) collective-permute-start(f32[24,512]{1,0:T(8,128)S(1)} %get-tuple-element.79), channel_id=1, source_target_pairs={{0,6},{1,7},{2,4},{3,5},{4,2},{5,3},{6,0},{7,1},{8,14},{9,15},{10,... | collective-permute-start | bytes 147464 | tf_op jit(solution)/shard_map/ppermute | solution.py:18
  96.2 1.5 %collective-permute-start.30 = (f32[96,512]{1,0:T(8,128)S(1)}, f32[96,512]{1,0:T(8,128)S(1)}, u32[]{:S(2)}, u32[]{:S(2)}) collective-permute-start(f32[96,512]{1,0:T(8,128)S(1)} %pad_maximum_fusion.11), channel_id=1, source_target_pairs={{0,1},{1,0},{2,3},{3,2},{4,5},{5,4},{6,7},{7,6},{8,9},{9,8},{10,11... | collective-permute-start | bytes 589832 | tf_op jit(solution)/shard_map/ppermute | solution.py:18
  97.8 1.0 copy-start.5
  97.8 1.0 copy-start.7
  97.8 1.1 copy-start.9
  101.1 1.2 %collective-permute-start.31 = (f32[4,512]{1,0:T(4,128)S(1)}, f32[4,512]{1,0:T(4,128)S(1)}, u32[]{:S(2)}, u32[]{:S(2)}) collective-permute-start(f32[4,512]{1,0:T(4,128)S(1)} %pad_maximum_fusion.15), channel_id=1, source_target_pairs={{0,1},{1,0},{2,3},{3,2},{4,5},{5,4},{6,7},{7,6},{8,9},{9,8},{10,11... | collective-permute-start | bytes 24584 | tf_op jit(solution)/shard_map/ppermute | solution.py:18
  102.3 3.7 %collective-permute-start.32 = (f32[4,512]{1,0:T(4,128)S(1)}, f32[4,512]{1,0:T(4,128)S(1)}, u32[]{:S(2)}, u32[]{:S(2)}) collective-permute-start(f32[4,512]{1,0:T(4,128)S(1)} %fusion.50), channel_id=1, source_target_pairs={{0,2},{1,3},{2,0},{3,1},{4,6},{5,7},{6,4},{7,5},{8,10},{9,11},{10,... | collective-permute-start | bytes 24584 | tf_op jit(solution)/shard_map/ppermute | solution.py:18
  106.1 3.7 %collective-permute-start.33 = (f32[4,512]{1,0:T(4,128)S(1)}, f32[4,512]{1,0:T(4,128)S(1)}, u32[]{:S(2)}, u32[]{:S(2)}) collective-permute-start(f32[4,512]{1,0:T(4,128)S(1)} %fusion.73), channel_id=1, source_target_pairs={{0,4},{1,5},{2,6},{3,7},{4,0},{5,1},{6,2},{7,3},{8,12},{9,13},{10,... | collective-permute-start | bytes 24584 | tf_op jit(solution)/shard_map/ppermute | solution.py:18
  109.8 4.2 %collective-permute-start.34 = (f32[4,512]{1,0:T(4,128)S(1)}, f32[4,512]{1,0:T(4,128)S(1)}, u32[]{:S(2)}, u32[]{:S(2)}) collective-permute-start(f32[4,512]{1,0:T(4,128)S(1)} %add.158), channel_id=1, source_target_pairs={{0,8},{8,0},{16,24},{24,16},{1,9},{9,1},{17,25},{25,17},{2,10},{10... | collective-permute-start | bytes 24584 | tf_op jit(solution)/shard_map/ppermute | solution.py:18
  112.4 6.6 %collective-permute-start.37 = (f32[128,512]{1,0:T(8,128)S(1)}, f32[128,512]{1,0:T(8,128)S(1)}, u32[]{:S(2)}, u32[]{:S(2)}) collective-permute-start(f32[128,512]{1,0:T(8,128)S(1)} %get-tuple-element.25), channel_id=1, source_target_pairs={{0,24},{8,0},{16,8},{24,16},{1,25},{9,1},{17,9},{25,17},{2,26},{10... | collective-permute-start | bytes 786440 | tf_op jit(solution)/shard_map/ppermute | solution.py:18
  113.9 5.1 %collective-permute-start.36 = (f32[128,512]{1,0:T(8,128)S(1)}, f32[128,512]{1,0:T(8,128)S(1)}, u32[]{:S(2)}, u32[]{:S(2)}) collective-permute-start(f32[128,512]{1,0:T(8,128)S(1)} %get-tuple-element.24), channel_id=1, source_target_pairs={{0,7},{1,0},{2,1},{3,2},{4,3},{5,4},{6,5},{7,6},{8,15},{9,8},{10,9... | collective-permute-start | bytes 786440 | tf_op jit(solution)/shard_map/ppermute | solution.py:18
  114.0 4.7 %collective-permute-start.35 = (f32[4,512]{1,0:T(4,128)S(1)}, f32[4,512]{1,0:T(4,128)S(1)}, u32[]{:S(2)}, u32[]{:S(2)}) collective-permute-start(f32[4,512]{1,0:T(4,128)S(1)} %add.159), channel_id=1, source_target_pairs={{0,16},{8,24},{16,0},{24,8},{1,17},{9,25},{17,1},{25,9},{2,18},{10... | collective-permute-start | bytes 24584 | tf_op jit(solution)/shard_map/ppermute | solution.py:18
  (4 other events, 2.7 us)

commit v2 on v0

v2 whole, which is shorter than its diff:
```python
import functools

import jax
import jax.numpy as jnp
from jax import lax
from jax.experimental import pallas as pl
from jax.experimental.pallas import tpu as pltpu
from jax.sharding import PartitionSpec as P

ITERS = 2
CHUNKS = 1
LIMIT = 8 * 1024 * 1024

VMEM = pl.BlockSpec(memory_space=pltpu.VMEM)
SMEM = pl.BlockSpec(memory_space=pltpu.SMEM)
wide = jnp.float32
short = jnp.bfloat16
highest = lax.Precision.HIGHEST


def call(body, inputs, outputs, scratch=(), flops=0, scalars=1):
    moved = sum(x.size * x.dtype.itemsize for x in inputs)
    return pl.pallas_call(
        body,
        out_shape=[jax.ShapeDtypeStruct(shape, kind) for shape, kind in outputs],
        in_specs=[SMEM] * scalars + [VMEM] * (len(inputs) - scalars),
        out_specs=[VMEM] * len(outputs),
        scratch_shapes=[pltpu.VMEM(shape, kind) for shape, kind in scratch],
        compiler_params=pltpu.CompilerParams(vmem_limit_bytes=LIMIT),
        cost_estimate=pl.CostEstimate(flops=flops, bytes_accessed=moved, transcendentals=0),
    )(*inputs)


def move(array, axis, target):
    peers = lax.axis_size(axis)
    return lax.ppermute(array, axis, [(i, target(i) % peers) for i in range(peers)])


def near(i):
    return i ^ 1


def far(i):
    return i - 1 if i % 2 == 0 else i + 1


def swap_edges(parts):
    last = move(parts[3], "grp", far)
    return [
        move(parts[0], "sub", near),
        move(parts[1], "sub", far),
        move(parts[2], "grp", near),
        last,
    ]


def gather_members(array):
    peers = lax.axis_size("sub")
    same = [array] + [move(array, "sub", lambda i, k=k: i ^ k) for k in range(2, peers, 2)]
    return same + [move(one, "sub", near) for one in same]


def group_terms(array):
    peers = lax.axis_size("grp")
    if peers <= 4:
        return [array] + [move(array, "grp", lambda i, k=k: i + k) for k in range(1, peers)]
    step = 1
    while step < peers:
        array = array + move(array, "grp", lambda i, k=step: i ^ k)
        step *= 2
    return [array]


def dot(first, second, precision=None):
    return jnp.dot(first, second, precision=precision, preferred_element_type=wide)


def dot_across(first, second):
    return lax.dot_general(first, second, (((1,), (1,)), ((), ())), preferred_element_type=wide)


def halves(value):
    high = value.astype(short)
    return high, (value - high.astype(wide)).astype(short)


def put_triple(ref, rows, value):
    depth = ref.shape[0] // 3
    high, low = halves(value)
    ref[pl.ds(rows, value.shape[0])] = high
    ref[pl.ds(depth + rows, value.shape[0])] = low
    ref[pl.ds(2 * depth + rows, value.shape[0])] = high


def column_sum(first, second):
    return jnp.sum(first * second, axis=0, keepdims=True)


def turning(odd, pairing):
    face = pairing.shape[-1]
    place = lax.broadcasted_iota(jnp.int32, (face, face), 0)
    table = jnp.where(place == pairing, -1.0, 0.0)
    identity = jnp.where(place == lax.broadcasted_iota(jnp.int32, (face, face), 1), 1.0, 0.0)
    chosen = jnp.where(odd == 1, 1.0, 0.0)
    top = jnp.concatenate([identity * (1.0 - chosen), table * chosen], 1)
    bottom = jnp.concatenate([identity * chosen, table * (1.0 - chosen)], 1)
    return jnp.concatenate([top, bottom], 0).astype(short)


def turn_block(odd, pattern, block, pairing, out):
    face = pairing.shape[-1]
    pair = 2 * face
    depth = 2 * pair
    turns = [turning(odd[a], pairing[a : a + 1]) for a in range(2)]
    for a in range(2):
        for b in range(2):
            rows = []
            for i in range(2):
                rows.append(
                    jnp.concatenate(
                        [
                            block[
                                pl.ds((2 * a + i) * face, face), pl.ds((2 * b + j) * face, face)
                            ]
                            * pattern[2 * a + i, 2 * b + j].astype(wide)
                            for j in range(2)
                        ],
                        1,
                    )
                )
            for k, part in enumerate(halves(jnp.concatenate(rows, 0))):
                part = dot_across(dot(turns[a], part).astype(short), turns[b]).astype(short)
                here = pl.ds(a * pair, pair)
                if k == 0:
                    out[here, pl.ds(b * pair, pair)] = part
                    out[here, pl.ds(depth + b * pair, pair)] = part
                else:
                    out[here, pl.ds(2 * depth + b * pair, pair)] = part
    return turns


def dirichlet_kernel(odd, pattern, block, pairing, out):
    turn_block(odd, pattern, block, pairing, out)


def dual_kernel(odd, pattern, block, pairing, coupling, out, table, flat):
    turns = turn_block(odd, pattern, block, pairing, out)
    pair = 2 * pairing.shape[-1]
    depth = 2 * pair
    for a in range(2):
        here = pl.ds(a * pair, pair)
        high, low = (dot_across(v, turns[a]) for v in halves(coupling[:, here]))
        table[here] = (high + low).T
        flat[:, here] = high.astype(short)
        flat[:, pl.ds(depth + a * pair, pair)] = high.astype(short)
        flat[:, pl.ds(2 * depth + a * pair, pair)] = low.astype(short)


def label_kernel(member, weight, rows, out):
    corners = rows.shape[-1]
    out[...] = jnp.full(out.shape, -1.0, wide)
    out[:1, :corners] = weight[...]
    out[1:2, :corners] = rows[...].astype(wide)
    out[2:3, :corners] = jnp.full((1, corners), member[0, 0].astype(wide))


def table_kernel(coupling, *refs):
    labels, (apply, table, columns) = refs[:-3], refs[-3:]
    corners = coupling.shape[1]
    rows = corners + 8
    columns[...] = jnp.zeros(columns.shape, wide)
    for i, label in enumerate(labels):
        columns[pl.ds(i * rows, rows), :8] = label[...].T[:rows]
    across = columns[...].T
    weight, row, member = (across[i : i + 1] for i in range(3))
    same = (columns[:, 1:2] == row) & (columns[:, 2:3] == member) & (columns[:, 1:2] >= 0)
    linked = jnp.where(same, 1.0, 0.0)
    total = jnp.sum(linked * weight, axis=1, keepdims=True)
    table[...] = linked / jnp.where(total > 0, total, 1.0)
    high, low = halves(dot(coupling[...], table[:corners], highest))
    width = table.shape[1]
    apply[:, :width] = high
    apply[:, width : 2 * width] = high
    apply[:, 2 * width :] = low


def start_kernel(odd, matrix, right, upper, from_left, from_below, field, triple, last):
    face = from_left.shape[0]
    for axis, (own, other) in enumerate(((right, from_left), (upper, from_below))):
        here = pl.ds(2 * axis * face, face)
        there = pl.ds((2 * axis + 1) * face, face)
        first = jnp.where(odd[axis] == 1, other[...], own[...])
        second = jnp.where(odd[axis] == 1, own[...], other[...])
        field[here] = first
        field[there] = second
        put_triple(triple, 2 * axis * face, first)
        put_triple(triple, (2 * axis + 1) * face, second)
    last[...] = dot(matrix[pl.ds(3 * face, face)], triple[...])


def start_rest_kernel(matrix, triple, field, last, first, second, third, sums):
    face = last.shape[0]
    total = column_sum(field[pl.ds(3 * face, face)], last[...])
    local = dot(matrix[: 3 * face], triple[...])
    for i, out in enumerate((first, second, third)):
        out[...] = local[i * face : (i + 1) * face]
    sums[...] = jnp.broadcast_to(total + column_sum(field[: 3 * face], local), sums.shape)


def dual_first_kernel(matrix, flat, gamma, *refs):
    parts, others, (field, dense, message, triple) = refs[:4], refs[7:3:-1], refs[8:]
    face = parts[0].shape[0]
    corners = flat.shape[0]
    for i in range(4):
        value = parts[i][...] + others[i][...]
        field[pl.ds(i * face, face)] = value
        put_triple(triple, i * face, value)
    local = dot(matrix[...], triple[...])
    dense[...] = local
    message[:corners] = dot(flat[...], triple[...])
    message[pl.ds(corners, 8)] = jnp.zeros((8, field.shape[1]), wide)
    message[pl.ds(corners, 1)] = gamma[:1]
    message[pl.ds(corners + 1, 1)] = column_sum(field[...], local)


def coarse_last_kernel(table, dense, *refs):
    every, (triple, last) = refs[:-2], refs[-2:]
    face = last.shape[0]
    for i, message in enumerate(every):
        put_triple(triple, i * message.shape[0], message[...])
    last[...] = dense[pl.ds(3 * face, face)] + dot(table[pl.ds(3 * face, face)], triple[...])


def plane_sums(every, sizes, table, values, total):
    rows = every[0].shape[0]
    for i, message in enumerate(every):
        values[pl.ds(i * rows, rows)] = message[...]
    coarse = dot(table[...], values[...], highest)
    sums = every[0][pl.ds(rows - 8, 8)]
    for message in every[1:]:
        sums = sums + message[pl.ds(rows - 8, 8)]
    total[...] = sums
    for place, group in sizes:
        extra = jnp.zeros((1, total.shape[1]), wide)
        for i, message in enumerate(group):
            here = slice(i * rows, i * rows + rows - 8)
            extra = extra + column_sum(coarse[here], message[pl.ds(0, rows - 8)])
        total[pl.ds(place, 1)] = sums[place : place + 1] + extra


def coarse_rest_kernel(table, dense, triple, coarse_table, *refs):
    every, (first, second, third, total, values) = refs[:-5], refs[-5:]
    face = first.shape[0]
    local = dense[: 3 * face] + dot(table[: 3 * face], triple[...])
    first[...] = local[:face]
    second[...] = local[face : 2 * face]
    plane_sums(every, [(1, every)], coarse_table, values, total)
    third[:face] = local[2 * face :]
    third[pl.ds(face, 8)] = total[...]


def energy_kernel(count, table, *refs):
    total, values = refs[-2:]
    plane_sums(refs[:count], [(2, refs[:count]), (3, refs[count:-2])], table, values, total)


def second_last_kernel(matrix, total, *refs):
    parts, others, (field, triple, last) = refs[:4], refs[7:3:-1], refs[8:]
    face = parts[0].shape[0]
    for i in range(4):
        value = parts[i][:face] + others[i][:face]
        field[pl.ds(i * face, face)] = value
        put_triple(triple, i * face, value)
    last[:face] = dot(matrix[pl.ds(3 * face, face)], triple[...])
    last[pl.ds(face, 8)] = total[...] + others[2][pl.ds(face, 8)]


def second_rest_kernel(matrix, triple, *outs):
    face = outs[0].shape[0]
    local = dot(matrix[: 3 * face], triple[...])
    for i, out in enumerate(outs):
        out[...] = local[i * face : (i + 1) * face]


def added(refs):
    value = refs[0][...]
    for ref in refs[1:]:
        value = value + ref[...]
    return value


def dual_second_kernel(matrix, flat, residual, search, image, *refs):
    parts, others, totals = refs[:4], refs[7:3:-1], refs[8:-6]
    residual_next, search_next, dense, message, old_total, triple = refs[-6:]
    face = parts[0].shape[0]
    corners = flat.shape[0]
    if totals:
        total = added(totals)
    else:
        total = parts[3][pl.ds(face, 8)] + others[3][pl.ds(face, 8)]
    old_total[...] = total
    alpha = total[:1] / total[1:2]
    gamma = cross = jnp.zeros_like(alpha)
    for i in range(4):
        here = pl.ds(i * face, face)
        older = image[here]
        first = residual[here] - alpha * older
        second = search[here] - alpha * (parts[i][:face] + others[i][:face])
        residual_next[here] = first
        search_next[here] = second
        put_triple(triple, i * face, second)
        gamma = gamma + column_sum(first, second)
        cross = cross + column_sum(second, older)
    local = dot(matrix[...], triple[...])
    dense[...] = local
    message[:corners] = dot(flat[...], triple[...])
    message[pl.ds(corners, 8)] = jnp.zeros((8, local.shape[1]), wide)
    message[pl.ds(corners, 1)] = 0.5 * gamma
    message[pl.ds(corners + 1, 1)] = 0.5 * cross
    message[pl.ds(corners + 2, 1)] = column_sum(search_next[...], local)
    message[pl.ds(corners + 3, 1)] = column_sum(search[...], local)


def coarse_back_kernel(odd, table, dense, *refs):
    every, (back_sub, back_grp, own, triple) = refs[:-4], refs[-4:]
    face = back_sub.shape[0]
    for i, message in enumerate(every):
        put_triple(triple, i * message.shape[0], message[...])
    for axis, back in enumerate((back_sub, back_grp)):
        side = odd[axis] * face
        for out, rows, place in ((back, face, face - side), (own, face, side)):
            here = pl.ds(pl.multiple_of(2 * axis * face + place, face), face)
            value = dense[here] + dot(table[here], triple[...])
            if out is own:
                own[pl.ds(axis * face, face)] = value
            else:
                out[...] = value


def final_kernel(odd, own, residual, search, image, search_next, *refs):
    (from_right, from_above), totals, (solution, final) = refs[:2], refs[2:-2], refs[-2:]
    face = from_right.shape[0]
    older = totals[0]
    newer = added(totals[1:])
    gamma, slope = older[:1], older[1:2]
    alpha = gamma / slope
    gamma_next, cross, steep, cross_other = (newer[i : i + 1] for i in range(4))
    beta = gamma_next / gamma
    alpha_next = gamma_next / (steep + beta * (cross + cross_other + beta * slope))
    for axis, back in enumerate((from_right, from_above)):
        here = pl.ds(pl.multiple_of((2 * axis + odd[axis]) * face, face), face)
        out = pl.ds(axis * face, face)
        first = search[here]
        solution[out] = alpha * first + alpha_next * (search_next[here] + beta * first)
        newest = own[out] + back[...] + beta * image[here]
        final[out] = residual[here] - alpha_next * newest


def per_device(
    jump_data,
    dual_block,
    dirichlet_block,
    coupling,
    corner_weight,
    corner_rows,
    membership,
    face_pairing,
    block_pattern,
):
    face = face_pairing.shape[-1]
    corners = corner_rows.shape[-1]
    loads = jump_data.shape[-1] // CHUNKS
    depth = 4 * face
    rows = corners + 8
    members = lax.axis_size("sub")
    ride = lax.axis_size("grp") == 4
    pattern = block_pattern[0, 0]
    pairing = face_pairing[0, 0]
    odd = jnp.stack([lax.axis_index("sub") % 2, lax.axis_index("grp") % 2]).astype(jnp.int32)
    part = ((face, loads), wide)
    more = ((face + 8, loads), wide)
    eight = ((8, loads), wide)
    whole = ((depth, loads), wide)
    triple = ((3 * depth, loads), short)
    matrix = ((depth, 3 * depth), short)
    message = ((rows, loads), wide)
    gathered = ((3 * members * rows, loads), short)
    values = ((members * rows, loads), wide)
    work = 6 * depth * depth * loads
    chunks = range(CHUNKS)

    jump = jump_data[0, 0]
    starts = []
    for i in chunks:
        columns = slice(i * loads, (i + 1) * loads)
        right, upper = jump[:face, columns], jump[face:, columns]
        from_below = move(upper, "grp", lambda i: i + 1)
        from_left = move(right, "sub", lambda i: i + 1)
        starts.append((right, upper, from_left, from_below))
    (label,) = call(
        label_kernel, [membership, corner_weight[0], corner_rows[0]], [((8, 128), wide)]
    )
    labels = gather_members(label)
    (dirichlet,) = call(
        dirichlet_kernel,
        [odd, pattern, dirichlet_block[0, 0], pairing],
        [matrix],
        flops=4 * depth * depth * depth,
        scalars=2,
    )
    steps = []
    labels[0], dirichlet, *labels[1:] = lax.optimization_barrier(
        (labels[0], dirichlet, *labels[1:])
    )
    for right, upper, from_left, from_below in starts:
        residual, field, last = call(
            start_kernel,
            [odd, dirichlet, right, upper, from_left, from_below],
            [whole, triple, part],
            flops=work // 4,
        )
        *parts, gamma_part = call(
            start_rest_kernel,
            [dirichlet, field, residual, last],
            [part] * 3 + [eight],
            flops=work,
            scalars=0,
        )
        steps.append((residual, gamma_part, parts + [last]))
    steps = [(r, g, p, swap_edges(p)) for r, g, p in steps]

    others = steps[0][3]
    odd_given, others[0] = lax.optimization_barrier((odd, others[0]))
    dual, coupling_table, coupling_flat = call(
        dual_kernel,
        [odd_given, pattern, dual_block[0, 0], pairing, coupling[0, 0].T],
        [matrix, ((depth, corners), wide), ((corners, 3 * depth), short)],
        flops=4 * depth * depth * depth,
        scalars=2,
    )
    apply_table, coarse_table = call(
        table_kernel,
        [coupling_table, *labels],
        [((depth, 3 * members * rows), short), ((members * rows, members * rows), wide)],
        [((members * rows, 128), wide)],
        scalars=0,
    )
    gamma_part, apply_table, coarse_table = lax.optimization_barrier(
        (steps[0][1], apply_table, coarse_table)
    )
    steps[0] = (steps[0][0], gamma_part, *steps[0][2:])

    firsts = []
    for residual, gamma_part, parts, others in steps:
        search, dense, sent = call(
            dual_first_kernel,
            [dual, coupling_flat, gamma_part, *parts, *others[::-1]],
            [whole, whole, message],
            [triple],
            flops=work,
            scalars=0,
        )
        firsts.append((search, dense, gather_members(sent)))
    images = []
    for _, dense, every in firsts:
        field, last = call(
            coarse_last_kernel, [apply_table, dense, *every], [gathered, part], scalars=0
        )
        *parts, total = call(
            coarse_rest_kernel,
            [apply_table, dense, field, coarse_table, *every],
            [part, part, more, eight],
            [values],
            scalars=0,
        )
        images.append((total, parts + [last], swap_edges(parts + [last])))
    seconds = []
    for total, parts, others in images:
        image, field, last = call(
            second_last_kernel,
            [dirichlet, total, *parts, *others[::-1]],
            [whole, triple, more],
            flops=work // 4,
            scalars=0,
        )
        parts = call(second_rest_kernel, [dirichlet, field], [part] * 3, flops=work, scalars=0)
        parts = list(parts) + [last]
        totals = [] if ride else group_terms(total)
        seconds.append((image, totals, parts, swap_edges(parts)))
    thirds = []
    for (residual, *_), (search, *_), (image, totals, parts, others) in zip(steps, firsts, seconds):
        *kept, sent, old_total = call(
            dual_second_kernel,
            [dual, coupling_flat, residual, search, image, *parts, *others[::-1], *totals],
            [whole, whole, whole, message, eight],
            [triple],
            flops=work,
            scalars=0,
        )
        thirds.append((*kept, old_total, gather_members(sent)))
    results = []
    for (search, _, older), (image, *_), (residual, search_next, dense, old_total, every) in zip(
        firsts, seconds, thirds
    ):
        (total,) = call(
            functools.partial(energy_kernel, members),
            [coarse_table, *every, *older],
            [eight],
            [values],
            scalars=0,
        )
        totals = group_terms(total)
        back_sub, back_grp, own = call(
            coarse_back_kernel,
            [odd, apply_table, dense, *every],
            [part, part, ((2 * face, loads), wide)],
            [gathered],
        )
        from_above = move(back_grp, "grp", lambda i: i - 1)
        from_right = move(back_sub, "sub", lambda i: i - 1)
        results.append(
            call(
                final_kernel,
                [
                    odd,
                    own,
                    residual,
                    search,
                    image,
                    search_next,
                    from_right,
                    from_above,
                    old_total,
                    *totals,
                ],
                [((2 * face, loads), wide)] * 2,
            )
        )
    if CHUNKS > 1:
        results = [[jnp.concatenate(pieces, 1) for pieces in zip(*results)]]
    (solution, final) = results[0]
    return (solution[None, None], final[None, None])


def solution(mesh):
    placed = (
        P("grp", "sub", None, None),
        P("grp", "sub", None, None),
        P("grp", "sub", None, None),
        P("grp", "sub", None, None),
        P("grp", "sub", None),
        P("grp", "sub", None),
        P("grp", "sub"),
        P("grp", "sub", None, None),
        P("grp", "sub", None, None),
    )
    return jax.shard_map(
        per_device,
        mesh=mesh,
        in_specs=placed,
        out_specs=(P("grp", "sub", None, None), P("grp", "sub", None, None)),
        check_vma=False,
    )
```

time: 261 us -> 102 us (0.39)
  blocking collectives: 159 us -> 0 us
  matrix products: 17.6 us -> 0 us
  starting transfers between devices: 18.5 us -> 35.8 us
  Pallas kernels: 0 us -> 14.6 us
  waiting for transfers between devices: 53.6 us -> 45.9 us
  other arithmetic: 4.21 us -> 0.07 us
  local copies, waits for them, and re-layouts: 6.6 us -> 3.85 us
    psum x3 -> x0, blocking collectives: 115 us -> none  [the longest x2 76.7 us: residual_product(): return lax.psum(column_sum(residual, search), ('grp', 'sub'))]
    all_gather x4 -> x0, blocking collectives: 37.1 us -> none  [the longest x2 20.5 us: coarse_apply(): lax.all_gather(corner_values[None, None], 'sub', axis=1, tiled=True)[0]]
    dot_general x27 -> x0, matrix products: 17.6 us -> none  [the longest x24 16.5 us: matmul(): jnp.dot(first, second, precision=highest, preferred_element_type=jnp.floa...]
    ppermute x16 -> x40, starting transfers between devices: 18.5 us -> 35.8 us  [move(): lax.ppermute(array, axis, [(i, target(i) % peers) for i in range(peers)])]
    pallas_call x0 -> x15, Pallas kernels: none -> 14.6 us  [call(): pl.pallas_call(body, out_shape=[jax.ShapeDtypeStruct(shape, kind) for sha...]
    ppermute x16 -> x40, waiting for transfers between devices: 53.6 us -> 45.9 us  [move(): lax.ppermute(array, axis, [(i, target(i) % peers) for i in range(peers)])]
    unnamed x1 -> x0, blocking collectives: 6.92 us -> none
    sub x6 -> x0, other arithmetic: 2.65 us -> none  [the longest x2 2.33 us: per_device(): residual = residual - alpha * image]
  transfers between devices with their start and end apart: 16 -> 40, of which waited for: 14 -> 23; matrix products, arithmetic and copies ran while one was open for 1% -> 0% of each run, Pallas kernels for 0% -> 5%
where the time goes in v2:
time: 102 us
  waiting for transfers between devices  45.9 us (45%)
  starting transfers between devices  35.8 us (35%)
  Pallas kernels  14.6 us (14%)
  local copies, waits for them, and re-layouts  3.85 us (4%)
  between operations  1.53 us (2%)
    ppermute x40, waiting for transfers between devices, move(): lax.ppermute(array, axis, [(i, target(i) % peers) for i in range(peers)])  45.9 us
    ppermute x40, starting transfers between devices, move(): lax.ppermute(array, axis, [(i, target(i) % peers) for i in range(peers)])  35.8 us
    pallas_call x15, Pallas kernels, call(): pl.pallas_call(body, out_shape=[jax.ShapeDtypeStruct(shape, kind) for sha...  14.6 us
    unnamed x18, local copies, waits for them, and re-layouts  2.69 us
  transfers between devices with their start and end apart: 40, of which 23 were waited for; matrix products, arithmetic and copies ran while one was open for 0% of the time, Pallas kernels for 5%

profile of v2, /device:TPU:0, one launch (start us, length us, event | category | flops | bytes accessed | tf_op | source)
XLA Modules:
  0.0 101.8 jit_solution(2901462134742052852)
XLA Ops:
  0.6 1.2 %slice_bitcast_fusion = (f32[128,512]{1,0:T(8,128)S(1)}, f32[128,512]{1,0:T(8,128)S(1)}) fusion(f32[1,1,256,512]{3,2,1,0:T(8,128)} %param.9), kind=kLoop, calls=%fused_computation | loop fusion | bytes 1048576 | tf_op jit(solution)/shard_map/slice | solution.py:396
  1.8 3.1 %collective-permute-start.8 = (f32[128,512]{1,0:T(8,128)S(1)}, f32[128,512]{1,0:T(8,128)S(1)}, u32[]{:S(2)}, u32[]{:S(2)}) collective-permute-start(f32[128,512]{1,0:T(8,128)S(1)} %get-tuple-element.104.upper), channel_id=1, source_target_pairs={{0,8},{8,16},{16,24},{24,0},{1,9},{9,17},{17,25},{25,1},{2,10},{10... | collective-permute-start | bytes 786440 | tf_op jit(solution)/shard_map/ppermute | solution.py:36
  6.8 1.6 %collective-permute-start.3 = (f32[8,128]{1,0:T(8,128)S(1)}, f32[8,128]{1,0:T(8,128)S(1)}, u32[]{:S(2)}, u32[]{:S(2)}) collective-permute-start(f32[8,128]{1,0:T(8,128)S(1)} %shard_map.104.refs_0_), channel_id=1, source_target_pairs={{0,1},{1,0},{2,3},{3,2},{4,5},{5,4},{6,7},{7,6},{8,9},{9,8},{10,11... | collective-permute-start | bytes 12296 | tf_op jit(solution)/shard_map/ppermute | solution.py:36
  8.4 1.4 %collective-permute-start.2 = (f32[8,128]{1,0:T(8,128)S(1)}, f32[8,128]{1,0:T(8,128)S(1)}, u32[]{:S(2)}, u32[]{:S(2)}) collective-permute-start(f32[8,128]{1,0:T(8,128)S(1)} %shard_map.104.refs_0_), channel_id=1, source_target_pairs={{0,6},{1,7},{2,4},{3,5},{4,2},{5,3},{6,0},{7,1},{8,14},{9,15},{10,... | collective-permute-start | bytes 12296 | tf_op jit(solution)/shard_map/ppermute | solution.py:36
  9.9 1.5 %collective-permute-start.1 = (f32[8,128]{1,0:T(8,128)S(1)}, f32[8,128]{1,0:T(8,128)S(1)}, u32[]{:S(2)}, u32[]{:S(2)}) collective-permute-start(f32[8,128]{1,0:T(8,128)S(1)} %shard_map.104.refs_0_), channel_id=1, source_target_pairs={{0,4},{1,5},{2,6},{3,7},{4,0},{5,1},{6,2},{7,3},{8,12},{9,13},{10,... | collective-permute-start | bytes 12296 | tf_op jit(solution)/shard_map/ppermute | solution.py:36
  12.0 0.9 collective-permute-done.2.refs_3_
  13.5 1.5 %collective-permute-done.refs_1_ = f32[8,128]{1,0:T(8,128)S(1)} collective-permute-done((f32[8,128]{1,0:T(8,128)S(1)}, f32[8,128]{1,0:T(8,128)S(1)}, u32[]{:S(2)}, u32[]{:S(2)}) %collective-permute-start) | collective-permute-done | bytes 4128 | tf_op jit(solution)/shard_map/ppermute | solution.py:36
  16.4 1.4 %shard_map.105.matrix = bf16[512,1536]{1,0:T(8,128)(2,1)S(1)} custom-call(s32[2]{0:T(128)S(1)} %pad_add_fusion.odd, s32[4,4]{1,0:T(4,128)S(1)} %bitcast.18, f32[512,512]{1,0:T(8,128)S(1)} %bitcast.17, s32[2,128]{1,0:T(2,128)S(1)} %bitcast.20), custom_call_target="tpu_custom_call" | custom-call | flops 536870912 | bytes 1049672 | tf_op jit(solution)/shard_map/pallas_call | solution.py:23
  17.8 1.1 %shard_map.106 = (f32[512,512]{1,0:T(8,128)S(1)}, bf16[1536,512]{1,0:T(8,128)(2,1)S(1)}, f32[128,512]{1,0:T(8,128)S(1)}) custom-call(s32[2]{0:T(128)S(1)} %pad_add_fusion.odd, bf16[512,1536]{1,0:T(8,128)(2,1)S(1)} %shard_map.105.matrix, f32[128,512]{1,0:T(8,128)S(1)} %get-tuple-element.105.right, f32[128,512]{1,0:T(8,128)S(1)} %get-tuple-element.104.upper, ...), custom_call_target="tpu_custom_call" | custom-call | flops 201326592 | bytes 2621448 | tf_op jit(solution)/shard_map/pallas_call | solution.py:23
  19.0 0.8 shard_map.107
  20.4 1.2 %collective-permute-start.12 = (f32[128,512]{1,0:T(8,128)S(1)}, f32[128,512]{1,0:T(8,128)S(1)}, u32[]{:S(2)}, u32[]{:S(2)}) collective-permute-start(f32[128,512]{1,0:T(8,128)S(1)} %get-tuple-element.75.refs_1_), channel_id=1, source_target_pairs={{0,7},{1,2},{2,1},{3,4},{4,3},{5,6},{6,5},{7,0},{8,15},{9,10},{10,... | collective-permute-start | bytes 786440 | tf_op jit(solution)/shard_map/ppermute | solution.py:36
  21.5 1.6 %collective-permute-start.11 = (f32[128,512]{1,0:T(8,128)S(1)}, f32[128,512]{1,0:T(8,128)S(1)}, u32[]{:S(2)}, u32[]{:S(2)}) collective-permute-start(f32[128,512]{1,0:T(8,128)S(1)} %get-tuple-element.76.refs_2_), channel_id=1, source_target_pairs={{0,8},{8,0},{16,24},{24,16},{1,9},{9,1},{17,25},{25,17},{2,10},{10... | collective-permute-start | bytes 786440 | tf_op jit(solution)/shard_map/ppermute | solution.py:36
  23.1 2.5 %collective-permute-start.10 = (f32[128,512]{1,0:T(8,128)S(1)}, f32[128,512]{1,0:T(8,128)S(1)}, u32[]{:S(2)}, u32[]{:S(2)}) collective-permute-start(f32[128,512]{1,0:T(8,128)S(1)} %get-tuple-element.56.last.refs_3_), channel_id=1, source_target_pairs={{0,24},{8,16},{16,8},{24,0},{1,25},{9,17},{17,9},{25,1},{2,26},{10... | collective-permute-start | bytes 786440 | tf_op jit(solution)/shard_map/ppermute | solution.py:36
  25.6 1.6 %shard_map.108 = (bf16[512,1536]{1,0:T(8,128)(2,1)S(1)}, f32[512,24]{1,0:T(8,128)S(1)}, bf16[24,1536]{1,0:T(8,128)(2,1)S(1)}) custom-call(s32[2]{0:T(128)S(1)} %pad_add_fusion.odd, s32[4,4]{1,0:T(4,128)S(1)} %bitcast.19, f32[512,512]{1,0:T(8,128)S(1)} %bitcast.24, s32[2,128]{1,0:T(2,128)S(1)} %bitcast.21, f32[24,512]{1,0:T(8,128)S(1)} %bitcast.25), custom_call_target="tpu_custom_call" | custom-call | flops 536870912 | bytes 1098824 | tf_op jit(solution)/shard_map/pallas_call | solution.py:23
  27.2 0.9 shard_map.109
  28.1 1.1 %collective-permute-done.12.refs_6_ = f32[128,512]{1,0:T(8,128)S(1)} collective-permute-done((f32[128,512]{1,0:T(8,128)S(1)}, f32[128,512]{1,0:T(8,128)S(1)}, u32[]{:S(2)}, u32[]{:S(2)}) %collective-permute-start.12) | collective-permute-done | bytes 262176 | tf_op jit(solution)/shard_map/ppermute | solution.py:36
  29.9 7.0 %collective-permute-done.10.refs_4_ = f32[128,512]{1,0:T(8,128)S(1)} collective-permute-done((f32[128,512]{1,0:T(8,128)S(1)}, f32[128,512]{1,0:T(8,128)S(1)}, u32[]{:S(2)}, u32[]{:S(2)}) %collective-permute-start.10) | collective-permute-done | bytes 262176 | tf_op jit(solution)/shard_map/ppermute | solution.py:36
  36.9 1.3 %shard_map.110 = (f32[512,512]{1,0:T(8,128)S(1)}, f32[512,512]{1,0:T(8,128)S(1)}, f32[32,512]{1,0:T(8,128)S(1)}) custom-call(bf16[512,1536]{1,0:T(8,128)(2,1)S(1)} %get-tuple-element.72.matrix, bf16[24,1536]{1,0:T(8,128)(2,1)S(1)} %get-tuple-element.73.flat, f32[8,512]{1,0:T(8,128)S(1)} %get-tuple-element.74.gamma, ...), custom_call_target="tpu_custom_call" | custom-call | flops 805306368 | bytes 3760128 | tf_op jit(solution)/shard_map/pallas_call | solution.py:23
  38.1 1.6 %collective-permute-start.15 = (f32[32,512]{1,0:T(8,128)S(1)}, f32[32,512]{1,0:T(8,128)S(1)}, u32[]{:S(2)}, u32[]{:S(2)}) collective-permute-start(f32[32,512]{1,0:T(8,128)S(1)} %get-tuple-element.80.refs_0_.refs_8_), channel_id=1, source_target_pairs={{0,6},{1,7},{2,4},{3,5},{4,2},{5,3},{6,0},{7,1},{8,14},{9,15},{10,... | collective-permute-start | bytes 196616 | tf_op jit(solution)/shard_map/ppermute | solution.py:36
  39.8 1.3 %collective-permute-start.14 = (f32[32,512]{1,0:T(8,128)S(1)}, f32[32,512]{1,0:T(8,128)S(1)}, u32[]{:S(2)}, u32[]{:S(2)}) collective-permute-start(f32[32,512]{1,0:T(8,128)S(1)} %get-tuple-element.80.refs_0_.refs_8_), channel_id=1, source_target_pairs={{0,4},{1,5},{2,6},{3,7},{4,0},{5,1},{6,2},{7,3},{8,12},{9,13},{10,... | collective-permute-start | bytes 196616 | tf_op jit(solution)/shard_map/ppermute | solution.py:36
  41.6 1.8 %collective-permute-done.15.refs_3_.refs_11_ = f32[32,512]{1,0:T(8,128)S(1)} collective-permute-done((f32[32,512]{1,0:T(8,128)S(1)}, f32[32,512]{1,0:T(8,128)S(1)}, u32[]{:S(2)}, u32[]{:S(2)}) %collective-permute-start.15) | collective-permute-done | bytes 65568 | tf_op jit(solution)/shard_map/ppermute | solution.py:36
  43.4 0.9 collective-permute-done.14.refs_2_.refs_10_
  44.3 0.9 collective-permute-done.13.refs_1_.refs_9_
  45.6 1.0 collective-permute-done.17.refs_5_.refs_13_
  46.9 0.9 shard_map.112
  48.1 1.5 %collective-permute-start.22 = (f32[128,512]{1,0:T(8,128)S(1)}, f32[128,512]{1,0:T(8,128)S(1)}, u32[]{:S(2)}, u32[]{:S(2)}) collective-permute-start(f32[128,512]{1,0:T(8,128)S(1)} %get-tuple-element.85.refs_1_), channel_id=1, source_target_pairs={{0,7},{1,2},{2,1},{3,4},{4,3},{5,6},{6,5},{7,0},{8,15},{9,10},{10,... | collective-permute-start | bytes 786440 | tf_op jit(solution)/shard_map/ppermute | solution.py:36
  49.6 2.0 %collective-permute-start.20 = (f32[128,512]{1,0:T(8,128)S(1)}, f32[128,512]{1,0:T(8,128)S(1)}, u32[]{:S(2)}, u32[]{:S(2)}) collective-permute-start(f32[128,512]{1,0:T(8,128)S(1)} %get-tuple-element.87.refs_3_), channel_id=1, source_target_pairs={{0,24},{8,16},{16,8},{24,0},{1,25},{9,17},{17,9},{25,1},{2,26},{10... | collective-permute-start | bytes 786440 | tf_op jit(solution)/shard_map/ppermute | solution.py:36
  51.6 5.9 %collective-permute-done.22.refs_6_ = f32[128,512]{1,0:T(8,128)S(1)} collective-permute-done((f32[128,512]{1,0:T(8,128)S(1)}, f32[128,512]{1,0:T(8,128)S(1)}, u32[]{:S(2)}, u32[]{:S(2)}) %collective-permute-start.22) | collective-permute-done | bytes 262176 | tf_op jit(solution)/shard_map/ppermute | solution.py:36
  57.5 4.8 %collective-permute-done.20.refs_4_ = f32[128,512]{1,0:T(8,128)S(1)} collective-permute-done((f32[128,512]{1,0:T(8,128)S(1)}, f32[128,512]{1,0:T(8,128)S(1)}, u32[]{:S(2)}, u32[]{:S(2)}) %collective-permute-start.20) | collective-permute-done | bytes 262176 | tf_op jit(solution)/shard_map/ppermute | solution.py:36
  62.8 2.1 %collective-permute-start.24 = (f32[136,512]{1,0:T(8,128)S(1)}, f32[136,512]{1,0:T(8,128)S(1)}, u32[]{:S(2)}, u32[]{:S(2)}) collective-permute-start(f32[136,512]{1,0:T(8,128)S(1)} %get-tuple-element.93.refs_3_), channel_id=1, source_target_pairs={{0,24},{8,16},{16,8},{24,0},{1,25},{9,17},{17,9},{25,1},{2,26},{10... | collective-permute-start | bytes 835592 | tf_op jit(solution)/shard_map/ppermute | solution.py:36
  65.8 1.6 %collective-permute-start.26 = (f32[128,512]{1,0:T(8,128)S(1)}, f32[128,512]{1,0:T(8,128)S(1)}, u32[]{:S(2)}, u32[]{:S(2)}) collective-permute-start(f32[128,512]{1,0:T(8,128)S(1)} %get-tuple-element.91.refs_1_), channel_id=1, source_target_pairs={{0,7},{1,2},{2,1},{3,4},{4,3},{5,6},{6,5},{7,0},{8,15},{9,10},{10,... | collective-permute-start | bytes 786440 | tf_op jit(solution)/shard_map/ppermute | solution.py:36
  67.5 1.4 %collective-permute-start.25 = (f32[128,512]{1,0:T(8,128)S(1)}, f32[128,512]{1,0:T(8,128)S(1)}, u32[]{:S(2)}, u32[]{:S(2)}) collective-permute-start(f32[128,512]{1,0:T(8,128)S(1)} %get-tuple-element.92.refs_2_), channel_id=1, source_target_pairs={{0,8},{8,0},{16,24},{24,16},{1,9},{9,1},{17,25},{25,17},{2,10},{10... | collective-permute-start | bytes 786440 | tf_op jit(solution)/shard_map/ppermute | solution.py:36
  68.9 6.5 %collective-permute-done.26.refs_6_ = f32[128,512]{1,0:T(8,128)S(1)} collective-permute-done((f32[128,512]{1,0:T(8,128)S(1)}, f32[128,512]{1,0:T(8,128)S(1)}, u32[]{:S(2)}, u32[]{:S(2)}) %collective-permute-start.26) | collective-permute-done | bytes 262176 | tf_op jit(solution)/shard_map/ppermute | solution.py:36
  75.4 2.9 %collective-permute-done.25.refs_5_ = f32[128,512]{1,0:T(8,128)S(1)} collective-permute-done((f32[128,512]{1,0:T(8,128)S(1)}, f32[128,512]{1,0:T(8,128)S(1)}, u32[]{:S(2)}, u32[]{:S(2)}) %collective-permute-start.25) | collective-permute-done | bytes 262176 | tf_op jit(solution)/shard_map/ppermute | solution.py:36
  78.3 1.5 %shard_map.115 = (f32[512,512]{1,0:T(8,128)S(1)}, f32[512,512]{1,0:T(8,128)S(1)}, f32[512,512]{1,0:T(8,128)S(1)}, f32[32,512]{1,0:T(8,128)S(1)}, f32[8,512]{1,0:T(8,128)S(1)}) custom-call(bf16[512,1536]{1,0:T(8,128)(2,1)S(1)} %get-tuple-element.72.matrix, bf16[24,1536]{1,0:T(8,128)(2,1)S(1)} %get-tuple-element.73.flat, ...), custom_call_target="tpu_custom_call" | custom-call | flops 805306368 | bytes 6922240 | tf_op jit(solution)/shard_map/pallas_call | solution.py:23
  79.8 1.6 %collective-permute-start.30 = (f32[32,512]{1,0:T(8,128)S(1)}, f32[32,512]{1,0:T(8,128)S(1)}, u32[]{:S(2)}, u32[]{:S(2)}) collective-permute-start(f32[32,512]{1,0:T(8,128)S(1)} %get-tuple-element.95.refs_0_), channel_id=1, source_target_pairs={{0,6},{1,7},{2,4},{3,5},{4,2},{5,3},{6,0},{7,1},{8,14},{9,15},{10,... | collective-permute-start | bytes 196616 | tf_op jit(solution)/shard_map/ppermute | solution.py:36
  81.4 1.0 collective-permute-start.29
  82.3 1.0 collective-permute-start.28
  83.3 1.8 %collective-permute-done.30.refs_3_ = f32[32,512]{1,0:T(8,128)S(1)} collective-permute-done((f32[32,512]{1,0:T(8,128)S(1)}, f32[32,512]{1,0:T(8,128)S(1)}, u32[]{:S(2)}, u32[]{:S(2)}) %collective-permute-start.30) | collective-permute-done | bytes 65568 | tf_op jit(solution)/shard_map/ppermute | solution.py:36
  85.1 1.1 %collective-permute-done.29.refs_2_ = f32[32,512]{1,0:T(8,128)S(1)} collective-permute-done((f32[32,512]{1,0:T(8,128)S(1)}, f32[32,512]{1,0:T(8,128)S(1)}, u32[]{:S(2)}, u32[]{:S(2)}) %collective-permute-start.29) | collective-permute-done | bytes 65568 | tf_op jit(solution)/shard_map/ppermute | solution.py:36
  87.8 1.2 %shard_map.116 = (f32[128,512]{1,0:T(8,128)S(1)}, f32[128,512]{1,0:T(8,128)S(1)}, f32[256,512]{1,0:T(8,128)S(1)}) custom-call(s32[2]{0:T(128)S(1)} %pad_add_fusion.odd, bf16[512,768]{1,0:T(8,128)(2,1)S(1)} %get-tuple-element.71.table, f32[512,512]{1,0:T(8,128)S(1)} %get-tuple-element.94.dense, f32[32,512]{1,0:T(8,128)S(1)} %get-tuple-element.95.refs_0_, ...), custom_call_target="tpu_custom_call" | custom-call | bytes 2359304 | tf_op jit(solution)/shard_map/pallas_call | solution.py:23
  89.0 1.3 %collective-permute-start.35 = (f32[128,512]{1,0:T(8,128)S(1)}, f32[128,512]{1,0:T(8,128)S(1)}, u32[]{:S(2)}, u32[]{:S(2)}) collective-permute-start(f32[128,512]{1,0:T(8,128)S(1)} %get-tuple-element.99), channel_id=1, source_target_pairs={{0,7},{1,0},{2,1},{3,2},{4,3},{5,4},{6,5},{7,6},{8,15},{9,8},{10,9... | collective-permute-start | bytes 786440 | tf_op jit(solution)/shard_map/ppermute | solution.py:36
  90.3 2.4 %collective-permute-start.36 = (f32[128,512]{1,0:T(8,128)S(1)}, f32[128,512]{1,0:T(8,128)S(1)}, u32[]{:S(2)}, u32[]{:S(2)}) collective-permute-start(f32[128,512]{1,0:T(8,128)S(1)} %get-tuple-element.100), channel_id=1, source_target_pairs={{0,24},{8,0},{16,8},{24,16},{1,25},{9,1},{17,9},{25,17},{2,26},{10... | collective-permute-start | bytes 786440 | tf_op jit(solution)/shard_map/ppermute | solution.py:36
  93.7 0.9 collective-permute-start.38
  94.6 0.9 collective-permute-start.37
  95.5 3.0 %collective-permute-done.39.refs_6_ = f32[8,512]{1,0:T(8,128)S(1)} collective-permute-done((f32[8,512]{1,0:T(8,128)S(1)}, f32[8,512]{1,0:T(8,128)S(1)}, u32[]{:S(2)}, u32[]{:S(2)}) %collective-permute-start.39) | collective-permute-done | bytes 16416 | tf_op jit(solution)/shard_map/ppermute | solution.py:36
  99.1 1.0 %collective-permute-done.37.refs_4_ = f32[8,512]{1,0:T(8,128)S(1)} collective-permute-done((f32[8,512]{1,0:T(8,128)S(1)}, f32[8,512]{1,0:T(8,128)S(1)}, u32[]{:S(2)}, u32[]{:S(2)}) %collective-permute-start.37) | collective-permute-done | bytes 16416 | tf_op jit(solution)/shard_map/ppermute | solution.py:36
  100.1 1.7 %shard_map.118 = (f32[256,512]{1,0:T(8,128)}, f32[256,512]{1,0:T(8,128)}) custom-call(s32[2]{0:T(128)S(1)} %pad_add_fusion.odd, f32[256,512]{1,0:T(8,128)S(1)} %get-tuple-element.96.own, f32[512,512]{1,0:T(8,128)S(1)} %get-tuple-element.97.residual, f32[512,512]{1,0:T(8,128)S(1)} %get-tuple-element.78.search, f32[512,512]{1,0:T(8,128)S(1)} %get-tuple-element.88.image, ...), custom_call_target="tpu_custom_call" | custom-call | bytes 5324808 | tf_op jit(solution)/shard_map/pallas_call | solution.py:23
  (67 shorter events, 11.3 us)
Async XLA Ops:
  0.6 14.4 %copy-start = (f32[1,1,512,512]{3,2,1,0:T(8,128)S(1)}, f32[1,1,512,512]{3,2,1,0:T(8,128)}, u32[]{:S(2)}) copy-start(f32[1,1,512,512]{3,2,1,0:T(8,128)} %param.11) | copy-start | bytes 3145732
  1.8 16.0 %collective-permute-start.8 = (f32[128,512]{1,0:T(8,128)S(1)}, f32[128,512]{1,0:T(8,128)S(1)}, u32[]{:S(2)}, u32[]{:S(2)}) collective-permute-start(f32[128,512]{1,0:T(8,128)S(1)} %get-tuple-element.104.upper), channel_id=1, source_target_pairs={{0,8},{8,16},{16,24},{24,0},{1,9},{9,17},{17,25},{25,1},{2,10},{10... | collective-permute-start | bytes 786440 | tf_op jit(solution)/shard_map/ppermute | solution.py:36
  4.9 12.9 %collective-permute-start.7 = (f32[128,512]{1,0:T(8,128)S(1)}, f32[128,512]{1,0:T(8,128)S(1)}, u32[]{:S(2)}, u32[]{:S(2)}) collective-permute-start(f32[128,512]{1,0:T(8,128)S(1)} %get-tuple-element.105.right), channel_id=1, source_target_pairs={{0,1},{1,2},{2,3},{3,4},{4,5},{5,6},{6,7},{7,0},{8,9},{9,10},{10,1... | collective-permute-start | bytes 786440 | tf_op jit(solution)/shard_map/ppermute | solution.py:36
  5.5 0.7 copy-start.5
  6.8 4.6 %collective-permute-start.3 = (f32[8,128]{1,0:T(8,128)S(1)}, f32[8,128]{1,0:T(8,128)S(1)}, u32[]{:S(2)}, u32[]{:S(2)}) collective-permute-start(f32[8,128]{1,0:T(8,128)S(1)} %shard_map.104.refs_0_), channel_id=1, source_target_pairs={{0,1},{1,0},{2,3},{3,2},{4,5},{5,4},{6,7},{7,6},{8,9},{9,8},{10,11... | collective-permute-start | bytes 12296 | tf_op jit(solution)/shard_map/ppermute | solution.py:36
  8.4 4.5 %collective-permute-start.2 = (f32[8,128]{1,0:T(8,128)S(1)}, f32[8,128]{1,0:T(8,128)S(1)}, u32[]{:S(2)}, u32[]{:S(2)}) collective-permute-start(f32[8,128]{1,0:T(8,128)S(1)} %shard_map.104.refs_0_), channel_id=1, source_target_pairs={{0,6},{1,7},{2,4},{3,5},{4,2},{5,3},{6,0},{7,1},{8,14},{9,15},{10,... | collective-permute-start | bytes 12296 | tf_op jit(solution)/shard_map/ppermute | solution.py:36
  9.9 3.6 %collective-permute-start.1 = (f32[8,128]{1,0:T(8,128)S(1)}, f32[8,128]{1,0:T(8,128)S(1)}, u32[]{:S(2)}, u32[]{:S(2)}) collective-permute-start(f32[8,128]{1,0:T(8,128)S(1)} %shard_map.104.refs_0_), channel_id=1, source_target_pairs={{0,4},{1,5},{2,6},{3,7},{4,0},{5,1},{6,2},{7,3},{8,12},{9,13},{10,... | collective-permute-start | bytes 12296 | tf_op jit(solution)/shard_map/ppermute | solution.py:36
  11.4 3.6 %collective-permute-start = (f32[8,128]{1,0:T(8,128)S(1)}, f32[8,128]{1,0:T(8,128)S(1)}, u32[]{:S(2)}, u32[]{:S(2)}) collective-permute-start(f32[8,128]{1,0:T(8,128)S(1)} %shard_map.104.refs_0_), channel_id=1, source_target_pairs={{0,2},{1,3},{2,0},{3,1},{4,6},{5,7},{6,4},{7,5},{8,10},{9,11},{10,... | collective-permute-start | bytes 12296 | tf_op jit(solution)/shard_map/ppermute | solution.py:36
  13.0 4.8 %collective-permute-start.6 = (f32[8,128]{1,0:T(8,128)S(1)}, f32[8,128]{1,0:T(8,128)S(1)}, u32[]{:S(2)}, u32[]{:S(2)}) collective-permute-start(f32[8,128]{1,0:T(8,128)S(1)} %collective-permute-done.2.refs_3_), channel_id=1, source_target_pairs={{0,1},{1,0},{2,3},{3,2},{4,5},{5,4},{6,7},{7,6},{8,9},{9,8},{10,11... | collective-permute-start | bytes 12296 | tf_op jit(solution)/shard_map/ppermute | solution.py:36
  13.5 4.3 %collective-permute-start.5 = (f32[8,128]{1,0:T(8,128)S(1)}, f32[8,128]{1,0:T(8,128)S(1)}, u32[]{:S(2)}, u32[]{:S(2)}) collective-permute-start(f32[8,128]{1,0:T(8,128)S(1)} %collective-permute-done.1.refs_2_), channel_id=1, source_target_pairs={{0,1},{1,0},{2,3},{3,2},{4,5},{5,4},{6,7},{7,6},{8,9},{9,8},{10,11... | collective-permute-start | bytes 12296 | tf_op jit(solution)/shard_map/ppermute | solution.py:36
  15.0 2.8 %collective-permute-start.4 = (f32[8,128]{1,0:T(8,128)S(1)}, f32[8,128]{1,0:T(8,128)S(1)}, u32[]{:S(2)}, u32[]{:S(2)}) collective-permute-start(f32[8,128]{1,0:T(8,128)S(1)} %collective-permute-done.refs_1_), channel_id=1, source_target_pairs={{0,1},{1,0},{2,3},{3,2},{4,5},{5,4},{6,7},{7,6},{8,9},{9,8},{10,11... | collective-permute-start | bytes 12296 | tf_op jit(solution)/shard_map/ppermute | solution.py:36
  15.0 0.7 copy-start.1
  15.7 0.7 copy-start.3
  18.9 6.6 %copy-start.2 = (s32[1,1,4,4]{3,2,1,0:T(4,128)S(1)}, s32[1,1,4,4]{3,2,1,0:T(4,128)}, u32[]{:S(2)}) copy-start(s32[1,1,4,4]{3,2,1,0:T(4,128)} %param.17) | copy-start | bytes 196
  19.0 6.6 %copy-start.4 = (s32[1,1,2,128]{3,2,1,0:T(2,128)S(1)}, s32[1,1,2,128]{3,2,1,0:T(2,128)}, u32[]{:S(2)}) copy-start(s32[1,1,2,128]{3,2,1,0:T(2,128)} %param.16) | copy-start | bytes 3076
  19.0 6.6 %copy-start.7 = (f32[1,1,512,512]{3,2,1,0:T(8,128)S(1)}, f32[1,1,512,512]{3,2,1,0:T(8,128)}, u32[]{:S(2)}) copy-start(f32[1,1,512,512]{3,2,1,0:T(8,128)} %param.10) | copy-start | bytes 3145732
  19.0 6.6 %copy-start.8 = (f32[1,1,512,24]{2,3,1,0:T(8,128)S(1)}, f32[1,1,512,24]{2,3,1,0:T(8,128)}, u32[]{:S(2)}) copy-start(f32[1,1,512,24]{2,3,1,0:T(8,128)} %param.12) | copy-start | bytes 147460
  19.8 5.8 %collective-permute-start.9 = (f32[128,512]{1,0:T(8,128)S(1)}, f32[128,512]{1,0:T(8,128)S(1)}, u32[]{:S(2)}, u32[]{:S(2)}) collective-permute-start(f32[128,512]{1,0:T(8,128)S(1)} %get-tuple-element.58.refs_0_), channel_id=1, source_target_pairs={{0,1},{1,0},{2,3},{3,2},{4,5},{5,4},{6,7},{7,6},{8,9},{9,8},{10,11... | collective-permute-start | bytes 786440 | tf_op jit(solution)/shard_map/ppermute | solution.py:36
  20.4 8.8 %collective-permute-start.12 = (f32[128,512]{1,0:T(8,128)S(1)}, f32[128,512]{1,0:T(8,128)S(1)}, u32[]{:S(2)}, u32[]{:S(2)}) collective-permute-start(f32[128,512]{1,0:T(8,128)S(1)} %get-tuple-element.75.refs_1_), channel_id=1, source_target_pairs={{0,7},{1,2},{2,1},{3,4},{4,3},{5,6},{6,5},{7,0},{8,15},{9,10},{10,... | collective-permute-start | bytes 786440 | tf_op jit(solution)/shard_map/ppermute | solution.py:36
  21.5 8.3 %collective-permute-start.11 = (f32[128,512]{1,0:T(8,128)S(1)}, f32[128,512]{1,0:T(8,128)S(1)}, u32[]{:S(2)}, u32[]{:S(2)}) collective-permute-start(f32[128,512]{1,0:T(8,128)S(1)} %get-tuple-element.76.refs_2_), channel_id=1, source_target_pairs={{0,8},{8,0},{16,24},{24,16},{1,9},{9,1},{17,25},{25,17},{2,10},{10... | collective-permute-start | bytes 786440 | tf_op jit(solution)/shard_map/ppermute | solution.py:36
  23.1 13.8 %collective-permute-start.10 = (f32[128,512]{1,0:T(8,128)S(1)}, f32[128,512]{1,0:T(8,128)S(1)}, u32[]{:S(2)}, u32[]{:S(2)}) collective-permute-start(f32[128,512]{1,0:T(8,128)S(1)} %get-tuple-element.56.last.refs_3_), channel_id=1, source_target_pairs={{0,24},{8,16},{16,8},{24,0},{1,25},{9,17},{17,9},{25,1},{2,26},{10... | collective-permute-start | bytes 786440 | tf_op jit(solution)/shard_map/ppermute | solution.py:36
  38.1 5.3 %collective-permute-start.15 = (f32[32,512]{1,0:T(8,128)S(1)}, f32[32,512]{1,0:T(8,128)S(1)}, u32[]{:S(2)}, u32[]{:S(2)}) collective-permute-start(f32[32,512]{1,0:T(8,128)S(1)} %get-tuple-element.80.refs_0_.refs_8_), channel_id=1, source_target_pairs={{0,6},{1,7},{2,4},{3,5},{4,2},{5,3},{6,0},{7,1},{8,14},{9,15},{10,... | collective-permute-start | bytes 196616 | tf_op jit(solution)/shard_map/ppermute | solution.py:36
  39.8 4.6 %collective-permute-start.14 = (f32[32,512]{1,0:T(8,128)S(1)}, f32[32,512]{1,0:T(8,128)S(1)}, u32[]{:S(2)}, u32[]{:S(2)}) collective-permute-start(f32[32,512]{1,0:T(8,128)S(1)} %get-tuple-element.80.refs_0_.refs_8_), channel_id=1, source_target_pairs={{0,4},{1,5},{2,6},{3,7},{4,0},{5,1},{6,2},{7,3},{8,12},{9,13},{10,... | collective-permute-start | bytes 196616 | tf_op jit(solution)/shard_map/ppermute | solution.py:36
  41.0 4.3 %collective-permute-start.13 = (f32[32,512]{1,0:T(8,128)S(1)}, f32[32,512]{1,0:T(8,128)S(1)}, u32[]{:S(2)}, u32[]{:S(2)}) collective-permute-start(f32[32,512]{1,0:T(8,128)S(1)} %get-tuple-element.80.refs_0_.refs_8_), channel_id=1, source_target_pairs={{0,2},{1,3},{2,0},{3,1},{4,6},{5,7},{6,4},{7,5},{8,10},{9,11},{10,... | collective-permute-start | bytes 196616 | tf_op jit(solution)/shard_map/ppermute | solution.py:36
  41.6 3.7 %collective-permute-start.16 = (f32[32,512]{1,0:T(8,128)S(1)}, f32[32,512]{1,0:T(8,128)S(1)}, u32[]{:S(2)}, u32[]{:S(2)}) collective-permute-start(f32[32,512]{1,0:T(8,128)S(1)} %get-tuple-element.80.refs_0_.refs_8_), channel_id=1, source_target_pairs={{0,1},{1,0},{2,3},{3,2},{4,5},{5,4},{6,7},{7,6},{8,9},{9,8},{10,11... | collective-permute-start | bytes 196616 | tf_op jit(solution)/shard_map/ppermute | solution.py:36
  43.4 1.9 %collective-permute-start.19 = (f32[32,512]{1,0:T(8,128)S(1)}, f32[32,512]{1,0:T(8,128)S(1)}, u32[]{:S(2)}, u32[]{:S(2)}) collective-permute-start(f32[32,512]{1,0:T(8,128)S(1)} %collective-permute-done.15.refs_3_.refs_11_), channel_id=1, source_target_pairs={{0,1},{1,0},{2,3},{3,2},{4,5},{5,4},{6,7},{7,6},{8,9},{9,8},{10,11... | collective-permute-start | bytes 196616 | tf_op jit(solution)/shard_map/ppermute | solution.py:36
  44.3 1.3 %collective-permute-start.18 = (f32[32,512]{1,0:T(8,128)S(1)}, f32[32,512]{1,0:T(8,128)S(1)}, u32[]{:S(2)}, u32[]{:S(2)}) collective-permute-start(f32[32,512]{1,0:T(8,128)S(1)} %collective-permute-done.14.refs_2_.refs_10_), channel_id=1, source_target_pairs={{0,1},{1,0},{2,3},{3,2},{4,5},{5,4},{6,7},{7,6},{8,9},{9,8},{10,11... | collective-permute-start | bytes 196616 | tf_op jit(solution)/shard_map/ppermute | solution.py:36
  45.3 1.3 %collective-permute-start.17 = (f32[32,512]{1,0:T(8,128)S(1)}, f32[32,512]{1,0:T(8,128)S(1)}, u32[]{:S(2)}, u32[]{:S(2)}) collective-permute-start(f32[32,512]{1,0:T(8,128)S(1)} %collective-permute-done.13.refs_1_.refs_9_), channel_id=1, source_target_pairs={{0,1},{1,0},{2,3},{3,2},{4,5},{5,4},{6,7},{7,6},{8,9},{9,8},{10,11... | collective-permute-start | bytes 196616 | tf_op jit(solution)/shard_map/ppermute | solution.py:36
  47.8 14.5 %collective-permute-start.21 = (f32[136,512]{1,0:T(8,128)S(1)}, f32[136,512]{1,0:T(8,128)S(1)}, u32[]{:S(2)}, u32[]{:S(2)}) collective-permute-start(f32[136,512]{1,0:T(8,128)S(1)} %get-tuple-element.86.refs_2_), channel_id=1, source_target_pairs={{0,8},{8,0},{16,24},{24,16},{1,9},{9,1},{17,25},{25,17},{2,10},{10... | collective-permute-start | bytes 835592 | tf_op jit(solution)/shard_map/ppermute | solution.py:36
  47.9 3.7 %collective-permute-start.23 = (f32[128,512]{1,0:T(8,128)S(1)}, f32[128,512]{1,0:T(8,128)S(1)}, u32[]{:S(2)}, u32[]{:S(2)}) collective-permute-start(f32[128,512]{1,0:T(8,128)S(1)} %get-tuple-element.84.refs_0_), channel_id=1, source_target_pairs={{0,1},{1,0},{2,3},{3,2},{4,5},{5,4},{6,7},{7,6},{8,9},{9,8},{10,11... | collective-permute-start | bytes 786440 | tf_op jit(solution)/shard_map/ppermute | solution.py:36
  48.1 9.4 %collective-permute-start.22 = (f32[128,512]{1,0:T(8,128)S(1)}, f32[128,512]{1,0:T(8,128)S(1)}, u32[]{:S(2)}, u32[]{:S(2)}) collective-permute-start(f32[128,512]{1,0:T(8,128)S(1)} %get-tuple-element.85.refs_1_), channel_id=1, source_target_pairs={{0,7},{1,2},{2,1},{3,4},{4,3},{5,6},{6,5},{7,0},{8,15},{9,10},{10,... | collective-permute-start | bytes 786440 | tf_op jit(solution)/shard_map/ppermute | solution.py:36
  49.6 12.7 %collective-permute-start.20 = (f32[128,512]{1,0:T(8,128)S(1)}, f32[128,512]{1,0:T(8,128)S(1)}, u32[]{:S(2)}, u32[]{:S(2)}) collective-permute-start(f32[128,512]{1,0:T(8,128)S(1)} %get-tuple-element.87.refs_3_), channel_id=1, source_target_pairs={{0,24},{8,16},{16,8},{24,0},{1,25},{9,17},{17,9},{25,1},{2,26},{10... | collective-permute-start | bytes 786440 | tf_op jit(solution)/shard_map/ppermute | solution.py:36
  62.8 15.4 %collective-permute-start.24 = (f32[136,512]{1,0:T(8,128)S(1)}, f32[136,512]{1,0:T(8,128)S(1)}, u32[]{:S(2)}, u32[]{:S(2)}) collective-permute-start(f32[136,512]{1,0:T(8,128)S(1)} %get-tuple-element.93.refs_3_), channel_id=1, source_target_pairs={{0,24},{8,16},{16,8},{24,0},{1,25},{9,17},{17,9},{25,1},{2,26},{10... | collective-permute-start | bytes 835592 | tf_op jit(solution)/shard_map/ppermute | solution.py:36
  65.8 3.1 %collective-permute-start.27 = (f32[128,512]{1,0:T(8,128)S(1)}, f32[128,512]{1,0:T(8,128)S(1)}, u32[]{:S(2)}, u32[]{:S(2)}) collective-permute-start(f32[128,512]{1,0:T(8,128)S(1)} %get-tuple-element.90.refs_0_), channel_id=1, source_target_pairs={{0,1},{1,0},{2,3},{3,2},{4,5},{5,4},{6,7},{7,6},{8,9},{9,8},{10,11... | collective-permute-start | bytes 786440 | tf_op jit(solution)/shard_map/ppermute | solution.py:36
  65.8 9.5 %collective-permute-start.26 = (f32[128,512]{1,0:T(8,128)S(1)}, f32[128,512]{1,0:T(8,128)S(1)}, u32[]{:S(2)}, u32[]{:S(2)}) collective-permute-start(f32[128,512]{1,0:T(8,128)S(1)} %get-tuple-element.91.refs_1_), channel_id=1, source_target_pairs={{0,7},{1,2},{2,1},{3,4},{4,3},{5,6},{6,5},{7,0},{8,15},{9,10},{10,... | collective-permute-start | bytes 786440 | tf_op jit(solution)/shard_map/ppermute | solution.py:36
  67.5 10.8 %collective-permute-start.25 = (f32[128,512]{1,0:T(8,128)S(1)}, f32[128,512]{1,0:T(8,128)S(1)}, u32[]{:S(2)}, u32[]{:S(2)}) collective-permute-start(f32[128,512]{1,0:T(8,128)S(1)} %get-tuple-element.92.refs_2_), channel_id=1, source_target_pairs={{0,8},{8,0},{16,24},{24,16},{1,9},{9,1},{17,25},{25,17},{2,10},{10... | collective-permute-start | bytes 786440 | tf_op jit(solution)/shard_map/ppermute | solution.py:36
  79.8 5.3 %collective-permute-start.30 = (f32[32,512]{1,0:T(8,128)S(1)}, f32[32,512]{1,0:T(8,128)S(1)}, u32[]{:S(2)}, u32[]{:S(2)}) collective-permute-start(f32[32,512]{1,0:T(8,128)S(1)} %get-tuple-element.95.refs_0_), channel_id=1, source_target_pairs={{0,6},{1,7},{2,4},{3,5},{4,2},{5,3},{6,0},{7,1},{8,14},{9,15},{10,... | collective-permute-start | bytes 196616 | tf_op jit(solution)/shard_map/ppermute | solution.py:36
  81.4 4.8 %collective-permute-start.29 = (f32[32,512]{1,0:T(8,128)S(1)}, f32[32,512]{1,0:T(8,128)S(1)}, u32[]{:S(2)}, u32[]{:S(2)}) collective-permute-start(f32[32,512]{1,0:T(8,128)S(1)} %get-tuple-element.95.refs_0_), channel_id=1, source_target_pairs={{0,4},{1,5},{2,6},{3,7},{4,0},{5,1},{6,2},{7,3},{8,12},{9,13},{10,... | collective-permute-start | bytes 196616 | tf_op jit(solution)/shard_map/ppermute | solution.py:36
  82.3 4.3 %collective-permute-start.28 = (f32[32,512]{1,0:T(8,128)S(1)}, f32[32,512]{1,0:T(8,128)S(1)}, u32[]{:S(2)}, u32[]{:S(2)}) collective-permute-start(f32[32,512]{1,0:T(8,128)S(1)} %get-tuple-element.95.refs_0_), channel_id=1, source_target_pairs={{0,2},{1,3},{2,0},{3,1},{4,6},{5,7},{6,4},{7,5},{8,10},{9,11},{10,... | collective-permute-start | bytes 196616 | tf_op jit(solution)/shard_map/ppermute | solution.py:36
  83.3 3.3 %collective-permute-start.31 = (f32[32,512]{1,0:T(8,128)S(1)}, f32[32,512]{1,0:T(8,128)S(1)}, u32[]{:S(2)}, u32[]{:S(2)}) collective-permute-start(f32[32,512]{1,0:T(8,128)S(1)} %get-tuple-element.95.refs_0_), channel_id=1, source_target_pairs={{0,1},{1,0},{2,3},{3,2},{4,5},{5,4},{6,7},{7,6},{8,9},{9,8},{10,11... | collective-permute-start | bytes 196616 | tf_op jit(solution)/shard_map/ppermute | solution.py:36
  85.1 1.6 %collective-permute-start.34 = (f32[32,512]{1,0:T(8,128)S(1)}, f32[32,512]{1,0:T(8,128)S(1)}, u32[]{:S(2)}, u32[]{:S(2)}) collective-permute-start(f32[32,512]{1,0:T(8,128)S(1)} %collective-permute-done.30.refs_3_), channel_id=1, source_target_pairs={{0,1},{1,0},{2,3},{3,2},{4,5},{5,4},{6,7},{7,6},{8,9},{9,8},{10,11... | collective-permute-start | bytes 196616 | tf_op jit(solution)/shard_map/ppermute | solution.py:36
  86.1 1.3 %collective-permute-start.33 = (f32[32,512]{1,0:T(8,128)S(1)}, f32[32,512]{1,0:T(8,128)S(1)}, u32[]{:S(2)}, u32[]{:S(2)}) collective-permute-start(f32[32,512]{1,0:T(8,128)S(1)} %collective-permute-done.29.refs_2_), channel_id=1, source_target_pairs={{0,1},{1,0},{2,3},{3,2},{4,5},{5,4},{6,7},{7,6},{8,9},{9,8},{10,11... | collective-permute-start | bytes 196616 | tf_op jit(solution)/shard_map/ppermute | solution.py:36
  86.6 1.3 %collective-permute-start.32 = (f32[32,512]{1,0:T(8,128)S(1)}, f32[32,512]{1,0:T(8,128)S(1)}, u32[]{:S(2)}, u32[]{:S(2)}) collective-permute-start(f32[32,512]{1,0:T(8,128)S(1)} %collective-permute-done.28.refs_1_), channel_id=1, source_target_pairs={{0,1},{1,0},{2,3},{3,2},{4,5},{5,4},{6,7},{7,6},{8,9},{9,8},{10,11... | collective-permute-start | bytes 196616 | tf_op jit(solution)/shard_map/ppermute | solution.py:36
  89.0 11.1 %collective-permute-start.35 = (f32[128,512]{1,0:T(8,128)S(1)}, f32[128,512]{1,0:T(8,128)S(1)}, u32[]{:S(2)}, u32[]{:S(2)}) collective-permute-start(f32[128,512]{1,0:T(8,128)S(1)} %get-tuple-element.99), channel_id=1, source_target_pairs={{0,7},{1,0},{2,1},{3,2},{4,3},{5,4},{6,5},{7,6},{8,15},{9,8},{10,9... | collective-permute-start | bytes 786440 | tf_op jit(solution)/shard_map/ppermute | solution.py:36
  90.3 9.8 %collective-permute-start.36 = (f32[128,512]{1,0:T(8,128)S(1)}, f32[128,512]{1,0:T(8,128)S(1)}, u32[]{:S(2)}, u32[]{:S(2)}) collective-permute-start(f32[128,512]{1,0:T(8,128)S(1)} %get-tuple-element.100), channel_id=1, source_target_pairs={{0,24},{8,0},{16,8},{24,16},{1,25},{9,1},{17,9},{25,17},{2,26},{10... | collective-permute-start | bytes 786440 | tf_op jit(solution)/shard_map/ppermute | solution.py:36
  93.4 5.1 %collective-permute-start.39 = (f32[8,512]{1,0:T(8,128)S(1)}, f32[8,512]{1,0:T(8,128)S(1)}, u32[]{:S(2)}, u32[]{:S(2)}) collective-permute-start(f32[8,512]{1,0:T(8,128)S(1)} %shard_map.117.refs_3_), channel_id=1, source_target_pairs={{0,24},{8,0},{16,8},{24,16},{1,25},{9,1},{17,9},{25,17},{2,26},{10... | collective-permute-start | bytes 49160 | tf_op jit(solution)/shard_map/ppermute | solution.py:36
  93.7 5.4 %collective-permute-start.38 = (f32[8,512]{1,0:T(8,128)S(1)}, f32[8,512]{1,0:T(8,128)S(1)}, u32[]{:S(2)}, u32[]{:S(2)}) collective-permute-start(f32[8,512]{1,0:T(8,128)S(1)} %shard_map.117.refs_3_), channel_id=1, source_target_pairs={{0,16},{8,24},{16,0},{24,8},{1,17},{9,25},{17,1},{25,9},{2,18},{10... | collective-permute-start | bytes 49160 | tf_op jit(solution)/shard_map/ppermute | solution.py:36
  94.6 5.5 %collective-permute-start.37 = (f32[8,512]{1,0:T(8,128)S(1)}, f32[8,512]{1,0:T(8,128)S(1)}, u32[]{:S(2)}, u32[]{:S(2)}) collective-permute-start(f32[8,512]{1,0:T(8,128)S(1)} %shard_map.117.refs_3_), channel_id=1, source_target_pairs={{0,8},{8,16},{16,24},{24,0},{1,9},{9,17},{17,25},{25,1},{2,10},{10... | collective-permute-start | bytes 49160 | tf_op jit(solution)/shard_map/ppermute | solution.py:36
  (1 other events, 0.7 us)

commit v3 on v0

v3 whole, which is shorter than its diff:
```python
import functools

import jax
import jax.numpy as jnp
from jax import lax
from jax.experimental import pallas as pl
from jax.experimental.pallas import tpu as pltpu
from jax.sharding import PartitionSpec as P

ITERS = 2
LIMIT = 8 * 1024 * 1024

VMEM = pl.BlockSpec(memory_space=pltpu.VMEM)
SMEM = pl.BlockSpec(memory_space=pltpu.SMEM)
wide = jnp.float32
short = jnp.bfloat16
highest = lax.Precision.HIGHEST


def call(body, inputs, outputs, scratch=(), flops=0, scalars=1):
    moved = sum(x.size * x.dtype.itemsize for x in inputs)
    return pl.pallas_call(
        body,
        out_shape=[jax.ShapeDtypeStruct(shape, kind) for shape, kind in outputs],
        in_specs=[SMEM] * scalars + [VMEM] * (len(inputs) - scalars),
        out_specs=[VMEM] * len(outputs),
        scratch_shapes=[pltpu.VMEM(shape, kind) for shape, kind in scratch],
        compiler_params=pltpu.CompilerParams(vmem_limit_bytes=LIMIT),
        cost_estimate=pl.CostEstimate(flops=flops, bytes_accessed=moved, transcendentals=0),
    )(*inputs)


def move(array, axis, target):
    peers = lax.axis_size(axis)
    return lax.ppermute(array, axis, [(i, target(i) % peers) for i in range(peers)])


def near(i):
    return i ^ 1


def far(i):
    return i - 1 if i % 2 == 0 else i + 1


def swap_edges(parts):
    return [
        move(parts[0], "sub", near),
        move(parts[1], "sub", far),
        move(parts[2], "grp", near),
        move(parts[3], "grp", far),
    ]


def gather_members(array):
    return lax.all_gather(array, "sub", axis=0, tiled=True)


def group_terms(array):
    peers = lax.axis_size("grp")
    if peers <= 4:
        return [array] + [move(array, "grp", lambda i, k=k: i + k) for k in range(1, peers)]
    step = 1
    while step < peers:
        array = array + move(array, "grp", lambda i, k=step: i ^ k)
        step *= 2
    return [array]


def dot(first, second, precision=None):
    return jnp.dot(first, second, precision=precision, preferred_element_type=wide)


def dot_across(first, second):
    return lax.dot_general(first, second, (((1,), (1,)), ((), ())), preferred_element_type=wide)


def halves(value):
    high = value.astype(short)
    return high, (value - high.astype(wide)).astype(short)


def put_triple(ref, rows, value, base=0, depth=None):
    depth = depth or ref.shape[0] // 3
    high, low = halves(value)
    for i, part in enumerate((high, low, high)):
        ref[pl.ds(base + i * depth + rows, value.shape[0])] = part


def parities():
    return lax.axis_index("sub") % 2, lax.axis_index("grp") % 2


def far_sub():
    sub, peers = lax.axis_index("sub"), lax.axis_size("sub")
    return lax.rem(jnp.where(sub % 2 == 1, sub + 1, sub + peers - 1), peers)


def column_sum(first, second):
    return jnp.sum(first * second, axis=0, keepdims=True)


def turning(odd, pairing):
    face = pairing.shape[-1]
    place = lax.broadcasted_iota(jnp.int32, (face, face), 0)
    table = jnp.where(place == pairing, -1.0, 0.0)
    identity = jnp.where(place == lax.broadcasted_iota(jnp.int32, (face, face), 1), 1.0, 0.0)
    chosen = jnp.where(odd == 1, 1.0, 0.0)
    top = jnp.concatenate([identity * (1.0 - chosen), table * chosen], 1)
    bottom = jnp.concatenate([identity * chosen, table * (1.0 - chosen)], 1)
    return jnp.concatenate([top, bottom], 0).astype(short)


def turn_block(pattern, block, pairing, out):
    face = pairing.shape[-1]
    pair = 2 * face
    odd = parities()
    turns = [turning(odd[a], pairing[a : a + 1]) for a in range(2)]
    for a in range(2):
        for b in range(2):
            rows = []
            for i in range(2):
                rows.append(
                    jnp.concatenate(
                        [
                            block[
                                pl.ds((2 * a + i) * face, face), pl.ds((2 * b + j) * face, face)
                            ]
                            * pattern[2 * a + i, 2 * b + j].astype(wide)
                            for j in range(2)
                        ],
                        1,
                    )
                )
            for k, part in enumerate(halves(jnp.concatenate(rows, 0))):
                part = dot_across(dot(turns[a], part).astype(short), turns[b]).astype(short)
                here = pl.ds(a * pair, pair)
                for i in (0, 1) if k == 0 else (2,):
                    out[here, pl.ds((3 * b + i) * pair, pair)] = part
    return turns


def dual_kernel(pattern, block, pairing, out):
    turn_block(pattern, block, pairing, out)


def put_table(out, rows, value):
    high, low = halves(value)
    width = value.shape[1]
    for i, part in enumerate((high, high, low)):
        out[rows, pl.ds(32 * i, width)] = part


def put_values(out, value):
    high, low = halves(value)
    for i, part in enumerate((high, low, high)):
        out[pl.ds(32 * i, 32)] = part
    out[pl.ds(96, 32)] = jnp.zeros((32, value.shape[1]), short)


def dirichlet_kernel(pattern, block, pairing, coupling, out, flat, table, *slips):
    every_turn = turn_block(pattern, block, pairing, out)
    face = pairing.shape[-1]
    pair = 2 * face
    table[...] = jnp.zeros(table.shape, short)
    for a, turns in enumerate(every_turn):
        here = pl.ds(a * pair, pair)
        high, low = (dot_across(v, turns) for v in halves(coupling[:, here]))
        for i, half in enumerate((high, high, low)):
            flat[:, pl.ds((3 * a + i) * pair, pair)] = half.astype(short)
        total = high + low
        put_table(table, here, total.T)
        for i in range(2):
            slip = slips[2 * a + i]
            slip[...] = jnp.zeros(slip.shape, wide)
            for k in range(coupling.shape[0] // 8):
                slip[:, pl.ds(k * face, face)] = total[
                    8 * k : 8 * k + 8, i * face : (i + 1) * face
                ]


def neighbour_kernel(corners, *refs):
    for message, out in zip(refs[:2], refs[2:]):
        face = out.shape[0]
        slip = message[pl.ds(face, 8)]
        parts = [slip[:, k * face : (k + 1) * face] for k in range(corners // 8)]
        out[...] = jnp.zeros(out.shape, short)
        put_table(out, pl.ds(0, face), jnp.concatenate(parts, 0).T)


def label_kernel(member, weight, rows, out):
    corners = rows.shape[-1]
    out[...] = jnp.full(out.shape, -1.0, wide)
    out[:1, :corners] = weight[...]
    out[1:2, :corners] = rows[...].astype(wide)
    out[2:3, :corners] = jnp.full((1, corners), member[0, 0].astype(wide))


def table_kernel(labels, table, columns):
    rows = 32
    columns[...] = jnp.zeros(columns.shape, wide)
    for i in range(labels.shape[0] // 8):
        columns[pl.ds(i * rows, rows), :8] = labels[pl.ds(8 * i, 8)].T[:rows]
    across = columns[...].T
    weight, row, member = (across[i : i + 1] for i in range(3))
    same = (columns[:, 1:2] == row) & (columns[:, 2:3] == member) & (columns[:, 1:2] >= 0)
    linked = jnp.where(same, 1.0, 0.0)
    total = jnp.sum(linked * weight, axis=1, keepdims=True)
    high, low = halves(linked / jnp.where(total > 0, total, 1.0))
    width = table.shape[0]
    table[:, :width] = high
    table[:, width : 2 * width] = high
    table[:, 2 * width :] = low


def start_kernel(matrix, right, upper, from_left, from_below, field, triple, last):
    face = from_left.shape[0]
    odd = parities()
    for axis, (own, other) in enumerate(((right, from_left), (upper, from_below))):
        here = pl.ds(2 * axis * face, face)
        there = pl.ds((2 * axis + 1) * face, face)
        first = jnp.where(odd[axis] == 1, other[...], own[...])
        second = jnp.where(odd[axis] == 1, own[...], other[...])
        field[here] = first
        field[there] = second
        put_triple(triple, 0, first, 6 * axis * face, 2 * face)
        put_triple(triple, face, second, 6 * axis * face, 2 * face)
    last[...] = dot(matrix[pl.ds(3 * face, face)], triple[...])


def start_rest_kernel(matrix, triple, field, last, *refs):
    slips, (first, second, third, fourth, sums) = refs[:4], refs[4:]
    face = last.shape[0]
    total = column_sum(field[pl.ds(3 * face, face)], last[...])
    local = dot(matrix[: 3 * face], triple[...])
    for i, out in enumerate((first, second, third)):
        out[:face] = local[i * face : (i + 1) * face]
    fourth[:face] = last[...]
    for out, slip in zip((first, second, third, fourth), slips):
        out[pl.ds(face, 8)] = slip[...]
    sums[...] = jnp.broadcast_to(total + column_sum(field[: 3 * face], local), sums.shape)


def both_dots(matrix, *triples):
    width = triples[0].shape[0]
    return dot(matrix[:, :width], triples[0][...]) + dot(matrix[:, width:], triples[1][...])


def edges_kernel(third, fourth, far_one, near_one, field, triple):
    face = far_one.shape[0] - 8
    for i, (part, other) in enumerate(((third, near_one), (fourth, far_one))):
        value = part[:face] + other[:face]
        field[pl.ds(i * face, face)] = value
        put_triple(triple, i * face, value)


def dual_first_kernel(matrix, flat, gamma, field_grp, triple_grp, *refs):
    parts, others, (field, *outs, message, triple) = refs[:2], refs[2:4], refs[4:]
    face = outs[0].shape[0]
    corners = flat.shape[0]
    for i in range(2):
        value = parts[i][:face] + others[i][:face]
        field[pl.ds(i * face, face)] = value
        put_triple(triple, i * face, value)
    field[pl.ds(2 * face, 2 * face)] = field_grp[...]
    local = both_dots(matrix, triple, triple_grp)
    for i, out in enumerate(outs):
        out[...] = local[i * face : (i + 1) * face]
    message[:corners] = both_dots(flat, triple, triple_grp)
    message[pl.ds(corners, 8)] = jnp.zeros((8, field.shape[1]), wide)
    message[pl.ds(corners, 1)] = gamma[:1]
    message[pl.ds(corners + 1, 1)] = column_sum(field[...], local)


def coarse_kernel(corners, second, table, coupling, near_table, far_table, *refs):
    count = 2 if second else 1
    every, (passed, extra, triple, coarse, values) = refs[:count], refs[count:]
    rows = passed.shape[0]
    face = near_table.shape[0]
    put_triple(triple, 0, every[0][...])
    coarse[...] = dot(table[...], triple[...])
    sums = jnp.zeros((8, passed.shape[1]), wide)
    extras = [jnp.zeros((1, passed.shape[1]), wide) for _ in range(count)]
    for i in range(every[0].shape[0] // rows):
        here = pl.ds(i * rows, corners)
        sums = sums + every[0][pl.ds(i * rows + corners, 8)]
        for j in range(count):
            extras[j] = extras[j] + column_sum(coarse[here], every[j][here])
    sub = lax.axis_index("sub")
    own, partner, other = (
        pl.ds(pl.multiple_of(place * rows, rows), rows) for place in (sub, sub ^ 1, far_sub())
    )
    passed[...] = coarse[own]
    passed[pl.ds(corners, 8)] = sums
    for j, one in enumerate(extras):
        place = count + j
        passed[pl.ds(corners + place, 1)] = sums[place : place + 1] + one
    put_values(values, coarse[own])
    extra[...] = dot(coupling[...], values[...])
    put_values(values, coarse[partner])
    extra[:face] += dot(near_table[...], values[...])
    put_values(values, coarse[other])
    extra[pl.ds(face, face)] += dot(far_table[...], values[...])


def second_edges_kernel(corners, *refs):
    (extra, near_table, far_table, passed, near_passed, far_passed, *refs) = refs
    (third, fourth, far_one, near_one, field, triple, passing, sums, values) = refs
    face = third.shape[0]
    sides = ((third, near_one, near_table, near_passed), (fourth, far_one, far_table, far_passed))
    for i, (part, other, table, more) in enumerate(sides):
        put_values(values, more[...])
        value = part[...] + other[...] + extra[pl.ds((2 + i) * face, face)]
        value = value + dot(table[...], values[...])
        field[pl.ds(i * face, face)] = value
        put_triple(triple, i * face, value)
    eight = pl.ds(corners, 8)
    passing[...] = far_passed[eight]
    sums[...] = passed[eight] + near_passed[eight] + far_passed[eight]


def second_kernel(matrix, extra, passing, field_grp, triple_grp, *refs):
    parts, others, (field, *outs, triple) = refs[:2], refs[2:4], refs[4:]
    face = parts[0].shape[0]
    for i in range(2):
        here = pl.ds(i * face, face)
        value = parts[i][...] + others[i][...] + extra[here]
        field[here] = value
        put_triple(triple, i * face, value)
    field[pl.ds(2 * face, 2 * face)] = field_grp[...]
    local = both_dots(matrix, triple, triple_grp)
    for i, out in enumerate(outs):
        out[:face] = local[i * face : (i + 1) * face]
    outs[2][pl.ds(face, 8)] = passing[...]


def added(refs):
    value = refs[0][...]
    for ref in refs[1:]:
        value = value + ref[...]
    return value


def step_rows(total, residual, search, image, later, rows, residual_next, search_next):
    alpha = total[:1] / total[1:2]
    older = image[rows]
    first = residual[rows] - alpha * older
    second = search[rows] - alpha * later
    residual_next[...] = first
    search_next[...] = second
    return second, column_sum(first, second), column_sum(second, older)


def step_edges_kernel(residual, search, image, third, fourth, far_one, near_one, *refs):
    totals, (residual_next, search_next, triple, total, sums) = refs[:-5], refs[-5:]
    face = third.shape[0] - 8
    value = added(totals)
    if near_one.shape[0] > face:
        value = value + near_one[pl.ds(face, 8)]
    total[...] = value
    sums[...] = jnp.zeros(sums.shape, wide)
    for i, later in enumerate((third[:face] + near_one[:face], fourth[...] + far_one[...])):
        here = pl.ds(i * face, face)
        second, gamma, cross = step_rows(
            value,
            residual,
            search,
            image,
            later,
            pl.ds((2 + i) * face, face),
            residual_next.at[here],
            search_next.at[here],
        )
        put_triple(triple, i * face, second)
        sums[:1] += gamma
        sums[1:2] += cross


def step_kernel(matrix, flat, residual, search, image, total, *refs):
    (grp_residual, grp_search, triple_grp, grp_sums, *parts) = refs[:8]
    residual_next, search_next, back_sub, back_grp, dense, message, triple = refs[8:]
    face = back_sub.shape[0]
    corners = flat.shape[0]
    odd = parities()
    sums = grp_sums[:2]
    for i in range(2):
        here = pl.ds(i * face, face)
        second, gamma, cross = step_rows(
            total[...],
            residual,
            search,
            image,
            parts[i][...] + parts[2 + i][...],
            here,
            residual_next.at[here],
            search_next.at[here],
        )
        put_triple(triple, i * face, second)
        sums = sums + jnp.concatenate([gamma, cross], 0)
    half = pl.ds(2 * face, 2 * face)
    residual_next[half] = grp_residual[...]
    search_next[half] = grp_search[...]
    local = both_dots(matrix, triple, triple_grp)
    dense[...] = local
    for axis, back in enumerate((back_sub, back_grp)):
        here = pl.ds(pl.multiple_of((2 * axis + 1 - odd[axis]) * face, face), face)
        back[...] = dense[here]
    message[:corners] = both_dots(flat, triple, triple_grp)
    message[pl.ds(corners, 8)] = jnp.zeros((8, local.shape[1]), wide)
    message[pl.ds(corners, 2)] = 0.5 * sums
    message[pl.ds(corners + 2, 1)] = column_sum(search_next[...], local)
    message[pl.ds(corners + 3, 1)] = column_sum(search[...], local)


def owned_kernel(*refs):
    half = len(refs) // 2
    odd = parities()
    for whole, own in zip(refs[:half], refs[half:]):
        face = own.shape[0] // 2
        for axis in range(2):
            here = pl.ds(pl.multiple_of((2 * axis + odd[axis]) * face, face), face)
            own[pl.ds(axis * face, face)] = whole[here]


def final_kernel(corners, *refs):
    (residual, search, image, search_next, dense, extra, near_table, far_table, *refs) = refs
    from_right, from_above, old_total, near_passed, far_passed, *refs = refs
    totals, (solution, final, values) = refs[:-3], refs[-3:]
    face = from_right.shape[0]
    odd = parities()
    newer = added(totals)
    if len(totals) > 1:
        newer = newer[-8:] + near_passed[pl.ds(corners, 8)] + far_passed[pl.ds(corners, 8)]
    gamma, slope = old_total[:1], old_total[1:2]
    alpha = gamma / slope
    gamma_next, cross, steep, cross_other = (newer[i : i + 1] for i in range(4))
    beta = gamma_next / gamma
    alpha_next = gamma_next / (steep + beta * (cross + cross_other + beta * slope))
    upper = odd[1] == 1
    table = jnp.where(upper, far_table[...].astype(wide), near_table[...].astype(wide))
    put_values(values, jnp.where(upper, far_passed[...], near_passed[...]))
    last = dot(table.astype(short), values[...])
    for axis, back in enumerate((from_right, from_above)):
        here = pl.ds(pl.multiple_of((2 * axis + odd[axis]) * face, face), face)
        out = pl.ds(axis * face, face)
        first = search[out]
        solution[out] = alpha * first + alpha_next * (search_next[out] + beta * first)
        newest = dense[out] + extra[here] + back[...] + beta * image[out]
        if axis == 1:
            newest = newest + last
        final[out] = residual[out] - alpha_next * newest


def per_device(
    jump_data,
    dual_block,
    dirichlet_block,
    coupling,
    corner_weight,
    corner_rows,
    membership,
    face_pairing,
    block_pattern,
):
    face = face_pairing.shape[-1]
    corners = corner_rows.shape[-1]
    loads = jump_data.shape[-1]
    depth = 4 * face
    rows = corners + 8
    members = lax.axis_size("sub")
    ride = lax.axis_size("grp") == 4
    pattern = block_pattern[0, 0]
    pairing = face_pairing[0, 0]
    part = ((face, loads), wide)
    more = ((face + 8, loads), wide)
    eight = ((8, loads), wide)
    whole = ((depth, loads), wide)
    triple = ((3 * depth, loads), short)
    half = ((2 * face, loads), wide)
    half_triple = ((6 * face, loads), short)
    matrix = ((depth, 3 * depth), short)
    message = ((rows, loads), wide)
    gathered = ((members * rows, loads), wide)
    gathered_triple = ((3 * members * rows, loads), short)
    values = ((128, loads), short)
    table = ((face, 128), short)
    work = 6 * depth * depth * loads
    turn_work = 4 * depth * depth * depth

    jump = jump_data[0, 0]
    right, upper = jump[:face], jump[face:]
    from_below = move(upper, "grp", lambda i: i + 1)
    from_left = move(right, "sub", lambda i: i + 1)
    (label,) = call(
        label_kernel, [membership, corner_weight[0], corner_rows[0]], [((8, 128), wide)]
    )
    dirichlet, coupling_flat, coupling_table, *slips = call(
        dirichlet_kernel,
        [pattern, dirichlet_block[0, 0], pairing, coupling[0, 0].T],
        [matrix, ((corners, 3 * depth), short), ((depth, 128), short)] + [eight] * 4,
        flops=turn_work,
    )
    (dual,) = call(
        dual_kernel,
        [pattern, dual_block[0, 0], pairing],
        [matrix],
        flops=turn_work,
    )
    dirichlet, dual = lax.optimization_barrier((dirichlet, dual))
    residual, field, last = call(
        start_kernel,
        [dirichlet, right, upper, from_left, from_below],
        [whole, triple, part],
        flops=work // 4,
        scalars=0,
    )
    *parts, gamma_part = call(
        start_rest_kernel,
        [dirichlet, field, residual, last, *slips],
        [more] * 4 + [eight],
        flops=work,
        scalars=0,
    )

    others = swap_edges(parts)
    others[0], label_given = lax.optimization_barrier((others[0], label))
    labels = gather_members(label_given)
    (coarse_table,) = call(
        table_kernel,
        [labels],
        [((members * rows, 3 * members * rows), short)],
        [((members * rows, 128), wide)],
        scalars=0,
    )
    gamma_part, coarse_table = lax.optimization_barrier((gamma_part, coarse_table))

    edges = call(
        edges_kernel, [*parts[2:], others[3], others[2]], [half, half_triple], scalars=0
    )
    search, *image_parts, sent = call(
        dual_first_kernel,
        [dual, coupling_flat, gamma_part, *edges, *parts[:2], *others[:2]],
        [whole] + [part] * 4 + [message],
        [half_triple],
        flops=work,
        scalars=0,
    )
    first = move(image_parts[0], "sub", near)
    third, fourth = move(image_parts[2], "grp", near), move(image_parts[3], "grp", far)
    first, sent = lax.optimization_barrier((first, sent))
    every = gather_members(sent)
    image_parts[1], every = lax.optimization_barrier((image_parts[1], every))
    image_others = [first, move(image_parts[1], "sub", far), third, fourth]
    tables = []
    for axis in range(2):
        tables += call(
            functools.partial(neighbour_kernel, corners),
            others[2 * axis : 2 * axis + 2],
            [table] * 2,
            scalars=0,
        )
    passed, extra = call(
        functools.partial(coarse_kernel, corners, False),
        [coarse_table, coupling_table, *tables[:2], every],
        [message, whole],
        [gathered_triple, gathered, values],
        scalars=0,
    )
    near_passed, far_passed = move(passed, "grp", near), move(passed, "grp", far)
    *edges, passing, sums = call(
        functools.partial(second_edges_kernel, corners),
        [
            extra,
            *tables[2:],
            passed,
            near_passed,
            far_passed,
            *image_parts[2:],
            image_others[3],
            image_others[2],
        ],
        [half, half_triple, eight, eight],
        [values],
        scalars=0,
    )
    image, *later_parts = call(
        second_kernel,
        [dirichlet, extra, passing, *edges, *image_parts[:2], *image_others[:2]],
        [whole, part, part, more, part],
        [half_triple],
        flops=work,
        scalars=0,
    )
    later_others = swap_edges(later_parts)
    totals = [sums] if ride else group_terms(passed[corners:])
    if not ride:
        later_others[2] = later_others[2][:face]
    *edges, old_total, grp_sums = call(
        step_edges_kernel,
        [residual, search, image, *later_parts[2:], later_others[3], later_others[2], *totals],
        [half, half, half_triple, eight, eight],
        scalars=0,
    )
    residual_next, search_next, back_sub, back_grp, dense, sent = call(
        step_kernel,
        [
            dual,
            coupling_flat,
            residual,
            search,
            image,
            old_total,
            *edges,
            grp_sums,
            *later_parts[:2],
            *later_others[:2],
        ],
        [whole, whole, part, part, whole, message],
        [half_triple],
        flops=work,
        scalars=0,
    )
    from_above = move(back_grp, "grp", lambda i: i - 1)
    every_next = gather_members(sent)
    back_sub, every_next = lax.optimization_barrier((back_sub, every_next))
    from_right = move(back_sub, "sub", lambda i: i - 1)
    passed, extra = call(
        functools.partial(coarse_kernel, corners, True),
        [coarse_table, coupling_table, *tables[:2], every_next, every],
        [message, whole],
        [gathered_triple, gathered, values],
        scalars=0,
    )
    near_passed, far_passed = move(passed, "grp", near), move(passed, "grp", far)
    if ride:
        totals = [passed[corners:], move(passed[corners:], "grp", lambda i: i ^ 2)]
    else:
        totals = group_terms(passed[corners:])
    owned = []
    for arrays in ((residual_next, search), (image, search_next, dense)):
        owned += call(
            owned_kernel,
            arrays,
            [((2 * face, loads), wide)] * len(arrays),
            flops=0,
            scalars=0,
        )
    solution, final = call(
        functools.partial(final_kernel, corners),
        [
            *owned,
            extra,
            *tables[2:],
            from_right,
            from_above,
            old_total,
            near_passed,
            far_passed,
            *totals,
        ],
        [((2 * face, loads), wide)] * 2,
        [values],
        scalars=0,
    )
    return (solution[None, None], final[None, None])


def solution(mesh):
    placed = (
        P("grp", "sub", None, None),
        P("grp", "sub", None, None),
        P("grp", "sub", None, None),
        P("grp", "sub", None, None),
        P("grp", "sub", None),
        P("grp", "sub", None),
        P("grp", "sub"),
        P("grp", "sub", None, None),
        P("grp", "sub", None, None),
    )
    return jax.shard_map(
        per_device,
        mesh=mesh,
        in_specs=placed,
        out_specs=(P("grp", "sub", None, None), P("grp", "sub", None, None)),
        check_vma=False,
    )
```

time: 261 us -> 93.9 us (0.36)
  blocking collectives: 159 us -> 29 us
  waiting for transfers between devices: 53.6 us -> 22 us
  matrix products: 17.6 us -> 0 us
  Pallas kernels: 0 us -> 12.9 us
  starting transfers between devices: 18.5 us -> 25.7 us
  other arithmetic: 4.21 us -> 0 us
  local copies, waits for them, and re-layouts: 6.6 us -> 2.54 us
    psum x3 -> x0, blocking collectives: 115 us -> none  [the longest x2 76.7 us: residual_product(): return lax.psum(column_sum(residual, search), ('grp', 'sub'))]
    ppermute x16 -> x21, waiting for transfers between devices: 53.6 us -> 22 us  [move(): lax.ppermute(array, axis, [(i, target(i) % peers) for i in range(peers)])]
    dot_general x27 -> x0, matrix products: 17.6 us -> none  [the longest x24 16.5 us: matmul(): jnp.dot(first, second, precision=highest, preferred_element_type=jnp.floa...]
    pallas_call x0 -> x19, Pallas kernels: none -> 12.9 us  [call(): pl.pallas_call(body, out_shape=[jax.ShapeDtypeStruct(shape, kind) for sha...]
    all_gather x4 -> x3, blocking collectives: 37.1 us -> 29 us  [gather_members(): return lax.all_gather(array, 'sub', axis=0, tiled=True)]
    ppermute x16 -> x21, starting transfers between devices: 18.5 us -> 25.7 us  [move(): lax.ppermute(array, axis, [(i, target(i) % peers) for i in range(peers)])]
    unnamed x1 -> x0, blocking collectives: 6.92 us -> none
    unnamed x35 -> x14, local copies, waits for them, and re-layouts: 4.83 us -> 1.38 us
  transfers between devices with their start and end apart: 16 -> 21, of which waited for: 14 -> 7; matrix products, arithmetic and copies ran while one was open for 1% -> 0% of each run, Pallas kernels for 0% -> 7%
where the time goes in v3:
time: 93.9 us; the launch traced here: 93.6 us
  blocking collectives  29 us (31%)
  starting transfers between devices  25.7 us (27%)
  waiting for transfers between devices  22 us (23%)
  Pallas kernels  12.9 us (14%)
  local copies, waits for them, and re-layouts  2.54 us (3%)
  between operations  1.54 us (2%)
    all_gather x3, blocking collectives, gather_members(): return lax.all_gather(array, 'sub', axis=0, tiled=True)  29 us
    ppermute x21, starting transfers between devices, move(): lax.ppermute(array, axis, [(i, target(i) % peers) for i in range(peers)])  25.7 us
    ppermute x21, waiting for transfers between devices, move(): lax.ppermute(array, axis, [(i, target(i) % peers) for i in range(peers)])  22 us
    pallas_call x19, Pallas kernels, call(): pl.pallas_call(body, out_shape=[jax.ShapeDtypeStruct(shape, kind) for sha...  12.9 us
  transfers between devices with their start and end apart: 21, of which 7 were waited for; matrix products, arithmetic and copies ran while one was open for 0% of the time, Pallas kernels for 7%

profile of v3, /device:TPU:0, one launch (start us, length us, event | category | flops | bytes accessed | tf_op | source)
XLA Modules:
  0.0 93.6 jit_solution(12618559723794576200)
XLA Ops:
  0.6 1.2 %slice_bitcast_fusion = (f32[128,512]{1,0:T(8,128)S(1)}, f32[128,512]{1,0:T(8,128)S(1)}) fusion(f32[1,1,256,512]{3,2,1,0:T(8,128)} %param.9), kind=kLoop, calls=%fused_computation | loop fusion | bytes 1048576 | tf_op jit(solution)/shard_map/slice | solution.py:491
  1.8 3.1 %collective-permute-start.1 = (f32[128,512]{1,0:T(8,128)S(1)}, f32[128,512]{1,0:T(8,128)S(1)}, u32[]{:S(2)}, u32[]{:S(2)}) collective-permute-start(f32[128,512]{1,0:T(8,128)S(1)} %get-tuple-element.142.upper), channel_id=1, source_target_pairs={{0,8},{8,16},{16,24},{24,0},{1,9},{9,17},{17,25},{25,1},{2,10},{10... | collective-permute-start | bytes 786440 | tf_op jit(solution)/shard_map/ppermute | solution.py:35
  4.9 0.7 copy-done.1
  5.6 0.7 copy-done.2
  6.2 1.4 %shard_map.105.matrix = bf16[512,1536]{1,0:T(8,128)(2,1)S(1)} custom-call(s32[4,4]{1,0:T(4,128)S(1)} %bitcast.16, f32[512,512]{1,0:T(8,128)S(1)} %bitcast.15, s32[2,128]{1,0:T(2,128)S(1)} %bitcast.18), custom_call_target="tpu_custom_call" | custom-call | flops 536870912 | bytes 1049664 | tf_op jit(solution)/shard_map/pallas_call | solution.py:22
  7.7 1.7 %shard_map.104 = (bf16[512,1536]{1,0:T(8,128)(2,1)S(1)}, bf16[24,1536]{1,0:T(8,128)(2,1)S(1)}, bf16[512,128]{1,0:T(8,128)(2,1)S(1)}, f32[8,512]{1,0:T(8,128)S(1)...) custom-call(s32[4,4]{1,0:T(4,128)S(1)} %bitcast.17, f32[512,512]{1,0:T(8,128)S(1)} %bitcast.22, ...), custom_call_target="tpu_custom_call" | custom-call | flops 536870912 | bytes 1098816 | tf_op jit(solution)/shard_map/pallas_call | solution.py:22
  9.4 3.8 %collective-permute-done.1.from_below = f32[128,512]{1,0:T(8,128)S(1)} collective-permute-done((f32[128,512]{1,0:T(8,128)S(1)}, f32[128,512]{1,0:T(8,128)S(1)}, u32[]{:S(2)}, u32[]{:S(2)}) %collective-permute-start.1) | collective-permute-done | bytes 262176 | tf_op jit(solution)/shard_map/ppermute | solution.py:35
  13.2 0.6 shard_map.106
  13.8 0.8 shard_map.107
  14.6 0.1 collective-permute-start.2
  14.7 0.1 collective-permute-start.4
  14.8 2.4 %collective-permute-start.3 = (f32[136,512]{1,0:T(8,128)S(1)}, f32[136,512]{1,0:T(8,128)S(1)}, u32[]{:S(2)}, u32[]{:S(2)}) collective-permute-start(f32[136,512]{1,0:T(8,128)S(1)} %get-tuple-element.88.fourth), channel_id=1, source_target_pairs={{0,24},{8,16},{16,8},{24,0},{1,25},{9,17},{17,9},{25,1},{2,26},{10... | collective-permute-start | bytes 835592 | tf_op jit(solution)/shard_map/ppermute | solution.py:35
  17.2 1.7 %collective-permute-start.5 = (f32[136,512]{1,0:T(8,128)S(1)}, f32[136,512]{1,0:T(8,128)S(1)}, u32[]{:S(2)}, u32[]{:S(2)}) collective-permute-start(f32[136,512]{1,0:T(8,128)S(1)} %get-tuple-element.91.refs_1_), channel_id=1, source_target_pairs={{0,7},{1,2},{2,1},{3,4},{4,3},{5,6},{6,5},{7,0},{8,15},{9,10},{10,... | collective-permute-start | bytes 835592 | tf_op jit(solution)/shard_map/ppermute | solution.py:35
  19.6 9.2 %all_gather.9.labels = f32[64,128]{1,0:T(8,128)S(1)} all-gather(f32[8,128]{1,0:T(8,128)S(1)} %shard_map.108), channel_id=1, replica_groups=mesh['grp'=4,'sub'=8] {'sub'}, dimensions={0}, use_global_device_ids=true | all-gather | bytes 36864 | tf_op jit(solution)/shard_map/all_gather | solution.py:56
  28.8 0.4 shard_map.109.table
  29.2 1.0 %collective-permute-done.3.far_one.refs_1_ = f32[136,512]{1,0:T(8,128)S(1)} collective-permute-done((f32[136,512]{1,0:T(8,128)S(1)}, f32[136,512]{1,0:T(8,128)S(1)}, u32[]{:S(2)}, u32[]{:S(2)}) %collective-permute-start.3) | collective-permute-done | bytes 278560 | tf_op jit(solution)/shard_map/ppermute | solution.py:35
  30.2 0.1 shard_map.110
  30.4 1.2 %shard_map.111 = (f32[512,512]{1,0:T(8,128)S(1)}, f32[128,512]{1,0:T(8,128)S(1)}, f32[128,512]{1,0:T(8,128)S(1)}, f32[128,512]{1,0:T(8,128)S(1)}, f32[128,512]{1,0:T(8,128)S(1)}, /*index=5*/f32[32,512]{1,0:T(8,128)S(1)}) custom-call(bf16[512,1536]{1,0:T(8,128)(2,1)S(1)} %shard_map.105.matrix, bf16[24,1536]{1,0:T(8,128)(2,1)S(1)} %get-tuple-element.74.flat, ...), custom_call_target="tpu_custom_call" | custom-call | flops 805306368 | bytes 4087808 | tf_op jit(solution)/shard_map/pallas_call | solution.py:22
  31.6 1.3 %collective-permute-start.10 = (f32[128,512]{1,0:T(8,128)S(1)}, f32[128,512]{1,0:T(8,128)S(1)}, u32[]{:S(2)}, u32[]{:S(2)}) collective-permute-start(f32[128,512]{1,0:T(8,128)S(1)} %get-tuple-element.107.refs_6_), channel_id=1, source_target_pairs={{0,8},{8,0},{16,24},{24,16},{1,9},{9,1},{17,25},{25,17},{2,10},{10... | collective-permute-start | bytes 786440 | tf_op jit(solution)/shard_map/ppermute | solution.py:35
  32.9 1.7 %collective-permute-start.9 = (f32[128,512]{1,0:T(8,128)S(1)}, f32[128,512]{1,0:T(8,128)S(1)}, u32[]{:S(2)}, u32[]{:S(2)}) collective-permute-start(f32[128,512]{1,0:T(8,128)S(1)} %get-tuple-element.108.refs_7_), channel_id=1, source_target_pairs={{0,24},{8,16},{16,8},{24,0},{1,25},{9,17},{17,9},{25,1},{2,26},{10... | collective-permute-start | bytes 786440 | tf_op jit(solution)/shard_map/ppermute | solution.py:35
  34.6 9.9 %all_gather.10.refs_0_.refs_1_ = f32[256,512]{1,0:T(8,128)S(1)} all-gather(f32[32,512]{1,0:T(8,128)S(1)} %get-tuple-element.101), channel_id=1, replica_groups=mesh['grp'=4,'sub'=8] {'sub'}, dimensions={0}, use_global_device_ids=true | all-gather | bytes 589824 | tf_op jit(solution)/shard_map/all_gather | solution.py:56
  44.5 1.4 %collective-permute-start.11 = (f32[128,512]{1,0:T(8,128)S(1)}, f32[128,512]{1,0:T(8,128)S(1)}, u32[]{:S(2)}, u32[]{:S(2)}) collective-permute-start(f32[128,512]{1,0:T(8,128)S(1)} %get-tuple-element.112.refs_1_), channel_id=1, source_target_pairs={{0,7},{1,2},{2,1},{3,4},{4,3},{5,6},{6,5},{7,0},{8,15},{9,10},{10,... | collective-permute-start | bytes 786440 | tf_op jit(solution)/shard_map/ppermute | solution.py:35
  45.9 0.2 shard_map.112
  46.1 0.8 shard_map.113
  46.9 2.2 %collective-permute-start.8 = (f32[32,512]{1,0:T(8,128)S(1)}, f32[32,512]{1,0:T(8,128)S(1)}, u32[]{:S(2)}, u32[]{:S(2)}) collective-permute-start(f32[32,512]{1,0:T(8,128)S(1)} %get-tuple-element.106.refs_3_), channel_id=1, source_target_pairs={{0,24},{8,16},{16,8},{24,0},{1,25},{9,17},{17,9},{25,1},{2,26},{10... | collective-permute-start | bytes 196616 | tf_op jit(solution)/shard_map/ppermute | solution.py:35
  49.0 0.2 shard_map.114
  49.3 4.3 %collective-permute-done.8.refs_5_ = f32[32,512]{1,0:T(8,128)S(1)} collective-permute-done((f32[32,512]{1,0:T(8,128)S(1)}, f32[32,512]{1,0:T(8,128)S(1)}, u32[]{:S(2)}, u32[]{:S(2)}) %collective-permute-start.8) | collective-permute-done | bytes 65568 | tf_op jit(solution)/shard_map/ppermute | solution.py:35
  53.6 0.7 collective-permute-done.7.refs_4_
  54.3 0.2 shard_map.115
  54.6 1.0 %shard_map.116 = (f32[512,512]{1,0:T(8,128)S(1)}, f32[128,512]{1,0:T(8,128)S(1)}, f32[128,512]{1,0:T(8,128)S(1)}, f32[136,512]{1,0:T(8,128)S(1)}, f32[128,512]{1,0:T(8,128)S(1)}) custom-call(bf16[512,1536]{1,0:T(8,128)(2,1)S(1)} %get-tuple-element.75.matrix, f32[512,512]{1,0:T(8,128)S(1)} %get-tuple-element.103.refs_0_.extra, ...), custom_call_target="tpu_custom_call" | custom-call | flops 805306368 | bytes 4997120 | tf_op jit(solution)/shard_map/pallas_call | solution.py:22
  55.6 0.4 collective-permute-start.13
  56.0 1.7 %collective-permute-start.12 = (f32[128,512]{1,0:T(8,128)S(1)}, f32[128,512]{1,0:T(8,128)S(1)}, u32[]{:S(2)}, u32[]{:S(2)}) collective-permute-start(f32[128,512]{1,0:T(8,128)S(1)} %get-tuple-element.116.fourth), channel_id=1, source_target_pairs={{0,24},{8,16},{16,8},{24,0},{1,25},{9,17},{17,9},{25,1},{2,26},{10... | collective-permute-start | bytes 786440 | tf_op jit(solution)/shard_map/ppermute | solution.py:35
  57.7 1.6 %collective-permute-start.15 = (f32[128,512]{1,0:T(8,128)S(1)}, f32[128,512]{1,0:T(8,128)S(1)}, u32[]{:S(2)}, u32[]{:S(2)}) collective-permute-start(f32[128,512]{1,0:T(8,128)S(1)} %get-tuple-element.124.refs_5_), channel_id=1, source_target_pairs={{0,7},{1,2},{2,1},{3,4},{4,3},{5,6},{6,5},{7,0},{8,15},{9,10},{10,... | collective-permute-start | bytes 786440 | tf_op jit(solution)/shard_map/ppermute | solution.py:35
  59.2 10.3 %collective-permute-done.12.far_one = f32[128,512]{1,0:T(8,128)S(1)} collective-permute-done((f32[128,512]{1,0:T(8,128)S(1)}, f32[128,512]{1,0:T(8,128)S(1)}, u32[]{:S(2)}, u32[]{:S(2)}) %collective-permute-start.12) | collective-permute-done | bytes 262176 | tf_op jit(solution)/shard_map/ppermute | solution.py:35
  69.5 0.2 collective-permute-done.13.near_one
  69.7 0.5 shard_map.117
  70.2 1.4 %shard_map.118 = (f32[512,512]{1,0:T(8,128)S(1)}, f32[512,512]{1,0:T(8,128)S(1)}, f32[128,512]{1,0:T(8,128)S(1)}, f32[128,512]{1,0:T(8,128)S(1)}, f32[512,512]{1,0:T(8,128)S(1)}, /*index=5*/f32[32,512]{1,0:T(8,128)S(1)}) custom-call(bf16[512,1536]{1,0:T(8,128)(2,1)S(1)} %shard_map.105.matrix, bf16[24,1536]{1,0:T(8,128)(2,1)S(1)} %get-tuple-element.74.flat, ...), custom_call_target="tpu_custom_call" | custom-call | flops 805306368 | bytes 7708672 | tf_op jit(solution)/shard_map/pallas_call | solution.py:22
  71.7 2.2 %collective-permute-start.17 = (f32[128,512]{1,0:T(8,128)S(1)}, f32[128,512]{1,0:T(8,128)S(1)}, u32[]{:S(2)}, u32[]{:S(2)}) collective-permute-start(f32[128,512]{1,0:T(8,128)S(1)} %get-tuple-element.138), channel_id=1, source_target_pairs={{0,24},{8,0},{16,8},{24,16},{1,25},{9,1},{17,9},{25,17},{2,26},{10... | collective-permute-start | bytes 786440 | tf_op jit(solution)/shard_map/ppermute | solution.py:35
  73.9 9.9 %all_gather.11.refs_0_ = f32[256,512]{1,0:T(8,128)S(1)} all-gather(f32[32,512]{1,0:T(8,128)S(1)} %get-tuple-element.134), channel_id=1, replica_groups=mesh['grp'=4,'sub'=8] {'sub'}, dimensions={0}, use_global_device_ids=true | all-gather | bytes 589824 | tf_op jit(solution)/shard_map/all_gather | solution.py:56
  83.8 1.4 %collective-permute-start.16 = (f32[128,512]{1,0:T(8,128)S(1)}, f32[128,512]{1,0:T(8,128)S(1)}, u32[]{:S(2)}, u32[]{:S(2)}) collective-permute-start(f32[128,512]{1,0:T(8,128)S(1)} %get-tuple-element.137), channel_id=1, source_target_pairs={{0,7},{1,0},{2,1},{3,2},{4,3},{5,4},{6,5},{7,6},{8,15},{9,8},{10,9... | collective-permute-start | bytes 786440 | tf_op jit(solution)/shard_map/ppermute | solution.py:35
  85.2 0.8 shard_map.121
  86.0 1.0 %collective-permute-start.19 = (f32[32,512]{1,0:T(8,128)S(1)}, f32[32,512]{1,0:T(8,128)S(1)}, u32[]{:S(2)}, u32[]{:S(2)}) collective-permute-start(f32[32,512]{1,0:T(8,128)S(1)} %get-tuple-element.139), channel_id=1, source_target_pairs={{0,24},{8,16},{16,8},{24,0},{1,25},{9,17},{17,9},{25,1},{2,26},{10... | collective-permute-start | bytes 196616 | tf_op jit(solution)/shard_map/ppermute | solution.py:35
  87.0 0.5 collective-permute-start.18
  87.5 3.0 %collective-permute-start.20 = (f32[8,512]{1,0:T(8,128)S(1)}, f32[8,512]{1,0:T(8,128)S(1)}, u32[]{:S(2)}, u32[]{:S(2)}) collective-permute-start(f32[8,512]{1,0:T(8,128)S(1)} %slice.20.refs_13_), channel_id=1, source_target_pairs={{0,16},{8,24},{16,0},{24,8},{1,17},{9,25},{17,1},{25,9},{2,18},{10... | collective-permute-start | bytes 49160 | tf_op jit(solution)/shard_map/ppermute | solution.py:35
  90.4 0.1 shard_map.119
  90.5 0.1 shard_map.120
  90.6 1.7 %collective-permute-done.20.refs_14_ = f32[8,512]{1,0:T(8,128)S(1)} collective-permute-done((f32[8,512]{1,0:T(8,128)S(1)}, f32[8,512]{1,0:T(8,128)S(1)}, u32[]{:S(2)}, u32[]{:S(2)}) %collective-permute-start.20) | collective-permute-done | bytes 16416 | tf_op jit(solution)/shard_map/ppermute | solution.py:35
  92.3 1.3 %shard_map.122 = (f32[256,512]{1,0:T(8,128)}, f32[256,512]{1,0:T(8,128)}) custom-call(f32[256,512]{1,0:T(8,128)S(1)} %get-tuple-element.126.refs_0_, f32[256,512]{1,0:T(8,128)S(1)} %get-tuple-element.127.refs_1_, f32[256,512]{1,0:T(8,128)S(1)} %get-tuple-element.130.refs_2_, f32[256,512]{1,0:T(8,128)S(1)} %get-tuple-element.131.refs_3_, ...), custom_call_target="tpu_custom_call" | custom-call | bytes 4440064 | tf_op jit(solution)/shard_map/pallas_call | solution.py:22
  (32 shorter events, 0.1 us)
Async XLA Ops:
  0.6 4.2 %copy-start = (f32[1,1,512,512]{3,2,1,0:T(8,128)S(1)}, f32[1,1,512,512]{3,2,1,0:T(8,128)}, u32[]{:S(2)}) copy-start(f32[1,1,512,512]{3,2,1,0:T(8,128)} %param.10) | copy-start | bytes 3145732
  1.8 11.4 %collective-permute-start.1 = (f32[128,512]{1,0:T(8,128)S(1)}, f32[128,512]{1,0:T(8,128)S(1)}, u32[]{:S(2)}, u32[]{:S(2)}) collective-permute-start(f32[128,512]{1,0:T(8,128)S(1)} %get-tuple-element.142.upper), channel_id=1, source_target_pairs={{0,8},{8,16},{16,24},{24,0},{1,9},{9,17},{17,25},{25,1},{2,10},{10... | collective-permute-start | bytes 786440 | tf_op jit(solution)/shard_map/ppermute | solution.py:35
  4.9 8.3 %collective-permute-start = (f32[128,512]{1,0:T(8,128)S(1)}, f32[128,512]{1,0:T(8,128)S(1)}, u32[]{:S(2)}, u32[]{:S(2)}) collective-permute-start(f32[128,512]{1,0:T(8,128)S(1)} %get-tuple-element.143.right), channel_id=1, source_target_pairs={{0,1},{1,2},{2,3},{3,4},{4,5},{5,6},{6,7},{7,0},{8,9},{9,10},{10,1... | collective-permute-start | bytes 786440 | tf_op jit(solution)/shard_map/ppermute | solution.py:35
  4.9 0.7 copy-start.1
  5.6 0.7 copy-start.2
  6.2 1.4 %copy-start.5 = (f32[1,1,512,512]{3,2,1,0:T(8,128)S(1)}, f32[1,1,512,512]{3,2,1,0:T(8,128)}, u32[]{:S(2)}) copy-start(f32[1,1,512,512]{3,2,1,0:T(8,128)} %param.11) | copy-start | bytes 3145732
  6.2 1.4 %copy-start.6 = (f32[1,1,512,24]{2,3,1,0:T(8,128)S(1)}, f32[1,1,512,24]{2,3,1,0:T(8,128)}, u32[]{:S(2)}) copy-start(f32[1,1,512,24]{2,3,1,0:T(8,128)} %param.12) | copy-start | bytes 147460
  13.8 5.8 %copy-start.3 = (f32[1,1,24]{2,1,0:T(1,128)S(1)}, f32[1,1,24]{2,1,0:T(1,128)}, u32[]{:S(2)}) copy-start(f32[1,1,24]{2,1,0:T(1,128)} %param.13) | copy-start | bytes 292
  13.8 5.8 %copy-start.4 = (s32[1,1,24]{2,1,0:T(1,128)S(1)}, s32[1,1,24]{2,1,0:T(1,128)}, u32[]{:S(2)}) copy-start(s32[1,1,24]{2,1,0:T(1,128)} %param.14) | copy-start | bytes 292
  14.6 5.0 %collective-permute-start.2 = (f32[136,512]{1,0:T(8,128)S(1)}, f32[136,512]{1,0:T(8,128)S(1)}, u32[]{:S(2)}, u32[]{:S(2)}) collective-permute-start(f32[136,512]{1,0:T(8,128)S(1)} %get-tuple-element.84.refs_0_), channel_id=1, source_target_pairs={{0,1},{1,0},{2,3},{3,2},{4,5},{5,4},{6,7},{7,6},{8,9},{9,8},{10,11... | collective-permute-start | bytes 835592 | tf_op jit(solution)/shard_map/ppermute | solution.py:35
  14.7 14.5 %collective-permute-start.4 = (f32[136,512]{1,0:T(8,128)S(1)}, f32[136,512]{1,0:T(8,128)S(1)}, u32[]{:S(2)}, u32[]{:S(2)}) collective-permute-start(f32[136,512]{1,0:T(8,128)S(1)} %get-tuple-element.87.third), channel_id=1, source_target_pairs={{0,8},{8,0},{16,24},{24,16},{1,9},{9,1},{17,25},{25,17},{2,10},{10... | collective-permute-start | bytes 835592 | tf_op jit(solution)/shard_map/ppermute | solution.py:35
  14.8 15.5 %collective-permute-start.3 = (f32[136,512]{1,0:T(8,128)S(1)}, f32[136,512]{1,0:T(8,128)S(1)}, u32[]{:S(2)}, u32[]{:S(2)}) collective-permute-start(f32[136,512]{1,0:T(8,128)S(1)} %get-tuple-element.88.fourth), channel_id=1, source_target_pairs={{0,24},{8,16},{16,8},{24,0},{1,25},{9,17},{17,9},{25,1},{2,26},{10... | collective-permute-start | bytes 835592 | tf_op jit(solution)/shard_map/ppermute | solution.py:35
  17.2 13.2 %collective-permute-start.5 = (f32[136,512]{1,0:T(8,128)S(1)}, f32[136,512]{1,0:T(8,128)S(1)}, u32[]{:S(2)}, u32[]{:S(2)}) collective-permute-start(f32[136,512]{1,0:T(8,128)S(1)} %get-tuple-element.91.refs_1_), channel_id=1, source_target_pairs={{0,7},{1,2},{2,1},{3,4},{4,3},{5,6},{6,5},{7,0},{8,15},{9,10},{10,... | collective-permute-start | bytes 835592 | tf_op jit(solution)/shard_map/ppermute | solution.py:35
  31.6 3.0 %collective-permute-start.6 = (f32[128,512]{1,0:T(8,128)S(1)}, f32[128,512]{1,0:T(8,128)S(1)}, u32[]{:S(2)}, u32[]{:S(2)}) collective-permute-start(f32[128,512]{1,0:T(8,128)S(1)} %get-tuple-element.99.refs_0_), channel_id=1, source_target_pairs={{0,1},{1,0},{2,3},{3,2},{4,5},{5,4},{6,7},{7,6},{8,9},{9,8},{10,11... | collective-permute-start | bytes 786440 | tf_op jit(solution)/shard_map/ppermute | solution.py:35
  31.6 17.7 %collective-permute-start.10 = (f32[128,512]{1,0:T(8,128)S(1)}, f32[128,512]{1,0:T(8,128)S(1)}, u32[]{:S(2)}, u32[]{:S(2)}) collective-permute-start(f32[128,512]{1,0:T(8,128)S(1)} %get-tuple-element.107.refs_6_), channel_id=1, source_target_pairs={{0,8},{8,0},{16,24},{24,16},{1,9},{9,1},{17,25},{25,17},{2,10},{10... | collective-permute-start | bytes 786440 | tf_op jit(solution)/shard_map/ppermute | solution.py:35
  32.9 16.4 %collective-permute-start.9 = (f32[128,512]{1,0:T(8,128)S(1)}, f32[128,512]{1,0:T(8,128)S(1)}, u32[]{:S(2)}, u32[]{:S(2)}) collective-permute-start(f32[128,512]{1,0:T(8,128)S(1)} %get-tuple-element.108.refs_7_), channel_id=1, source_target_pairs={{0,24},{8,16},{16,8},{24,0},{1,25},{9,17},{17,9},{25,1},{2,26},{10... | collective-permute-start | bytes 786440 | tf_op jit(solution)/shard_map/ppermute | solution.py:35
  44.5 10.1 %collective-permute-start.11 = (f32[128,512]{1,0:T(8,128)S(1)}, f32[128,512]{1,0:T(8,128)S(1)}, u32[]{:S(2)}, u32[]{:S(2)}) collective-permute-start(f32[128,512]{1,0:T(8,128)S(1)} %get-tuple-element.112.refs_1_), channel_id=1, source_target_pairs={{0,7},{1,2},{2,1},{3,4},{4,3},{5,6},{6,5},{7,0},{8,15},{9,10},{10,... | collective-permute-start | bytes 786440 | tf_op jit(solution)/shard_map/ppermute | solution.py:35
  46.9 6.8 %collective-permute-start.8 = (f32[32,512]{1,0:T(8,128)S(1)}, f32[32,512]{1,0:T(8,128)S(1)}, u32[]{:S(2)}, u32[]{:S(2)}) collective-permute-start(f32[32,512]{1,0:T(8,128)S(1)} %get-tuple-element.106.refs_3_), channel_id=1, source_target_pairs={{0,24},{8,16},{16,8},{24,0},{1,25},{9,17},{17,9},{25,1},{2,26},{10... | collective-permute-start | bytes 196616 | tf_op jit(solution)/shard_map/ppermute | solution.py:35
  49.0 5.3 %collective-permute-start.7 = (f32[32,512]{1,0:T(8,128)S(1)}, f32[32,512]{1,0:T(8,128)S(1)}, u32[]{:S(2)}, u32[]{:S(2)}) collective-permute-start(f32[32,512]{1,0:T(8,128)S(1)} %get-tuple-element.106.refs_3_), channel_id=1, source_target_pairs={{0,8},{8,0},{16,24},{24,16},{1,9},{9,1},{17,25},{25,17},{2,10},{10... | collective-permute-start | bytes 196616 | tf_op jit(solution)/shard_map/ppermute | solution.py:35
  55.6 14.2 %collective-permute-start.13 = (f32[136,512]{1,0:T(8,128)S(1)}, f32[136,512]{1,0:T(8,128)S(1)}, u32[]{:S(2)}, u32[]{:S(2)}) collective-permute-start(f32[136,512]{1,0:T(8,128)S(1)} %get-tuple-element.115.third), channel_id=1, source_target_pairs={{0,8},{8,0},{16,24},{24,16},{1,9},{9,1},{17,25},{25,17},{2,10},{10... | collective-permute-start | bytes 835592 | tf_op jit(solution)/shard_map/ppermute | solution.py:35
  56.0 13.6 %collective-permute-start.12 = (f32[128,512]{1,0:T(8,128)S(1)}, f32[128,512]{1,0:T(8,128)S(1)}, u32[]{:S(2)}, u32[]{:S(2)}) collective-permute-start(f32[128,512]{1,0:T(8,128)S(1)} %get-tuple-element.116.fourth), channel_id=1, source_target_pairs={{0,24},{8,16},{16,8},{24,0},{1,25},{9,17},{17,9},{25,1},{2,26},{10... | collective-permute-start | bytes 786440 | tf_op jit(solution)/shard_map/ppermute | solution.py:35
  57.7 12.5 %collective-permute-start.14 = (f32[128,512]{1,0:T(8,128)S(1)}, f32[128,512]{1,0:T(8,128)S(1)}, u32[]{:S(2)}, u32[]{:S(2)}) collective-permute-start(f32[128,512]{1,0:T(8,128)S(1)} %get-tuple-element.123.refs_4_), channel_id=1, source_target_pairs={{0,1},{1,0},{2,3},{3,2},{4,5},{5,4},{6,7},{7,6},{8,9},{9,8},{10,11... | collective-permute-start | bytes 786440 | tf_op jit(solution)/shard_map/ppermute | solution.py:35
  57.7 12.5 %collective-permute-start.15 = (f32[128,512]{1,0:T(8,128)S(1)}, f32[128,512]{1,0:T(8,128)S(1)}, u32[]{:S(2)}, u32[]{:S(2)}) collective-permute-start(f32[128,512]{1,0:T(8,128)S(1)} %get-tuple-element.124.refs_5_), channel_id=1, source_target_pairs={{0,7},{1,2},{2,1},{3,4},{4,3},{5,6},{6,5},{7,0},{8,15},{9,10},{10,... | collective-permute-start | bytes 786440 | tf_op jit(solution)/shard_map/ppermute | solution.py:35
  71.7 20.6 %collective-permute-start.17 = (f32[128,512]{1,0:T(8,128)S(1)}, f32[128,512]{1,0:T(8,128)S(1)}, u32[]{:S(2)}, u32[]{:S(2)}) collective-permute-start(f32[128,512]{1,0:T(8,128)S(1)} %get-tuple-element.138), channel_id=1, source_target_pairs={{0,24},{8,0},{16,8},{24,16},{1,25},{9,1},{17,9},{25,17},{2,26},{10... | collective-permute-start | bytes 786440 | tf_op jit(solution)/shard_map/ppermute | solution.py:35
  83.8 8.5 %collective-permute-start.16 = (f32[128,512]{1,0:T(8,128)S(1)}, f32[128,512]{1,0:T(8,128)S(1)}, u32[]{:S(2)}, u32[]{:S(2)}) collective-permute-start(f32[128,512]{1,0:T(8,128)S(1)} %get-tuple-element.137), channel_id=1, source_target_pairs={{0,7},{1,0},{2,1},{3,2},{4,3},{5,4},{6,5},{7,6},{8,15},{9,8},{10,9... | collective-permute-start | bytes 786440 | tf_op jit(solution)/shard_map/ppermute | solution.py:35
  86.0 6.3 %collective-permute-start.19 = (f32[32,512]{1,0:T(8,128)S(1)}, f32[32,512]{1,0:T(8,128)S(1)}, u32[]{:S(2)}, u32[]{:S(2)}) collective-permute-start(f32[32,512]{1,0:T(8,128)S(1)} %get-tuple-element.139), channel_id=1, source_target_pairs={{0,24},{8,16},{16,8},{24,0},{1,25},{9,17},{17,9},{25,1},{2,26},{10... | collective-permute-start | bytes 196616 | tf_op jit(solution)/shard_map/ppermute | solution.py:35
  87.0 5.3 %collective-permute-start.18 = (f32[32,512]{1,0:T(8,128)S(1)}, f32[32,512]{1,0:T(8,128)S(1)}, u32[]{:S(2)}, u32[]{:S(2)}) collective-permute-start(f32[32,512]{1,0:T(8,128)S(1)} %get-tuple-element.139), channel_id=1, source_target_pairs={{0,8},{8,0},{16,24},{24,16},{1,9},{9,1},{17,25},{25,17},{2,10},{10... | collective-permute-start | bytes 196616 | tf_op jit(solution)/shard_map/ppermute | solution.py:35
  87.5 4.8 %collective-permute-start.20 = (f32[8,512]{1,0:T(8,128)S(1)}, f32[8,512]{1,0:T(8,128)S(1)}, u32[]{:S(2)}, u32[]{:S(2)}) collective-permute-start(f32[8,512]{1,0:T(8,128)S(1)} %slice.20.refs_13_), channel_id=1, source_target_pairs={{0,16},{8,24},{16,0},{24,8},{1,17},{9,25},{17,1},{25,9},{2,18},{10... | collective-permute-start | bytes 49160 | tf_op jit(solution)/shard_map/ppermute | solution.py:35

commit v4 on v3

--- a/solution.py
+++ b/solution.py
@@ -53,7 +53,17 @@
 
 
 def gather_members(array):
-    return lax.all_gather(array, "sub", axis=0, tiled=True)
+    peers = lax.axis_size("sub")
+    same = [array] + [move(array, "sub", lambda i, k=k: i ^ k) for k in range(2, peers, 2)]
+    return same + [move(one, "sub", near) for one in same]
+
+
+def order_of_members(peers):
+    return [*range(0, peers, 2), *range(1, peers, 2)]
+
+
+def member_rows(distance, rows):
+    return pl.ds(pl.multiple_of((lax.axis_index("sub") ^ distance) * rows, rows), rows)
 
 
 def group_terms(array):
@@ -199,8 +209,8 @@
 def table_kernel(labels, table, columns):
     rows = 32
     columns[...] = jnp.zeros(columns.shape, wide)
-    for i in range(labels.shape[0] // 8):
-        columns[pl.ds(i * rows, rows), :8] = labels[pl.ds(8 * i, 8)].T[:rows]
+    for i, distance in enumerate(order_of_members(labels.shape[0] // 8)):
+        columns[pl.ds(i * rows, rows), :8] = labels[member_rows(distance, 8)].T[:rows]
     across = columns[...].T
     weight, row, member = (across[i : i + 1] for i in range(3))
     same = (columns[:, 1:2] == row) & (columns[:, 2:3] == member) & (columns[:, 1:2] >= 0)
@@ -213,32 +223,24 @@
     table[:, 2 * width :] = low
 
 
-def start_kernel(matrix, right, upper, from_left, from_below, field, triple, last):
+def start_kernel(matrix, right, upper, from_left, from_below, *refs):
+    slips, (field, first, second, third, fourth, sums, triple) = refs[:4], refs[4:]
     face = from_left.shape[0]
     odd = parities()
     for axis, (own, other) in enumerate(((right, from_left), (upper, from_below))):
         here = pl.ds(2 * axis * face, face)
         there = pl.ds((2 * axis + 1) * face, face)
-        first = jnp.where(odd[axis] == 1, other[...], own[...])
-        second = jnp.where(odd[axis] == 1, own[...], other[...])
-        field[here] = first
-        field[there] = second
-        put_triple(triple, 0, first, 6 * axis * face, 2 * face)
-        put_triple(triple, face, second, 6 * axis * face, 2 * face)
-    last[...] = dot(matrix[pl.ds(3 * face, face)], triple[...])
-
-
-def start_rest_kernel(matrix, triple, field, last, *refs):
-    slips, (first, second, third, fourth, sums) = refs[:4], refs[4:]
-    face = last.shape[0]
-    total = column_sum(field[pl.ds(3 * face, face)], last[...])
-    local = dot(matrix[: 3 * face], triple[...])
-    for i, out in enumerate((first, second, third)):
+        one = jnp.where(odd[axis] == 1, other[...], own[...])
+        two = jnp.where(odd[axis] == 1, own[...], other[...])
+        field[here] = one
+        field[there] = two
+        put_triple(triple, 0, one, 6 * axis * face, 2 * face)
+        put_triple(triple, face, two, 6 * axis * face, 2 * face)
+    local = dot(matrix[...], triple[...])
+    for i, (out, slip) in enumerate(zip((first, second, third, fourth), slips)):
         out[:face] = local[i * face : (i + 1) * face]
-    fourth[:face] = last[...]
-    for out, slip in zip((first, second, third, fourth), slips):
         out[pl.ds(face, 8)] = slip[...]
-    sums[...] = jnp.broadcast_to(total + column_sum(field[: 3 * face], local), sums.shape)
+    sums[...] = jnp.broadcast_to(column_sum(field[...], local), sums.shape)
 
 
 def both_dots(matrix, *triples):
@@ -272,34 +274,41 @@
     message[pl.ds(corners + 1, 1)] = column_sum(field[...], local)
 
 
-def coarse_kernel(corners, second, table, coupling, near_table, far_table, *refs):
-    count = 2 if second else 1
-    every, (passed, extra, triple, coarse, values) = refs[:count], refs[count:]
+def coarse_kernel(corners, table, *refs):
+    *every, first_every, passed, coarse, triple = refs
     rows = passed.shape[0]
-    face = near_table.shape[0]
-    put_triple(triple, 0, every[0][...])
+    members = first_every.shape[0] // rows
+    older = [first_every.at[member_rows(d, rows)] for d in order_of_members(members)]
+    groups = [every, older] if every else [older]
+    count = len(groups)
+    for i in range(members):
+        put_triple(triple, i * rows, groups[0][i][...])
     coarse[...] = dot(table[...], triple[...])
     sums = jnp.zeros((8, passed.shape[1]), wide)
     extras = [jnp.zeros((1, passed.shape[1]), wide) for _ in range(count)]
-    for i in range(every[0].shape[0] // rows):
+    for i in range(members):
         here = pl.ds(i * rows, corners)
-        sums = sums + every[0][pl.ds(i * rows + corners, 8)]
+        sums = sums + groups[0][i][pl.ds(corners, 8)]
         for j in range(count):
-            extras[j] = extras[j] + column_sum(coarse[here], every[j][here])
-    sub = lax.axis_index("sub")
-    own, partner, other = (
-        pl.ds(pl.multiple_of(place * rows, rows), rows) for place in (sub, sub ^ 1, far_sub())
-    )
-    passed[...] = coarse[own]
+            extras[j] = extras[j] + column_sum(coarse[here], groups[j][i][pl.ds(0, corners)])
+    passed[...] = coarse[:rows]
     passed[pl.ds(corners, 8)] = sums
     for j, one in enumerate(extras):
         place = count + j
         passed[pl.ds(corners + place, 1)] = sums[place : place + 1] + one
-    put_values(values, coarse[own])
+
+
+def extra_kernel(coarse, coupling, near_table, far_table, extra, values):
+    rows = 32
+    face = near_table.shape[0]
+    members = coarse.shape[0] // rows
+    put_values(values, coarse[:rows])
     extra[...] = dot(coupling[...], values[...])
-    put_values(values, coarse[partner])
+    put_values(values, coarse[pl.ds(members // 2 * rows, rows)])
     extra[:face] += dot(near_table[...], values[...])
-    put_values(values, coarse[other])
+    distance = lax.shift_right_logical(far_sub() ^ lax.axis_index("sub") ^ 1, 1)
+    place = pl.multiple_of((members // 2 + distance) * rows, rows)
+    put_values(values, coarse[pl.ds(place, rows)])
     extra[pl.ds(face, face)] += dot(far_table[...], values[...])
 
 
@@ -507,24 +516,17 @@
         flops=turn_work,
     )
     dirichlet, dual = lax.optimization_barrier((dirichlet, dual))
-    residual, field, last = call(
+    residual, *parts, gamma_part = call(
         start_kernel,
-        [dirichlet, right, upper, from_left, from_below],
-        [whole, triple, part],
-        flops=work // 4,
-        scalars=0,
-    )
-    *parts, gamma_part = call(
-        start_rest_kernel,
-        [dirichlet, field, residual, last, *slips],
-        [more] * 4 + [eight],
+        [dirichlet, right, upper, from_left, from_below, *slips],
+        [whole] + [more] * 4 + [eight],
+        [triple],
         flops=work,
         scalars=0,
     )
-
     others = swap_edges(parts)
     others[0], label_given = lax.optimization_barrier((others[0], label))
-    labels = gather_members(label_given)
+    labels = lax.all_gather(label_given, "sub", axis=0, tiled=True)
     (coarse_table,) = call(
         table_kernel,
         [labels],
@@ -548,7 +550,7 @@
     first = move(image_parts[0], "sub", near)
     third, fourth = move(image_parts[2], "grp", near), move(image_parts[3], "grp", far)
     first, sent = lax.optimization_barrier((first, sent))
-    every = gather_members(sent)
+    every = lax.all_gather(sent, "sub", axis=0, tiled=True)
     image_parts[1], every = lax.optimization_barrier((image_parts[1], every))
     image_others = [first, move(image_parts[1], "sub", far), third, fourth]
     tables = []
@@ -559,12 +561,12 @@
             [table] * 2,
             scalars=0,
         )
-    passed, extra = call(
-        functools.partial(coarse_kernel, corners, False),
-        [coarse_table, coupling_table, *tables[:2], every],
-        [message, whole],
-        [gathered_triple, gathered, values],
-        scalars=0,
+    coarse_shapes = [message, gathered], [gathered_triple]
+    passed, coarse = call(
+        functools.partial(coarse_kernel, corners), [coarse_table, every], *coarse_shapes, scalars=0
+    )
+    (extra,) = call(
+        extra_kernel, [coarse, coupling_table, *tables[:2]], [whole], [values], scalars=0
     )
     near_passed, far_passed = move(passed, "grp", near), move(passed, "grp", far)
     *edges, passing, sums = call(
@@ -621,15 +623,16 @@
         scalars=0,
     )
     from_above = move(back_grp, "grp", lambda i: i - 1)
+    from_right = move(back_sub, "sub", lambda i: i - 1)
     every_next = gather_members(sent)
-    back_sub, every_next = lax.optimization_barrier((back_sub, every_next))
-    from_right = move(back_sub, "sub", lambda i: i - 1)
-    passed, extra = call(
-        functools.partial(coarse_kernel, corners, True),
-        [coarse_table, coupling_table, *tables[:2], every_next, every],
-        [message, whole],
-        [gathered_triple, gathered, values],
-        scalars=0,
+    passed, coarse = call(
+        functools.partial(coarse_kernel, corners),
+        [coarse_table, *every_next, every],
+        *coarse_shapes,
+        scalars=0,
+    )
+    (extra,) = call(
+        extra_kernel, [coarse, coupling_table, *tables[:2]], [whole], [values], scalars=0
     )
     near_passed, far_passed = move(passed, "grp", near), move(passed, "grp", far)
     if ride:

time: 93.9 us -> 91.3 us (0.972)
  blocking collectives: 29 us -> 19.1 us
  starting transfers between devices: 25.7 us -> 29.6 us
  waiting for transfers between devices: 22 us -> 25.6 us
    all_gather x3 -> x2, blocking collectives: 29 us -> 19.1 us  [the longest x1 9.85 us: per_device(): every = lax.all_gather(sent, 'sub', axis=0, tiled=True)]
    ppermute x21 -> x28, starting transfers between devices: 25.7 us -> 29.6 us  [move(): lax.ppermute(array, axis, [(i, target(i) % peers) for i in range(peers)])]
    ppermute x21 -> x28, waiting for transfers between devices: 22 us -> 25.6 us  [move(): lax.ppermute(array, axis, [(i, target(i) % peers) for i in range(peers)])]
    pallas_call x19 -> x20, Pallas kernels: 12.9 us -> 12.6 us  [call(): pl.pallas_call(body, out_shape=[jax.ShapeDtypeStruct(shape, kind) for sha...]
  transfers between devices with their start and end apart: 21 -> 28, of which waited for: 7 -> 13; matrix products, arithmetic and copies ran while one was open for 0% -> 0% of each run, Pallas kernels for 7% -> 7%
where the time goes in v4:
time: 91.3 us; the launch traced here: 91 us
  starting transfers between devices  29.6 us (32%)
  waiting for transfers between devices  25.6 us (28%)
  blocking collectives  19.1 us (21%)
  Pallas kernels  12.6 us (14%)
  local copies, waits for them, and re-layouts  2.54 us (3%)
  between operations  1.54 us (2%)
    ppermute x28, starting transfers between devices, move(): lax.ppermute(array, axis, [(i, target(i) % peers) for i in range(peers)])  29.6 us
    ppermute x28, waiting for transfers between devices, move(): lax.ppermute(array, axis, [(i, target(i) % peers) for i in range(peers)])  25.6 us
    pallas_call x20, Pallas kernels, call(): pl.pallas_call(body, out_shape=[jax.ShapeDtypeStruct(shape, kind) for sha...  12.6 us
    all_gather x1, blocking collectives, per_device(): every = lax.all_gather(sent, 'sub', axis=0, tiled=True)  9.85 us
    all_gather x1, blocking collectives, per_device(): labels = lax.all_gather(label_given, 'sub', axis=0, tiled=True)  9.23 us
  transfers between devices with their start and end apart: 28, of which 13 were waited for; matrix products, arithmetic and copies ran while one was open for 0% of the time, Pallas kernels for 7%

profile of v4, /device:TPU:0, one launch (start us, length us, event | category | flops | bytes accessed | tf_op | source)
XLA Modules:
  0.0 91.0 jit_solution(9226090359496467920)
XLA Ops:
  0.6 1.2 %slice_bitcast_fusion = (f32[128,512]{1,0:T(8,128)S(1)}, f32[128,512]{1,0:T(8,128)S(1)}) fusion(f32[1,1,256,512]{3,2,1,0:T(8,128)} %param.9), kind=kLoop, calls=%fused_computation | loop fusion | bytes 1048576 | tf_op jit(solution)/shard_map/slice | solution.py:500
  1.8 3.1 %collective-permute-start.1 = (f32[128,512]{1,0:T(8,128)S(1)}, f32[128,512]{1,0:T(8,128)S(1)}, u32[]{:S(2)}, u32[]{:S(2)}) collective-permute-start(f32[128,512]{1,0:T(8,128)S(1)} %get-tuple-element.134.upper), channel_id=1, source_target_pairs={{0,8},{8,16},{16,24},{24,0},{1,9},{9,17},{17,25},{25,1},{2,10},{10... | collective-permute-start | bytes 786440 | tf_op jit(solution)/shard_map/ppermute | solution.py:35
  4.9 0.7 copy-done.1
  5.6 0.7 copy-done.2
  6.2 1.4 %shard_map.105.matrix = bf16[512,1536]{1,0:T(8,128)(2,1)S(1)} custom-call(s32[4,4]{1,0:T(4,128)S(1)} %bitcast.16, f32[512,512]{1,0:T(8,128)S(1)} %bitcast.15, s32[2,128]{1,0:T(2,128)S(1)} %bitcast.18), custom_call_target="tpu_custom_call" | custom-call | flops 536870912 | bytes 1049664 | tf_op jit(solution)/shard_map/pallas_call | solution.py:22
  7.7 1.7 %shard_map.104 = (bf16[512,1536]{1,0:T(8,128)(2,1)S(1)}, bf16[24,1536]{1,0:T(8,128)(2,1)S(1)}, bf16[512,128]{1,0:T(8,128)(2,1)S(1)}, f32[8,512]{1,0:T(8,128)S(1)...) custom-call(s32[4,4]{1,0:T(4,128)S(1)} %bitcast.17, f32[512,512]{1,0:T(8,128)S(1)} %bitcast.22, ...), custom_call_target="tpu_custom_call" | custom-call | flops 536870912 | bytes 1098816 | tf_op jit(solution)/shard_map/pallas_call | solution.py:22
  9.4 3.8 %collective-permute-done.1.from_below = f32[128,512]{1,0:T(8,128)S(1)} collective-permute-done((f32[128,512]{1,0:T(8,128)S(1)}, f32[128,512]{1,0:T(8,128)S(1)}, u32[]{:S(2)}, u32[]{:S(2)}) %collective-permute-start.1) | collective-permute-done | bytes 262176 | tf_op jit(solution)/shard_map/ppermute | solution.py:35
  13.2 1.0 %shard_map.106 = (f32[512,512]{1,0:T(8,128)S(1)}, f32[136,512]{1,0:T(8,128)S(1)}, f32[136,512]{1,0:T(8,128)S(1)}, f32[136,512]{1,0:T(8,128)S(1)}, f32[136,512]{1,0:T(8,128)S(1)}, /*index=5*/f32[8,512]{1,0:T(8,128)S(1)}) custom-call(bf16[512,1536]{1,0:T(8,128)(2,1)S(1)} %get-tuple-element.71.matrix, f32[128,512]{1,0:T(8,128)S(1)} %get-tuple-element.135.right, ...), custom_call_target="tpu_custom_call" | custom-call | flops 805306368 | bytes 2686976 | tf_op jit(solution)/shard_map/pallas_call | solution.py:22
  14.4 2.4 %collective-permute-start.3 = (f32[136,512]{1,0:T(8,128)S(1)}, f32[136,512]{1,0:T(8,128)S(1)}, u32[]{:S(2)}, u32[]{:S(2)}) collective-permute-start(f32[136,512]{1,0:T(8,128)S(1)} %get-tuple-element.82.fourth), channel_id=1, source_target_pairs={{0,24},{8,16},{16,8},{24,0},{1,25},{9,17},{17,9},{25,1},{2,26},{10... | collective-permute-start | bytes 835592 | tf_op jit(solution)/shard_map/ppermute | solution.py:35
  16.8 1.7 %collective-permute-start.5 = (f32[136,512]{1,0:T(8,128)S(1)}, f32[136,512]{1,0:T(8,128)S(1)}, u32[]{:S(2)}, u32[]{:S(2)}) collective-permute-start(f32[136,512]{1,0:T(8,128)S(1)} %get-tuple-element.85.refs_1_), channel_id=1, source_target_pairs={{0,7},{1,2},{2,1},{3,4},{4,3},{5,6},{6,5},{7,0},{8,15},{9,10},{10,... | collective-permute-start | bytes 835592 | tf_op jit(solution)/shard_map/ppermute | solution.py:35
  19.2 9.2 %all_gather.6.labels = f32[64,128]{1,0:T(8,128)S(1)} all-gather(f32[8,128]{1,0:T(8,128)S(1)} %shard_map.107), channel_id=1, replica_groups=mesh['grp'=4,'sub'=8] {'sub'}, dimensions={0}, use_global_device_ids=true | all-gather | bytes 36864 | tf_op jit(solution)/shard_map/all_gather | solution.py:529
  28.5 0.4 shard_map.108.table
  28.9 1.0 %collective-permute-done.3.far_one.refs_1_ = f32[136,512]{1,0:T(8,128)S(1)} collective-permute-done((f32[136,512]{1,0:T(8,128)S(1)}, f32[136,512]{1,0:T(8,128)S(1)}, u32[]{:S(2)}, u32[]{:S(2)}) %collective-permute-start.3) | collective-permute-done | bytes 278560 | tf_op jit(solution)/shard_map/ppermute | solution.py:35
  30.0 1.2 %shard_map.110 = (f32[512,512]{1,0:T(8,128)S(1)}, f32[128,512]{1,0:T(8,128)S(1)}, f32[128,512]{1,0:T(8,128)S(1)}, f32[128,512]{1,0:T(8,128)S(1)}, f32[128,512]{1,0:T(8,128)S(1)}, /*index=5*/f32[32,512]{1,0:T(8,128)S(1)}) custom-call(bf16[512,1536]{1,0:T(8,128)(2,1)S(1)} %shard_map.105.matrix, bf16[24,1536]{1,0:T(8,128)(2,1)S(1)} %get-tuple-element.70.flat, ...), custom_call_target="tpu_custom_call" | custom-call | flops 805306368 | bytes 4087808 | tf_op jit(solution)/shard_map/pallas_call | solution.py:22
  31.2 1.3 %collective-permute-start.10 = (f32[128,512]{1,0:T(8,128)S(1)}, f32[128,512]{1,0:T(8,128)S(1)}, u32[]{:S(2)}, u32[]{:S(2)}) collective-permute-start(f32[128,512]{1,0:T(8,128)S(1)} %get-tuple-element.101.refs_6_), channel_id=1, source_target_pairs={{0,8},{8,0},{16,24},{24,16},{1,9},{9,1},{17,25},{25,17},{2,10},{10... | collective-permute-start | bytes 786440 | tf_op jit(solution)/shard_map/ppermute | solution.py:35
  32.5 1.8 %collective-permute-start.9 = (f32[128,512]{1,0:T(8,128)S(1)}, f32[128,512]{1,0:T(8,128)S(1)}, u32[]{:S(2)}, u32[]{:S(2)}) collective-permute-start(f32[128,512]{1,0:T(8,128)S(1)} %get-tuple-element.102.refs_7_), channel_id=1, source_target_pairs={{0,24},{8,16},{16,8},{24,0},{1,25},{9,17},{17,9},{25,1},{2,26},{10... | collective-permute-start | bytes 786440 | tf_op jit(solution)/shard_map/ppermute | solution.py:35
  34.3 9.8 %all_gather.7.refs_0_.refs_8_ = f32[256,512]{1,0:T(8,128)S(1)} all-gather(f32[32,512]{1,0:T(8,128)S(1)} %get-tuple-element.92), channel_id=1, replica_groups=mesh['grp'=4,'sub'=8] {'sub'}, dimensions={0}, use_global_device_ids=true | all-gather | bytes 589824 | tf_op jit(solution)/shard_map/all_gather | solution.py:553
  44.1 1.4 %collective-permute-start.11 = (f32[128,512]{1,0:T(8,128)S(1)}, f32[128,512]{1,0:T(8,128)S(1)}, u32[]{:S(2)}, u32[]{:S(2)}) collective-permute-start(f32[128,512]{1,0:T(8,128)S(1)} %get-tuple-element.106.refs_1_), channel_id=1, source_target_pairs={{0,7},{1,2},{2,1},{3,4},{4,3},{5,6},{6,5},{7,0},{8,15},{9,10},{10,... | collective-permute-start | bytes 786440 | tf_op jit(solution)/shard_map/ppermute | solution.py:35
  45.6 0.4 shard_map.111
  46.0 2.1 %collective-permute-start.8 = (f32[32,512]{1,0:T(8,128)S(1)}, f32[32,512]{1,0:T(8,128)S(1)}, u32[]{:S(2)}, u32[]{:S(2)}) collective-permute-start(f32[32,512]{1,0:T(8,128)S(1)} %get-tuple-element.100.refs_3_), channel_id=1, source_target_pairs={{0,24},{8,16},{16,8},{24,0},{1,25},{9,17},{17,9},{25,1},{2,26},{10... | collective-permute-start | bytes 196616 | tf_op jit(solution)/shard_map/ppermute | solution.py:35
  48.6 0.4 shard_map.113.refs_0_.extra
  49.0 3.7 %collective-permute-done.8.refs_5_ = f32[32,512]{1,0:T(8,128)S(1)} collective-permute-done((f32[32,512]{1,0:T(8,128)S(1)}, f32[32,512]{1,0:T(8,128)S(1)}, u32[]{:S(2)}, u32[]{:S(2)}) %collective-permute-start.8) | collective-permute-done | bytes 65568 | tf_op jit(solution)/shard_map/ppermute | solution.py:35
  52.7 0.7 collective-permute-done.7.refs_4_
  53.4 0.3 shard_map.115
  53.7 1.0 %shard_map.116 = (f32[512,512]{1,0:T(8,128)S(1)}, f32[128,512]{1,0:T(8,128)S(1)}, f32[128,512]{1,0:T(8,128)S(1)}, f32[136,512]{1,0:T(8,128)S(1)}, f32[128,512]{1,0:T(8,128)S(1)}) custom-call(bf16[512,1536]{1,0:T(8,128)(2,1)S(1)} %get-tuple-element.71.matrix, f32[512,512]{1,0:T(8,128)S(1)} %shard_map.113.refs_0_.extra, ...), custom_call_target="tpu_custom_call" | custom-call | flops 805306368 | bytes 4997120 | tf_op jit(solution)/shard_map/pallas_call | solution.py:22
  54.7 0.4 collective-permute-start.13
  55.0 1.7 %collective-permute-start.12 = (f32[128,512]{1,0:T(8,128)S(1)}, f32[128,512]{1,0:T(8,128)S(1)}, u32[]{:S(2)}, u32[]{:S(2)}) collective-permute-start(f32[128,512]{1,0:T(8,128)S(1)} %get-tuple-element.110.fourth), channel_id=1, source_target_pairs={{0,24},{8,16},{16,8},{24,0},{1,25},{9,17},{17,9},{25,1},{2,26},{10... | collective-permute-start | bytes 786440 | tf_op jit(solution)/shard_map/ppermute | solution.py:35
  56.8 1.6 %collective-permute-start.15 = (f32[128,512]{1,0:T(8,128)S(1)}, f32[128,512]{1,0:T(8,128)S(1)}, u32[]{:S(2)}, u32[]{:S(2)}) collective-permute-start(f32[128,512]{1,0:T(8,128)S(1)} %get-tuple-element.118.refs_5_), channel_id=1, source_target_pairs={{0,7},{1,2},{2,1},{3,4},{4,3},{5,6},{6,5},{7,0},{8,15},{9,10},{10,... | collective-permute-start | bytes 786440 | tf_op jit(solution)/shard_map/ppermute | solution.py:35
  58.3 10.5 %collective-permute-done.12.far_one = f32[128,512]{1,0:T(8,128)S(1)} collective-permute-done((f32[128,512]{1,0:T(8,128)S(1)}, f32[128,512]{1,0:T(8,128)S(1)}, u32[]{:S(2)}, u32[]{:S(2)}) %collective-permute-start.12) | collective-permute-done | bytes 262176 | tf_op jit(solution)/shard_map/ppermute | solution.py:35
  68.8 0.5 shard_map.117
  69.3 1.4 %shard_map.118 = (f32[512,512]{1,0:T(8,128)S(1)}, f32[512,512]{1,0:T(8,128)S(1)}, f32[128,512]{1,0:T(8,128)S(1)}, f32[128,512]{1,0:T(8,128)S(1)}, f32[512,512]{1,0:T(8,128)S(1)}, /*index=5*/f32[32,512]{1,0:T(8,128)S(1)}) custom-call(bf16[512,1536]{1,0:T(8,128)(2,1)S(1)} %shard_map.105.matrix, bf16[24,1536]{1,0:T(8,128)(2,1)S(1)} %get-tuple-element.70.flat, ...), custom_call_target="tpu_custom_call" | custom-call | flops 805306368 | bytes 7708672 | tf_op jit(solution)/shard_map/pallas_call | solution.py:22
  70.7 1.9 %collective-permute-start.23 = (f32[128,512]{1,0:T(8,128)S(1)}, f32[128,512]{1,0:T(8,128)S(1)}, u32[]{:S(2)}, u32[]{:S(2)}) collective-permute-start(f32[128,512]{1,0:T(8,128)S(1)} %get-tuple-element.129), channel_id=1, source_target_pairs={{0,7},{1,0},{2,1},{3,2},{4,3},{5,4},{6,5},{7,6},{8,15},{9,8},{10,9... | collective-permute-start | bytes 786440 | tf_op jit(solution)/shard_map/ppermute | solution.py:35
  72.7 1.8 %collective-permute-start.24 = (f32[128,512]{1,0:T(8,128)S(1)}, f32[128,512]{1,0:T(8,128)S(1)}, u32[]{:S(2)}, u32[]{:S(2)}) collective-permute-start(f32[128,512]{1,0:T(8,128)S(1)} %get-tuple-element.130), channel_id=1, source_target_pairs={{0,24},{8,0},{16,8},{24,16},{1,25},{9,1},{17,9},{25,17},{2,26},{10... | collective-permute-start | bytes 786440 | tf_op jit(solution)/shard_map/ppermute | solution.py:35
  74.5 0.8 collective-permute-start.18
  75.2 1.3 %collective-permute-start.17 = (f32[32,512]{1,0:T(8,128)S(1)}, f32[32,512]{1,0:T(8,128)S(1)}, u32[]{:S(2)}, u32[]{:S(2)}) collective-permute-start(f32[32,512]{1,0:T(8,128)S(1)} %get-tuple-element.127.refs_0_), channel_id=1, source_target_pairs={{0,4},{1,5},{2,6},{3,7},{4,0},{5,1},{6,2},{7,3},{8,12},{9,13},{10,... | collective-permute-start | bytes 196616 | tf_op jit(solution)/shard_map/ppermute | solution.py:35
  76.6 1.4 %collective-permute-start.16 = (f32[32,512]{1,0:T(8,128)S(1)}, f32[32,512]{1,0:T(8,128)S(1)}, u32[]{:S(2)}, u32[]{:S(2)}) collective-permute-start(f32[32,512]{1,0:T(8,128)S(1)} %get-tuple-element.127.refs_0_), channel_id=1, source_target_pairs={{0,2},{1,3},{2,0},{3,1},{4,6},{5,7},{6,4},{7,5},{8,10},{9,11},{10,... | collective-permute-start | bytes 196616 | tf_op jit(solution)/shard_map/ppermute | solution.py:35
  77.9 2.1 %collective-permute-done.18.refs_3_ = f32[32,512]{1,0:T(8,128)S(1)} collective-permute-done((f32[32,512]{1,0:T(8,128)S(1)}, f32[32,512]{1,0:T(8,128)S(1)}, u32[]{:S(2)}, u32[]{:S(2)}) %collective-permute-start.18) | collective-permute-done | bytes 65568 | tf_op jit(solution)/shard_map/ppermute | solution.py:35
  80.2 0.4 collective-permute-start.21
  80.8 0.5 collective-permute-done.22.refs_7_
  81.5 0.6 collective-permute-done.20.refs_5_
  82.1 0.5 shard_map.121
  82.5 1.5 %collective-permute-start.26 = (f32[32,512]{1,0:T(8,128)S(1)}, f32[32,512]{1,0:T(8,128)S(1)}, u32[]{:S(2)}, u32[]{:S(2)}) collective-permute-start(f32[32,512]{1,0:T(8,128)S(1)} %get-tuple-element.131), channel_id=1, source_target_pairs={{0,24},{8,16},{16,8},{24,0},{1,25},{9,17},{17,9},{25,1},{2,26},{10... | collective-permute-start | bytes 196616 | tf_op jit(solution)/shard_map/ppermute | solution.py:35
  84.0 0.4 collective-permute-start.25
  84.4 2.6 %collective-permute-start.27 = (f32[8,512]{1,0:T(8,128)S(1)}, f32[8,512]{1,0:T(8,128)S(1)}, u32[]{:S(2)}, u32[]{:S(2)}) collective-permute-start(f32[8,512]{1,0:T(8,128)S(1)} %slice.20.refs_13_), channel_id=1, source_target_pairs={{0,16},{8,24},{16,0},{24,8},{1,17},{9,25},{17,1},{25,9},{2,18},{10... | collective-permute-start | bytes 49160 | tf_op jit(solution)/shard_map/ppermute | solution.py:35
  87.2 0.4 shard_map.122.refs_5_
  87.5 1.8 %collective-permute-done.27.refs_14_ = f32[8,512]{1,0:T(8,128)S(1)} collective-permute-done((f32[8,512]{1,0:T(8,128)S(1)}, f32[8,512]{1,0:T(8,128)S(1)}, u32[]{:S(2)}, u32[]{:S(2)}) %collective-permute-start.27) | collective-permute-done | bytes 16416 | tf_op jit(solution)/shard_map/ppermute | solution.py:35
  89.4 0.3 collective-permute-done.25.refs_11_
  89.7 1.3 %shard_map.123 = (f32[256,512]{1,0:T(8,128)}, f32[256,512]{1,0:T(8,128)}) custom-call(f32[256,512]{1,0:T(8,128)S(1)} %get-tuple-element.120.refs_0_, f32[256,512]{1,0:T(8,128)S(1)} %get-tuple-element.121.refs_1_, f32[256,512]{1,0:T(8,128)S(1)} %get-tuple-element.124.refs_2_, f32[256,512]{1,0:T(8,128)S(1)} %get-tuple-element.125.refs_3_, ...), custom_call_target="tpu_custom_call" | custom-call | bytes 4440064 | tf_op jit(solution)/shard_map/pallas_call | solution.py:22
  (46 shorter events, 1.6 us)
Async XLA Ops:
  0.6 4.2 %copy-start = (f32[1,1,512,512]{3,2,1,0:T(8,128)S(1)}, f32[1,1,512,512]{3,2,1,0:T(8,128)}, u32[]{:S(2)}) copy-start(f32[1,1,512,512]{3,2,1,0:T(8,128)} %param.10) | copy-start | bytes 3145732
  1.8 11.4 %collective-permute-start.1 = (f32[128,512]{1,0:T(8,128)S(1)}, f32[128,512]{1,0:T(8,128)S(1)}, u32[]{:S(2)}, u32[]{:S(2)}) collective-permute-start(f32[128,512]{1,0:T(8,128)S(1)} %get-tuple-element.134.upper), channel_id=1, source_target_pairs={{0,8},{8,16},{16,24},{24,0},{1,9},{9,17},{17,25},{25,1},{2,10},{10... | collective-permute-start | bytes 786440 | tf_op jit(solution)/shard_map/ppermute | solution.py:35
  4.9 8.3 %collective-permute-start = (f32[128,512]{1,0:T(8,128)S(1)}, f32[128,512]{1,0:T(8,128)S(1)}, u32[]{:S(2)}, u32[]{:S(2)}) collective-permute-start(f32[128,512]{1,0:T(8,128)S(1)} %get-tuple-element.135.right), channel_id=1, source_target_pairs={{0,1},{1,2},{2,3},{3,4},{4,5},{5,6},{6,7},{7,0},{8,9},{9,10},{10,1... | collective-permute-start | bytes 786440 | tf_op jit(solution)/shard_map/ppermute | solution.py:35
  4.9 0.7 copy-start.1
  5.6 0.7 copy-start.2
  6.2 1.4 %copy-start.5 = (f32[1,1,512,512]{3,2,1,0:T(8,128)S(1)}, f32[1,1,512,512]{3,2,1,0:T(8,128)}, u32[]{:S(2)}) copy-start(f32[1,1,512,512]{3,2,1,0:T(8,128)} %param.11) | copy-start | bytes 3145732
  6.2 1.4 %copy-start.6 = (f32[1,1,512,24]{2,3,1,0:T(8,128)S(1)}, f32[1,1,512,24]{2,3,1,0:T(8,128)}, u32[]{:S(2)}) copy-start(f32[1,1,512,24]{2,3,1,0:T(8,128)} %param.12) | copy-start | bytes 147460
  9.4 9.8 %copy-start.3 = (f32[1,1,24]{2,1,0:T(1,128)S(1)}, f32[1,1,24]{2,1,0:T(1,128)}, u32[]{:S(2)}) copy-start(f32[1,1,24]{2,1,0:T(1,128)} %param.13) | copy-start | bytes 292
  9.4 9.8 %copy-start.4 = (s32[1,1,24]{2,1,0:T(1,128)S(1)}, s32[1,1,24]{2,1,0:T(1,128)}, u32[]{:S(2)}) copy-start(s32[1,1,24]{2,1,0:T(1,128)} %param.14) | copy-start | bytes 292
  14.3 5.0 %collective-permute-start.2 = (f32[136,512]{1,0:T(8,128)S(1)}, f32[136,512]{1,0:T(8,128)S(1)}, u32[]{:S(2)}, u32[]{:S(2)}) collective-permute-start(f32[136,512]{1,0:T(8,128)S(1)} %get-tuple-element.78.refs_0_), channel_id=1, source_target_pairs={{0,1},{1,0},{2,3},{3,2},{4,5},{5,4},{6,7},{7,6},{8,9},{9,8},{10,11... | collective-permute-start | bytes 835592 | tf_op jit(solution)/shard_map/ppermute | solution.py:35
  14.3 14.6 %collective-permute-start.4 = (f32[136,512]{1,0:T(8,128)S(1)}, f32[136,512]{1,0:T(8,128)S(1)}, u32[]{:S(2)}, u32[]{:S(2)}) collective-permute-start(f32[136,512]{1,0:T(8,128)S(1)} %get-tuple-element.81.third), channel_id=1, source_target_pairs={{0,8},{8,0},{16,24},{24,16},{1,9},{9,1},{17,25},{25,17},{2,10},{10... | collective-permute-start | bytes 835592 | tf_op jit(solution)/shard_map/ppermute | solution.py:35
  14.4 15.5 %collective-permute-start.3 = (f32[136,512]{1,0:T(8,128)S(1)}, f32[136,512]{1,0:T(8,128)S(1)}, u32[]{:S(2)}, u32[]{:S(2)}) collective-permute-start(f32[136,512]{1,0:T(8,128)S(1)} %get-tuple-element.82.fourth), channel_id=1, source_target_pairs={{0,24},{8,16},{16,8},{24,0},{1,25},{9,17},{17,9},{25,1},{2,26},{10... | collective-permute-start | bytes 835592 | tf_op jit(solution)/shard_map/ppermute | solution.py:35
  16.8 13.2 %collective-permute-start.5 = (f32[136,512]{1,0:T(8,128)S(1)}, f32[136,512]{1,0:T(8,128)S(1)}, u32[]{:S(2)}, u32[]{:S(2)}) collective-permute-start(f32[136,512]{1,0:T(8,128)S(1)} %get-tuple-element.85.refs_1_), channel_id=1, source_target_pairs={{0,7},{1,2},{2,1},{3,4},{4,3},{5,6},{6,5},{7,0},{8,15},{9,10},{10,... | collective-permute-start | bytes 835592 | tf_op jit(solution)/shard_map/ppermute | solution.py:35
  31.2 3.1 %collective-permute-start.6 = (f32[128,512]{1,0:T(8,128)S(1)}, f32[128,512]{1,0:T(8,128)S(1)}, u32[]{:S(2)}, u32[]{:S(2)}) collective-permute-start(f32[128,512]{1,0:T(8,128)S(1)} %get-tuple-element.90.refs_0_), channel_id=1, source_target_pairs={{0,1},{1,0},{2,3},{3,2},{4,5},{5,4},{6,7},{7,6},{8,9},{9,8},{10,11... | collective-permute-start | bytes 786440 | tf_op jit(solution)/shard_map/ppermute | solution.py:35
  31.2 17.7 %collective-permute-start.10 = (f32[128,512]{1,0:T(8,128)S(1)}, f32[128,512]{1,0:T(8,128)S(1)}, u32[]{:S(2)}, u32[]{:S(2)}) collective-permute-start(f32[128,512]{1,0:T(8,128)S(1)} %get-tuple-element.101.refs_6_), channel_id=1, source_target_pairs={{0,8},{8,0},{16,24},{24,16},{1,9},{9,1},{17,25},{25,17},{2,10},{10... | collective-permute-start | bytes 786440 | tf_op jit(solution)/shard_map/ppermute | solution.py:35
  32.5 16.4 %collective-permute-start.9 = (f32[128,512]{1,0:T(8,128)S(1)}, f32[128,512]{1,0:T(8,128)S(1)}, u32[]{:S(2)}, u32[]{:S(2)}) collective-permute-start(f32[128,512]{1,0:T(8,128)S(1)} %get-tuple-element.102.refs_7_), channel_id=1, source_target_pairs={{0,24},{8,16},{16,8},{24,0},{1,25},{9,17},{17,9},{25,1},{2,26},{10... | collective-permute-start | bytes 786440 | tf_op jit(solution)/shard_map/ppermute | solution.py:35
  44.1 9.6 %collective-permute-start.11 = (f32[128,512]{1,0:T(8,128)S(1)}, f32[128,512]{1,0:T(8,128)S(1)}, u32[]{:S(2)}, u32[]{:S(2)}) collective-permute-start(f32[128,512]{1,0:T(8,128)S(1)} %get-tuple-element.106.refs_1_), channel_id=1, source_target_pairs={{0,7},{1,2},{2,1},{3,4},{4,3},{5,6},{6,5},{7,0},{8,15},{9,10},{10,... | collective-permute-start | bytes 786440 | tf_op jit(solution)/shard_map/ppermute | solution.py:35
  46.0 6.7 %collective-permute-start.8 = (f32[32,512]{1,0:T(8,128)S(1)}, f32[32,512]{1,0:T(8,128)S(1)}, u32[]{:S(2)}, u32[]{:S(2)}) collective-permute-start(f32[32,512]{1,0:T(8,128)S(1)} %get-tuple-element.100.refs_3_), channel_id=1, source_target_pairs={{0,24},{8,16},{16,8},{24,0},{1,25},{9,17},{17,9},{25,1},{2,26},{10... | collective-permute-start | bytes 196616 | tf_op jit(solution)/shard_map/ppermute | solution.py:35
  48.1 5.3 %collective-permute-start.7 = (f32[32,512]{1,0:T(8,128)S(1)}, f32[32,512]{1,0:T(8,128)S(1)}, u32[]{:S(2)}, u32[]{:S(2)}) collective-permute-start(f32[32,512]{1,0:T(8,128)S(1)} %get-tuple-element.100.refs_3_), channel_id=1, source_target_pairs={{0,8},{8,0},{16,24},{24,16},{1,9},{9,1},{17,25},{25,17},{2,10},{10... | collective-permute-start | bytes 196616 | tf_op jit(solution)/shard_map/ppermute | solution.py:35
  54.7 14.1 %collective-permute-start.13 = (f32[136,512]{1,0:T(8,128)S(1)}, f32[136,512]{1,0:T(8,128)S(1)}, u32[]{:S(2)}, u32[]{:S(2)}) collective-permute-start(f32[136,512]{1,0:T(8,128)S(1)} %get-tuple-element.109.third), channel_id=1, source_target_pairs={{0,8},{8,0},{16,24},{24,16},{1,9},{9,1},{17,25},{25,17},{2,10},{10... | collective-permute-start | bytes 835592 | tf_op jit(solution)/shard_map/ppermute | solution.py:35
  55.0 13.8 %collective-permute-start.12 = (f32[128,512]{1,0:T(8,128)S(1)}, f32[128,512]{1,0:T(8,128)S(1)}, u32[]{:S(2)}, u32[]{:S(2)}) collective-permute-start(f32[128,512]{1,0:T(8,128)S(1)} %get-tuple-element.110.fourth), channel_id=1, source_target_pairs={{0,24},{8,16},{16,8},{24,0},{1,25},{9,17},{17,9},{25,1},{2,26},{10... | collective-permute-start | bytes 786440 | tf_op jit(solution)/shard_map/ppermute | solution.py:35
  56.8 12.5 %collective-permute-start.14 = (f32[128,512]{1,0:T(8,128)S(1)}, f32[128,512]{1,0:T(8,128)S(1)}, u32[]{:S(2)}, u32[]{:S(2)}) collective-permute-start(f32[128,512]{1,0:T(8,128)S(1)} %get-tuple-element.117.refs_4_), channel_id=1, source_target_pairs={{0,1},{1,0},{2,3},{3,2},{4,5},{5,4},{6,7},{7,6},{8,9},{9,8},{10,11... | collective-permute-start | bytes 786440 | tf_op jit(solution)/shard_map/ppermute | solution.py:35
  56.8 12.5 %collective-permute-start.15 = (f32[128,512]{1,0:T(8,128)S(1)}, f32[128,512]{1,0:T(8,128)S(1)}, u32[]{:S(2)}, u32[]{:S(2)}) collective-permute-start(f32[128,512]{1,0:T(8,128)S(1)} %get-tuple-element.118.refs_5_), channel_id=1, source_target_pairs={{0,7},{1,2},{2,1},{3,4},{4,3},{5,6},{6,5},{7,0},{8,15},{9,10},{10,... | collective-permute-start | bytes 786440 | tf_op jit(solution)/shard_map/ppermute | solution.py:35
  70.7 5.8 %collective-permute-start.19 = (f32[32,512]{1,0:T(8,128)S(1)}, f32[32,512]{1,0:T(8,128)S(1)}, u32[]{:S(2)}, u32[]{:S(2)}) collective-permute-start(f32[32,512]{1,0:T(8,128)S(1)} %get-tuple-element.127.refs_0_), channel_id=1, source_target_pairs={{0,1},{1,0},{2,3},{3,2},{4,5},{5,4},{6,7},{7,6},{8,9},{9,8},{10,11... | collective-permute-start | bytes 196616 | tf_op jit(solution)/shard_map/ppermute | solution.py:35
  70.7 18.9 %collective-permute-start.23 = (f32[128,512]{1,0:T(8,128)S(1)}, f32[128,512]{1,0:T(8,128)S(1)}, u32[]{:S(2)}, u32[]{:S(2)}) collective-permute-start(f32[128,512]{1,0:T(8,128)S(1)} %get-tuple-element.129), channel_id=1, source_target_pairs={{0,7},{1,0},{2,1},{3,2},{4,3},{5,4},{6,5},{7,6},{8,15},{9,8},{10,9... | collective-permute-start | bytes 786440 | tf_op jit(solution)/shard_map/ppermute | solution.py:35
  72.7 17.0 %collective-permute-start.24 = (f32[128,512]{1,0:T(8,128)S(1)}, f32[128,512]{1,0:T(8,128)S(1)}, u32[]{:S(2)}, u32[]{:S(2)}) collective-permute-start(f32[128,512]{1,0:T(8,128)S(1)} %get-tuple-element.130), channel_id=1, source_target_pairs={{0,24},{8,0},{16,8},{24,16},{1,25},{9,1},{17,9},{25,17},{2,26},{10... | collective-permute-start | bytes 786440 | tf_op jit(solution)/shard_map/ppermute | solution.py:35
  74.5 5.6 %collective-permute-start.18 = (f32[32,512]{1,0:T(8,128)S(1)}, f32[32,512]{1,0:T(8,128)S(1)}, u32[]{:S(2)}, u32[]{:S(2)}) collective-permute-start(f32[32,512]{1,0:T(8,128)S(1)} %get-tuple-element.127.refs_0_), channel_id=1, source_target_pairs={{0,6},{1,7},{2,4},{3,5},{4,2},{5,3},{6,0},{7,1},{8,14},{9,15},{10,... | collective-permute-start | bytes 196616 | tf_op jit(solution)/shard_map/ppermute | solution.py:35
  75.2 5.0 %collective-permute-start.17 = (f32[32,512]{1,0:T(8,128)S(1)}, f32[32,512]{1,0:T(8,128)S(1)}, u32[]{:S(2)}, u32[]{:S(2)}) collective-permute-start(f32[32,512]{1,0:T(8,128)S(1)} %get-tuple-element.127.refs_0_), channel_id=1, source_target_pairs={{0,4},{1,5},{2,6},{3,7},{4,0},{5,1},{6,2},{7,3},{8,12},{9,13},{10,... | collective-permute-start | bytes 196616 | tf_op jit(solution)/shard_map/ppermute | solution.py:35
  76.6 4.3 %collective-permute-start.16 = (f32[32,512]{1,0:T(8,128)S(1)}, f32[32,512]{1,0:T(8,128)S(1)}, u32[]{:S(2)}, u32[]{:S(2)}) collective-permute-start(f32[32,512]{1,0:T(8,128)S(1)} %get-tuple-element.127.refs_0_), channel_id=1, source_target_pairs={{0,2},{1,3},{2,0},{3,1},{4,6},{5,7},{6,4},{7,5},{8,10},{9,11},{10,... | collective-permute-start | bytes 196616 | tf_op jit(solution)/shard_map/ppermute | solution.py:35
  80.1 1.3 %collective-permute-start.22 = (f32[32,512]{1,0:T(8,128)S(1)}, f32[32,512]{1,0:T(8,128)S(1)}, u32[]{:S(2)}, u32[]{:S(2)}) collective-permute-start(f32[32,512]{1,0:T(8,128)S(1)} %collective-permute-done.18.refs_3_), channel_id=1, source_target_pairs={{0,1},{1,0},{2,3},{3,2},{4,5},{5,4},{6,7},{7,6},{8,9},{9,8},{10,11... | collective-permute-start | bytes 196616 | tf_op jit(solution)/shard_map/ppermute | solution.py:35
  80.2 1.3 %collective-permute-start.21 = (f32[32,512]{1,0:T(8,128)S(1)}, f32[32,512]{1,0:T(8,128)S(1)}, u32[]{:S(2)}, u32[]{:S(2)}) collective-permute-start(f32[32,512]{1,0:T(8,128)S(1)} %collective-permute-done.17.refs_2_), channel_id=1, source_target_pairs={{0,1},{1,0},{2,3},{3,2},{4,5},{5,4},{6,7},{7,6},{8,9},{9,8},{10,11... | collective-permute-start | bytes 196616 | tf_op jit(solution)/shard_map/ppermute | solution.py:35
  80.8 1.3 %collective-permute-start.20 = (f32[32,512]{1,0:T(8,128)S(1)}, f32[32,512]{1,0:T(8,128)S(1)}, u32[]{:S(2)}, u32[]{:S(2)}) collective-permute-start(f32[32,512]{1,0:T(8,128)S(1)} %collective-permute-done.16.refs_1_), channel_id=1, source_target_pairs={{0,1},{1,0},{2,3},{3,2},{4,5},{5,4},{6,7},{7,6},{8,9},{9,8},{10,11... | collective-permute-start | bytes 196616 | tf_op jit(solution)/shard_map/ppermute | solution.py:35
  82.5 6.8 %collective-permute-start.26 = (f32[32,512]{1,0:T(8,128)S(1)}, f32[32,512]{1,0:T(8,128)S(1)}, u32[]{:S(2)}, u32[]{:S(2)}) collective-permute-start(f32[32,512]{1,0:T(8,128)S(1)} %get-tuple-element.131), channel_id=1, source_target_pairs={{0,24},{8,16},{16,8},{24,0},{1,25},{9,17},{17,9},{25,1},{2,26},{10... | collective-permute-start | bytes 196616 | tf_op jit(solution)/shard_map/ppermute | solution.py:35
  84.0 5.6 %collective-permute-start.25 = (f32[32,512]{1,0:T(8,128)S(1)}, f32[32,512]{1,0:T(8,128)S(1)}, u32[]{:S(2)}, u32[]{:S(2)}) collective-permute-start(f32[32,512]{1,0:T(8,128)S(1)} %get-tuple-element.131), channel_id=1, source_target_pairs={{0,8},{8,0},{16,24},{24,16},{1,9},{9,1},{17,25},{25,17},{2,10},{10... | collective-permute-start | bytes 196616 | tf_op jit(solution)/shard_map/ppermute | solution.py:35
  84.4 5.0 %collective-permute-start.27 = (f32[8,512]{1,0:T(8,128)S(1)}, f32[8,512]{1,0:T(8,128)S(1)}, u32[]{:S(2)}, u32[]{:S(2)}) collective-permute-start(f32[8,512]{1,0:T(8,128)S(1)} %slice.20.refs_13_), channel_id=1, source_target_pairs={{0,16},{8,24},{16,0},{24,8},{1,17},{9,25},{17,1},{25,9},{2,18},{10... | collective-permute-start | bytes 49160 | tf_op jit(solution)/shard_map/ppermute | solution.py:35

commit v5 on v4

--- a/solution.py
+++ b/solution.py
@@ -60,10 +60,6 @@
 
 def order_of_members(peers):
     return [*range(0, peers, 2), *range(1, peers, 2)]
-
-
-def member_rows(distance, rows):
-    return pl.ds(pl.multiple_of((lax.axis_index("sub") ^ distance) * rows, rows), rows)
 
 
 def group_terms(array):
@@ -210,7 +206,9 @@
     rows = 32
     columns[...] = jnp.zeros(columns.shape, wide)
     for i, distance in enumerate(order_of_members(labels.shape[0] // 8)):
-        columns[pl.ds(i * rows, rows), :8] = labels[member_rows(distance, 8)].T[:rows]
+        columns[pl.ds(i * rows, rows), :8] = labels[
+            pl.ds(pl.multiple_of((lax.axis_index("sub") ^ distance) * 8, 8), 8)
+        ].T[:rows]
     across = columns[...].T
     weight, row, member = (across[i : i + 1] for i in range(3))
     same = (columns[:, 1:2] == row) & (columns[:, 2:3] == member) & (columns[:, 1:2] >= 0)
@@ -275,11 +273,10 @@
 
 
 def coarse_kernel(corners, table, *refs):
-    *every, first_every, passed, coarse, triple = refs
+    *every, passed, coarse, triple = refs
     rows = passed.shape[0]
-    members = first_every.shape[0] // rows
-    older = [first_every.at[member_rows(d, rows)] for d in order_of_members(members)]
-    groups = [every, older] if every else [older]
+    members = coarse.shape[0] // rows
+    groups = [every[:members], every[members:]] if len(every) > members else [every]
     count = len(groups)
     for i in range(members):
         put_triple(triple, i * rows, groups[0][i][...])
@@ -549,9 +546,7 @@
     )
     first = move(image_parts[0], "sub", near)
     third, fourth = move(image_parts[2], "grp", near), move(image_parts[3], "grp", far)
-    first, sent = lax.optimization_barrier((first, sent))
-    every = lax.all_gather(sent, "sub", axis=0, tiled=True)
-    image_parts[1], every = lax.optimization_barrier((image_parts[1], every))
+    every = gather_members(sent)
     image_others = [first, move(image_parts[1], "sub", far), third, fourth]
     tables = []
     for axis in range(2):
@@ -563,10 +558,18 @@
         )
     coarse_shapes = [message, gathered], [gathered_triple]
     passed, coarse = call(
-        functools.partial(coarse_kernel, corners), [coarse_table, every], *coarse_shapes, scalars=0
+        functools.partial(coarse_kernel, corners), [coarse_table, *every], *coarse_shapes, flops=0, scalars=0
     )
     (extra,) = call(
-        extra_kernel, [coarse, coupling_table, *tables[:2]], [whole], [values], scalars=0
+        extra_kernel,
+        [coarse, coupling_table, *tables[:2]],
+        [whole],
+        [values],
+        flops=8_000_000_000,
+        scalars=0,
+    )
+    image_others[2], image_others[3], passed = lax.optimization_barrier(
+        (image_others[2], image_others[3], passed)
     )
     near_passed, far_passed = move(passed, "grp", near), move(passed, "grp", far)
     *edges, passing, sums = call(
@@ -627,8 +630,9 @@
     every_next = gather_members(sent)
     passed, coarse = call(
         functools.partial(coarse_kernel, corners),
-        [coarse_table, *every_next, every],
+        [coarse_table, *every_next, *every],
         *coarse_shapes,
+        flops=1_000_000_000,
         scalars=0,
     )
     (extra,) = call(

time: 91.3 us -> 86.8 us (0.951)
  blocking collectives: 19.1 us -> 9.22 us
  starting transfers between devices: 29.6 us -> 34.4 us
    all_gather x1 -> x0, blocking collectives: 9.85 us -> none  [per_device(): every = lax.all_gather(sent, 'sub', axis=0, tiled=True)]
    ppermute x28 -> x35, starting transfers between devices: 29.6 us -> 34.4 us  [move(): lax.ppermute(array, axis, [(i, target(i) % peers) for i in range(peers)])]
    ppermute x28 -> x35, waiting for transfers between devices: 25.6 us -> 26.3 us  [move(): lax.ppermute(array, axis, [(i, target(i) % peers) for i in range(peers)])]
  transfers between devices with their start and end apart: 28 -> 35, of which waited for: 13 -> 15; matrix products, arithmetic and copies ran while one was open for 0% -> 0% of each run, Pallas kernels for 7% -> 8%
where the time goes in v5:
time: 86.8 us; the launch traced here: 86.6 us
  starting transfers between devices  34.4 us (40%)
  waiting for transfers between devices  26.3 us (30%)
  Pallas kernels  12.6 us (15%)
  blocking collectives  9.22 us (11%)
  local copies, waits for them, and re-layouts  2.54 us (3%)
  between operations  1.56 us (2%)
    ppermute x35, starting transfers between devices, move(): lax.ppermute(array, axis, [(i, target(i) % peers) for i in range(peers)])  34.4 us
    ppermute x35, waiting for transfers between devices, move(): lax.ppermute(array, axis, [(i, target(i) % peers) for i in range(peers)])  26.3 us
    pallas_call x20, Pallas kernels, call(): pl.pallas_call(body, out_shape=[jax.ShapeDtypeStruct(shape, kind) for sha...  12.6 us
    all_gather x1, blocking collectives, per_device(): labels = lax.all_gather(label_given, 'sub', axis=0, tiled=True)  9.22 us
  transfers between devices with their start and end apart: 35, of which 15 were waited for; matrix products, arithmetic and copies ran while one was open for 0% of the time, Pallas kernels for 8%

profile of v5, /device:TPU:0, one launch (start us, length us, event | category | flops | bytes accessed | tf_op | source)
XLA Modules:
  0.0 86.6 jit_solution(14435167638699575140)
XLA Ops:
  0.6 1.2 %slice_bitcast_fusion = (f32[128,512]{1,0:T(8,128)S(1)}, f32[128,512]{1,0:T(8,128)S(1)}) fusion(f32[1,1,256,512]{3,2,1,0:T(8,128)} %param.9), kind=kLoop, calls=%fused_computation | loop fusion | bytes 1048576 | tf_op jit(solution)/shard_map/slice | solution.py:497
  1.8 3.1 %collective-permute-start.1 = (f32[128,512]{1,0:T(8,128)S(1)}, f32[128,512]{1,0:T(8,128)S(1)}, u32[]{:S(2)}, u32[]{:S(2)}) collective-permute-start(f32[128,512]{1,0:T(8,128)S(1)} %get-tuple-element.132.upper), channel_id=1, source_target_pairs={{0,8},{8,16},{16,24},{24,0},{1,9},{9,17},{17,25},{25,1},{2,10},{10... | collective-permute-start | bytes 786440 | tf_op jit(solution)/shard_map/ppermute | solution.py:35
  4.9 0.7 copy-done.1
  5.6 0.7 copy-done.2
  6.2 1.4 %shard_map.105.matrix = bf16[512,1536]{1,0:T(8,128)(2,1)S(1)} custom-call(s32[4,4]{1,0:T(4,128)S(1)} %bitcast.16, f32[512,512]{1,0:T(8,128)S(1)} %bitcast.15, s32[2,128]{1,0:T(2,128)S(1)} %bitcast.18), custom_call_target="tpu_custom_call" | custom-call | flops 536870912 | bytes 1049664 | tf_op jit(solution)/shard_map/pallas_call | solution.py:22
  7.7 1.7 %shard_map.104 = (bf16[512,1536]{1,0:T(8,128)(2,1)S(1)}, bf16[24,1536]{1,0:T(8,128)(2,1)S(1)}, bf16[512,128]{1,0:T(8,128)(2,1)S(1)}, f32[8,512]{1,0:T(8,128)S(1)...) custom-call(s32[4,4]{1,0:T(4,128)S(1)} %bitcast.17, f32[512,512]{1,0:T(8,128)S(1)} %bitcast.22, ...), custom_call_target="tpu_custom_call" | custom-call | flops 536870912 | bytes 1098816 | tf_op jit(solution)/shard_map/pallas_call | solution.py:22
  9.4 3.8 %collective-permute-done.1.from_below = f32[128,512]{1,0:T(8,128)S(1)} collective-permute-done((f32[128,512]{1,0:T(8,128)S(1)}, f32[128,512]{1,0:T(8,128)S(1)}, u32[]{:S(2)}, u32[]{:S(2)}) %collective-permute-start.1) | collective-permute-done | bytes 262176 | tf_op jit(solution)/shard_map/ppermute | solution.py:35
  13.2 1.1 %shard_map.106 = (f32[512,512]{1,0:T(8,128)S(1)}, f32[136,512]{1,0:T(8,128)S(1)}, f32[136,512]{1,0:T(8,128)S(1)}, f32[136,512]{1,0:T(8,128)S(1)}, f32[136,512]{1,0:T(8,128)S(1)}, /*index=5*/f32[8,512]{1,0:T(8,128)S(1)}) custom-call(bf16[512,1536]{1,0:T(8,128)(2,1)S(1)} %get-tuple-element.70.matrix, f32[128,512]{1,0:T(8,128)S(1)} %get-tuple-element.133.right, ...), custom_call_target="tpu_custom_call" | custom-call | flops 805306368 | bytes 2686976 | tf_op jit(solution)/shard_map/pallas_call | solution.py:22
  14.4 2.4 %collective-permute-start.3 = (f32[136,512]{1,0:T(8,128)S(1)}, f32[136,512]{1,0:T(8,128)S(1)}, u32[]{:S(2)}, u32[]{:S(2)}) collective-permute-start(f32[136,512]{1,0:T(8,128)S(1)} %get-tuple-element.81.fourth), channel_id=1, source_target_pairs={{0,24},{8,16},{16,8},{24,0},{1,25},{9,17},{17,9},{25,1},{2,26},{10... | collective-permute-start | bytes 835592 | tf_op jit(solution)/shard_map/ppermute | solution.py:35
  16.8 1.7 %collective-permute-start.5 = (f32[136,512]{1,0:T(8,128)S(1)}, f32[136,512]{1,0:T(8,128)S(1)}, u32[]{:S(2)}, u32[]{:S(2)}) collective-permute-start(f32[136,512]{1,0:T(8,128)S(1)} %get-tuple-element.84.refs_1_), channel_id=1, source_target_pairs={{0,7},{1,2},{2,1},{3,4},{4,3},{5,6},{6,5},{7,0},{8,15},{9,10},{10,... | collective-permute-start | bytes 835592 | tf_op jit(solution)/shard_map/ppermute | solution.py:35
  19.2 9.2 %all_gather.3.labels = f32[64,128]{1,0:T(8,128)S(1)} all-gather(f32[8,128]{1,0:T(8,128)S(1)} %shard_map.107), channel_id=1, replica_groups=mesh['grp'=4,'sub'=8] {'sub'}, dimensions={0}, use_global_device_ids=true | all-gather | bytes 36864 | tf_op jit(solution)/shard_map/all_gather | solution.py:526
  28.5 0.4 shard_map.108.table
  28.9 1.0 %collective-permute-done.3.far_one.refs_1_ = f32[136,512]{1,0:T(8,128)S(1)} collective-permute-done((f32[136,512]{1,0:T(8,128)S(1)}, f32[136,512]{1,0:T(8,128)S(1)}, u32[]{:S(2)}, u32[]{:S(2)}) %collective-permute-start.3) | collective-permute-done | bytes 278560 | tf_op jit(solution)/shard_map/ppermute | solution.py:35
  30.0 1.2 %shard_map.110 = (f32[512,512]{1,0:T(8,128)S(1)}, f32[128,512]{1,0:T(8,128)S(1)}, f32[128,512]{1,0:T(8,128)S(1)}, f32[128,512]{1,0:T(8,128)S(1)}, f32[128,512]{1,0:T(8,128)S(1)}, /*index=5*/f32[32,512]{1,0:T(8,128)S(1)}) custom-call(bf16[512,1536]{1,0:T(8,128)(2,1)S(1)} %shard_map.105.matrix, bf16[24,1536]{1,0:T(8,128)(2,1)S(1)} %get-tuple-element.69.flat, ...), custom_call_target="tpu_custom_call" | custom-call | flops 805306368 | bytes 4087808 | tf_op jit(solution)/shard_map/pallas_call | solution.py:22
  31.2 1.3 %collective-permute-start.13 = (f32[128,512]{1,0:T(8,128)S(1)}, f32[128,512]{1,0:T(8,128)S(1)}, u32[]{:S(2)}, u32[]{:S(2)}) collective-permute-start(f32[128,512]{1,0:T(8,128)S(1)} %get-tuple-element.95.refs_6_), channel_id=1, source_target_pairs={{0,8},{8,0},{16,24},{24,16},{1,9},{9,1},{17,25},{25,17},{2,10},{10... | collective-permute-start | bytes 786440 | tf_op jit(solution)/shard_map/ppermute | solution.py:35
  32.5 1.7 %collective-permute-start.14 = (f32[128,512]{1,0:T(8,128)S(1)}, f32[128,512]{1,0:T(8,128)S(1)}, u32[]{:S(2)}, u32[]{:S(2)}) collective-permute-start(f32[128,512]{1,0:T(8,128)S(1)} %get-tuple-element.96.refs_7_), channel_id=1, source_target_pairs={{0,24},{8,16},{16,8},{24,0},{1,25},{9,17},{17,9},{25,1},{2,26},{10... | collective-permute-start | bytes 786440 | tf_op jit(solution)/shard_map/ppermute | solution.py:35
  34.2 2.5 %collective-permute-start.8 = (f32[32,512]{1,0:T(8,128)S(1)}, f32[32,512]{1,0:T(8,128)S(1)}, u32[]{:S(2)}, u32[]{:S(2)}) collective-permute-start(f32[32,512]{1,0:T(8,128)S(1)} %get-tuple-element.88.refs_0_.refs_8_), channel_id=1, source_target_pairs={{0,6},{1,7},{2,4},{3,5},{4,2},{5,3},{6,0},{7,1},{8,14},{9,15},{10,... | collective-permute-start | bytes 196616 | tf_op jit(solution)/shard_map/ppermute | solution.py:35
  36.7 0.5 collective-permute-start.7
  37.2 0.5 collective-permute-start.6
  37.7 1.9 %collective-permute-done.8.refs_3_.refs_11_ = f32[32,512]{1,0:T(8,128)S(1)} collective-permute-done((f32[32,512]{1,0:T(8,128)S(1)}, f32[32,512]{1,0:T(8,128)S(1)}, u32[]{:S(2)}, u32[]{:S(2)}) %collective-permute-start.8) | collective-permute-done | bytes 65568 | tf_op jit(solution)/shard_map/ppermute | solution.py:35
  39.6 1.4 %collective-permute-done.7.refs_2_.refs_10_ = f32[32,512]{1,0:T(8,128)S(1)} collective-permute-done((f32[32,512]{1,0:T(8,128)S(1)}, f32[32,512]{1,0:T(8,128)S(1)}, u32[]{:S(2)}, u32[]{:S(2)}) %collective-permute-start.7) | collective-permute-done | bytes 65568 | tf_op jit(solution)/shard_map/ppermute | solution.py:35
  41.0 0.4 collective-permute-done.6.refs_1_.refs_9_
  42.0 0.5 collective-permute-start.17
  42.5 1.4 %collective-permute-start.18 = (f32[128,512]{1,0:T(8,128)S(1)}, f32[128,512]{1,0:T(8,128)S(1)}, u32[]{:S(2)}, u32[]{:S(2)}) collective-permute-start(f32[128,512]{1,0:T(8,128)S(1)} %get-tuple-element.105.refs_1_), channel_id=1, source_target_pairs={{0,7},{1,2},{2,1},{3,4},{4,3},{5,6},{6,5},{7,0},{8,15},{9,10},{10,... | collective-permute-start | bytes 786440 | tf_op jit(solution)/shard_map/ppermute | solution.py:35
  44.0 0.4 shard_map.111
  44.4 0.9 %collective-permute-done.14.refs_8_ = f32[128,512]{1,0:T(8,128)S(1)} collective-permute-done((f32[128,512]{1,0:T(8,128)S(1)}, f32[128,512]{1,0:T(8,128)S(1)}, u32[]{:S(2)}, u32[]{:S(2)}) %collective-permute-start.14) | collective-permute-done | bytes 262176 | tf_op jit(solution)/shard_map/ppermute | solution.py:35
  45.3 1.8 %collective-permute-start.16 = (f32[32,512]{1,0:T(8,128)S(1)}, f32[32,512]{1,0:T(8,128)S(1)}, u32[]{:S(2)}, u32[]{:S(2)}) collective-permute-start(f32[32,512]{1,0:T(8,128)S(1)} %get-tuple-element.98.refs_3_), channel_id=1, source_target_pairs={{0,24},{8,16},{16,8},{24,0},{1,25},{9,17},{17,9},{25,1},{2,26},{10... | collective-permute-start | bytes 196616 | tf_op jit(solution)/shard_map/ppermute | solution.py:35
  47.7 3.7 %collective-permute-done.16.refs_5_ = f32[32,512]{1,0:T(8,128)S(1)} collective-permute-done((f32[32,512]{1,0:T(8,128)S(1)}, f32[32,512]{1,0:T(8,128)S(1)}, u32[]{:S(2)}, u32[]{:S(2)}) %collective-permute-start.16) | collective-permute-done | bytes 65568 | tf_op jit(solution)/shard_map/ppermute | solution.py:35
  51.4 0.5 collective-permute-done.15.refs_4_
  52.3 1.0 %shard_map.116 = (f32[512,512]{1,0:T(8,128)S(1)}, f32[128,512]{1,0:T(8,128)S(1)}, f32[128,512]{1,0:T(8,128)S(1)}, f32[136,512]{1,0:T(8,128)S(1)}, f32[128,512]{1,0:T(8,128)S(1)}) custom-call(bf16[512,1536]{1,0:T(8,128)(2,1)S(1)} %get-tuple-element.70.matrix, f32[512,512]{1,0:T(8,128)S(1)} %shard_map.113.refs_0_.extra, ...), custom_call_target="tpu_custom_call" | custom-call | flops 805306368 | bytes 4997120 | tf_op jit(solution)/shard_map/pallas_call | solution.py:22
  53.4 2.1 %collective-permute-start.19 = (f32[128,512]{1,0:T(8,128)S(1)}, f32[128,512]{1,0:T(8,128)S(1)}, u32[]{:S(2)}, u32[]{:S(2)}) collective-permute-start(f32[128,512]{1,0:T(8,128)S(1)} %get-tuple-element.108.fourth), channel_id=1, source_target_pairs={{0,24},{8,16},{16,8},{24,0},{1,25},{9,17},{17,9},{25,1},{2,26},{10... | collective-permute-start | bytes 786440 | tf_op jit(solution)/shard_map/ppermute | solution.py:35
  55.4 2.3 %collective-permute-start.22 = (f32[128,512]{1,0:T(8,128)S(1)}, f32[128,512]{1,0:T(8,128)S(1)}, u32[]{:S(2)}, u32[]{:S(2)}) collective-permute-start(f32[128,512]{1,0:T(8,128)S(1)} %get-tuple-element.116.refs_5_), channel_id=1, source_target_pairs={{0,7},{1,2},{2,1},{3,4},{4,3},{5,6},{6,5},{7,0},{8,15},{9,10},{10,... | collective-permute-start | bytes 786440 | tf_op jit(solution)/shard_map/ppermute | solution.py:35
  57.7 8.9 %collective-permute-done.19.far_one = f32[128,512]{1,0:T(8,128)S(1)} collective-permute-done((f32[128,512]{1,0:T(8,128)S(1)}, f32[128,512]{1,0:T(8,128)S(1)}, u32[]{:S(2)}, u32[]{:S(2)}) %collective-permute-start.19) | collective-permute-done | bytes 262176 | tf_op jit(solution)/shard_map/ppermute | solution.py:35
  66.6 0.5 shard_map.117
  67.1 1.4 %shard_map.118 = (f32[512,512]{1,0:T(8,128)S(1)}, f32[512,512]{1,0:T(8,128)S(1)}, f32[128,512]{1,0:T(8,128)S(1)}, f32[128,512]{1,0:T(8,128)S(1)}, f32[512,512]{1,0:T(8,128)S(1)}, /*index=5*/f32[32,512]{1,0:T(8,128)S(1)}) custom-call(bf16[512,1536]{1,0:T(8,128)(2,1)S(1)} %shard_map.105.matrix, bf16[24,1536]{1,0:T(8,128)(2,1)S(1)} %get-tuple-element.69.flat, ...), custom_call_target="tpu_custom_call" | custom-call | flops 805306368 | bytes 7708672 | tf_op jit(solution)/shard_map/pallas_call | solution.py:22
  68.5 2.6 %collective-permute-start.25 = (f32[32,512]{1,0:T(8,128)S(1)}, f32[32,512]{1,0:T(8,128)S(1)}, u32[]{:S(2)}, u32[]{:S(2)}) collective-permute-start(f32[32,512]{1,0:T(8,128)S(1)} %get-tuple-element.125.refs_0_), channel_id=1, source_target_pairs={{0,6},{1,7},{2,4},{3,5},{4,2},{5,3},{6,0},{7,1},{8,14},{9,15},{10,... | collective-permute-start | bytes 196616 | tf_op jit(solution)/shard_map/ppermute | solution.py:35
  71.1 0.8 collective-permute-start.24
  72.0 1.7 %collective-permute-start.30 = (f32[128,512]{1,0:T(8,128)S(1)}, f32[128,512]{1,0:T(8,128)S(1)}, u32[]{:S(2)}, u32[]{:S(2)}) collective-permute-start(f32[128,512]{1,0:T(8,128)S(1)} %get-tuple-element.127), channel_id=1, source_target_pairs={{0,7},{1,0},{2,1},{3,2},{4,3},{5,4},{6,5},{7,6},{8,15},{9,8},{10,9... | collective-permute-start | bytes 786440 | tf_op jit(solution)/shard_map/ppermute | solution.py:35
  73.8 1.8 %collective-permute-start.31 = (f32[128,512]{1,0:T(8,128)S(1)}, f32[128,512]{1,0:T(8,128)S(1)}, u32[]{:S(2)}, u32[]{:S(2)}) collective-permute-start(f32[128,512]{1,0:T(8,128)S(1)} %get-tuple-element.128), channel_id=1, source_target_pairs={{0,24},{8,0},{16,8},{24,16},{1,25},{9,1},{17,9},{25,17},{2,26},{10... | collective-permute-start | bytes 786440 | tf_op jit(solution)/shard_map/ppermute | solution.py:35
  75.6 0.5 collective-permute-start.28
  76.2 0.6 collective-permute-done.29.refs_7_
  77.0 0.4 collective-permute-done.27.refs_5_
  77.4 0.4 shard_map.121
  77.9 1.8 %collective-permute-start.33 = (f32[32,512]{1,0:T(8,128)S(1)}, f32[32,512]{1,0:T(8,128)S(1)}, u32[]{:S(2)}, u32[]{:S(2)}) collective-permute-start(f32[32,512]{1,0:T(8,128)S(1)} %get-tuple-element.129), channel_id=1, source_target_pairs={{0,24},{8,16},{16,8},{24,0},{1,25},{9,17},{17,9},{25,1},{2,26},{10... | collective-permute-start | bytes 196616 | tf_op jit(solution)/shard_map/ppermute | solution.py:35
  79.6 0.4 collective-permute-start.32
  80.0 2.3 %collective-permute-start.34 = (f32[8,512]{1,0:T(8,128)S(1)}, f32[8,512]{1,0:T(8,128)S(1)}, u32[]{:S(2)}, u32[]{:S(2)}) collective-permute-start(f32[8,512]{1,0:T(8,128)S(1)} %slice.20.refs_13_), channel_id=1, source_target_pairs={{0,16},{8,24},{16,0},{24,8},{1,17},{9,25},{17,1},{25,9},{2,18},{10... | collective-permute-start | bytes 49160 | tf_op jit(solution)/shard_map/ppermute | solution.py:35
  82.9 2.1 %collective-permute-done.34.refs_14_ = f32[8,512]{1,0:T(8,128)S(1)} collective-permute-done((f32[8,512]{1,0:T(8,128)S(1)}, f32[8,512]{1,0:T(8,128)S(1)}, u32[]{:S(2)}, u32[]{:S(2)}) %collective-permute-start.34) | collective-permute-done | bytes 16416 | tf_op jit(solution)/shard_map/ppermute | solution.py:35
  85.3 1.3 %shard_map.123 = (f32[256,512]{1,0:T(8,128)}, f32[256,512]{1,0:T(8,128)}) custom-call(f32[256,512]{1,0:T(8,128)S(1)} %get-tuple-element.118.refs_0_, f32[256,512]{1,0:T(8,128)S(1)} %get-tuple-element.119.refs_1_, f32[256,512]{1,0:T(8,128)S(1)} %get-tuple-element.122.refs_2_, f32[256,512]{1,0:T(8,128)S(1)} %get-tuple-element.123.refs_3_, ...), custom_call_target="tpu_custom_call" | custom-call | bytes 4440064 | tf_op jit(solution)/shard_map/pallas_call | solution.py:22
  (59 shorter events, 3.3 us)
Async XLA Ops:
  0.6 4.2 %copy-start = (f32[1,1,512,512]{3,2,1,0:T(8,128)S(1)}, f32[1,1,512,512]{3,2,1,0:T(8,128)}, u32[]{:S(2)}) copy-start(f32[1,1,512,512]{3,2,1,0:T(8,128)} %param.10) | copy-start | bytes 3145732
  1.8 11.4 %collective-permute-start.1 = (f32[128,512]{1,0:T(8,128)S(1)}, f32[128,512]{1,0:T(8,128)S(1)}, u32[]{:S(2)}, u32[]{:S(2)}) collective-permute-start(f32[128,512]{1,0:T(8,128)S(1)} %get-tuple-element.132.upper), channel_id=1, source_target_pairs={{0,8},{8,16},{16,24},{24,0},{1,9},{9,17},{17,25},{25,1},{2,10},{10... | collective-permute-start | bytes 786440 | tf_op jit(solution)/shard_map/ppermute | solution.py:35
  4.9 8.3 %collective-permute-start = (f32[128,512]{1,0:T(8,128)S(1)}, f32[128,512]{1,0:T(8,128)S(1)}, u32[]{:S(2)}, u32[]{:S(2)}) collective-permute-start(f32[128,512]{1,0:T(8,128)S(1)} %get-tuple-element.133.right), channel_id=1, source_target_pairs={{0,1},{1,2},{2,3},{3,4},{4,5},{5,6},{6,7},{7,0},{8,9},{9,10},{10,1... | collective-permute-start | bytes 786440 | tf_op jit(solution)/shard_map/ppermute | solution.py:35
  4.9 0.7 copy-start.1
  5.6 0.7 copy-start.2
  6.2 1.4 %copy-start.5 = (f32[1,1,512,512]{3,2,1,0:T(8,128)S(1)}, f32[1,1,512,512]{3,2,1,0:T(8,128)}, u32[]{:S(2)}) copy-start(f32[1,1,512,512]{3,2,1,0:T(8,128)} %param.11) | copy-start | bytes 3145732
  6.2 1.4 %copy-start.6 = (f32[1,1,512,24]{2,3,1,0:T(8,128)S(1)}, f32[1,1,512,24]{2,3,1,0:T(8,128)}, u32[]{:S(2)}) copy-start(f32[1,1,512,24]{2,3,1,0:T(8,128)} %param.12) | copy-start | bytes 147460
  9.4 9.8 %copy-start.3 = (f32[1,1,24]{2,1,0:T(1,128)S(1)}, f32[1,1,24]{2,1,0:T(1,128)}, u32[]{:S(2)}) copy-start(f32[1,1,24]{2,1,0:T(1,128)} %param.13) | copy-start | bytes 292
  9.4 9.8 %copy-start.4 = (s32[1,1,24]{2,1,0:T(1,128)S(1)}, s32[1,1,24]{2,1,0:T(1,128)}, u32[]{:S(2)}) copy-start(s32[1,1,24]{2,1,0:T(1,128)} %param.14) | copy-start | bytes 292
  14.3 5.0 %collective-permute-start.2 = (f32[136,512]{1,0:T(8,128)S(1)}, f32[136,512]{1,0:T(8,128)S(1)}, u32[]{:S(2)}, u32[]{:S(2)}) collective-permute-start(f32[136,512]{1,0:T(8,128)S(1)} %get-tuple-element.77.refs_0_), channel_id=1, source_target_pairs={{0,1},{1,0},{2,3},{3,2},{4,5},{5,4},{6,7},{7,6},{8,9},{9,8},{10,11... | collective-permute-start | bytes 835592 | tf_op jit(solution)/shard_map/ppermute | solution.py:35
  14.3 14.6 %collective-permute-start.4 = (f32[136,512]{1,0:T(8,128)S(1)}, f32[136,512]{1,0:T(8,128)S(1)}, u32[]{:S(2)}, u32[]{:S(2)}) collective-permute-start(f32[136,512]{1,0:T(8,128)S(1)} %get-tuple-element.80.third), channel_id=1, source_target_pairs={{0,8},{8,0},{16,24},{24,16},{1,9},{9,1},{17,25},{25,17},{2,10},{10... | collective-permute-start | bytes 835592 | tf_op jit(solution)/shard_map/ppermute | solution.py:35
  14.4 15.5 %collective-permute-start.3 = (f32[136,512]{1,0:T(8,128)S(1)}, f32[136,512]{1,0:T(8,128)S(1)}, u32[]{:S(2)}, u32[]{:S(2)}) collective-permute-start(f32[136,512]{1,0:T(8,128)S(1)} %get-tuple-element.81.fourth), channel_id=1, source_target_pairs={{0,24},{8,16},{16,8},{24,0},{1,25},{9,17},{17,9},{25,1},{2,26},{10... | collective-permute-start | bytes 835592 | tf_op jit(solution)/shard_map/ppermute | solution.py:35
  16.8 13.2 %collective-permute-start.5 = (f32[136,512]{1,0:T(8,128)S(1)}, f32[136,512]{1,0:T(8,128)S(1)}, u32[]{:S(2)}, u32[]{:S(2)}) collective-permute-start(f32[136,512]{1,0:T(8,128)S(1)} %get-tuple-element.84.refs_1_), channel_id=1, source_target_pairs={{0,7},{1,2},{2,1},{3,4},{4,3},{5,6},{6,5},{7,0},{8,15},{9,10},{10,... | collective-permute-start | bytes 835592 | tf_op jit(solution)/shard_map/ppermute | solution.py:35
  31.2 13.2 %collective-permute-start.13 = (f32[128,512]{1,0:T(8,128)S(1)}, f32[128,512]{1,0:T(8,128)S(1)}, u32[]{:S(2)}, u32[]{:S(2)}) collective-permute-start(f32[128,512]{1,0:T(8,128)S(1)} %get-tuple-element.95.refs_6_), channel_id=1, source_target_pairs={{0,8},{8,0},{16,24},{24,16},{1,9},{9,1},{17,25},{25,17},{2,10},{10... | collective-permute-start | bytes 786440 | tf_op jit(solution)/shard_map/ppermute | solution.py:35
  32.5 12.8 %collective-permute-start.14 = (f32[128,512]{1,0:T(8,128)S(1)}, f32[128,512]{1,0:T(8,128)S(1)}, u32[]{:S(2)}, u32[]{:S(2)}) collective-permute-start(f32[128,512]{1,0:T(8,128)S(1)} %get-tuple-element.96.refs_7_), channel_id=1, source_target_pairs={{0,24},{8,16},{16,8},{24,0},{1,25},{9,17},{17,9},{25,1},{2,26},{10... | collective-permute-start | bytes 786440 | tf_op jit(solution)/shard_map/ppermute | solution.py:35
  34.2 3.0 %collective-permute-start.9 = (f32[32,512]{1,0:T(8,128)S(1)}, f32[32,512]{1,0:T(8,128)S(1)}, u32[]{:S(2)}, u32[]{:S(2)}) collective-permute-start(f32[32,512]{1,0:T(8,128)S(1)} %get-tuple-element.88.refs_0_.refs_8_), channel_id=1, source_target_pairs={{0,1},{1,0},{2,3},{3,2},{4,5},{5,4},{6,7},{7,6},{8,9},{9,8},{10,11... | collective-permute-start | bytes 196616 | tf_op jit(solution)/shard_map/ppermute | solution.py:35
  34.2 5.4 %collective-permute-start.8 = (f32[32,512]{1,0:T(8,128)S(1)}, f32[32,512]{1,0:T(8,128)S(1)}, u32[]{:S(2)}, u32[]{:S(2)}) collective-permute-start(f32[32,512]{1,0:T(8,128)S(1)} %get-tuple-element.88.refs_0_.refs_8_), channel_id=1, source_target_pairs={{0,6},{1,7},{2,4},{3,5},{4,2},{5,3},{6,0},{7,1},{8,14},{9,15},{10,... | collective-permute-start | bytes 196616 | tf_op jit(solution)/shard_map/ppermute | solution.py:35
  36.7 4.4 %collective-permute-start.7 = (f32[32,512]{1,0:T(8,128)S(1)}, f32[32,512]{1,0:T(8,128)S(1)}, u32[]{:S(2)}, u32[]{:S(2)}) collective-permute-start(f32[32,512]{1,0:T(8,128)S(1)} %get-tuple-element.88.refs_0_.refs_8_), channel_id=1, source_target_pairs={{0,4},{1,5},{2,6},{3,7},{4,0},{5,1},{6,2},{7,3},{8,12},{9,13},{10,... | collective-permute-start | bytes 196616 | tf_op jit(solution)/shard_map/ppermute | solution.py:35
  37.2 4.3 %collective-permute-start.6 = (f32[32,512]{1,0:T(8,128)S(1)}, f32[32,512]{1,0:T(8,128)S(1)}, u32[]{:S(2)}, u32[]{:S(2)}) collective-permute-start(f32[32,512]{1,0:T(8,128)S(1)} %get-tuple-element.88.refs_0_.refs_8_), channel_id=1, source_target_pairs={{0,2},{1,3},{2,0},{3,1},{4,6},{5,7},{6,4},{7,5},{8,10},{9,11},{10,... | collective-permute-start | bytes 196616 | tf_op jit(solution)/shard_map/ppermute | solution.py:35
  39.6 2.4 %collective-permute-start.12 = (f32[32,512]{1,0:T(8,128)S(1)}, f32[32,512]{1,0:T(8,128)S(1)}, u32[]{:S(2)}, u32[]{:S(2)}) collective-permute-start(f32[32,512]{1,0:T(8,128)S(1)} %collective-permute-done.8.refs_3_.refs_11_), channel_id=1, source_target_pairs={{0,1},{1,0},{2,3},{3,2},{4,5},{5,4},{6,7},{7,6},{8,9},{9,8},{10,11... | collective-permute-start | bytes 196616 | tf_op jit(solution)/shard_map/ppermute | solution.py:35
  41.0 1.5 %collective-permute-start.11 = (f32[32,512]{1,0:T(8,128)S(1)}, f32[32,512]{1,0:T(8,128)S(1)}, u32[]{:S(2)}, u32[]{:S(2)}) collective-permute-start(f32[32,512]{1,0:T(8,128)S(1)} %collective-permute-done.7.refs_2_.refs_10_), channel_id=1, source_target_pairs={{0,1},{1,0},{2,3},{3,2},{4,5},{5,4},{6,7},{7,6},{8,9},{9,8},{10,11... | collective-permute-start | bytes 196616 | tf_op jit(solution)/shard_map/ppermute | solution.py:35
  41.5 2.5 %collective-permute-start.10 = (f32[32,512]{1,0:T(8,128)S(1)}, f32[32,512]{1,0:T(8,128)S(1)}, u32[]{:S(2)}, u32[]{:S(2)}) collective-permute-start(f32[32,512]{1,0:T(8,128)S(1)} %collective-permute-done.6.refs_1_.refs_9_), channel_id=1, source_target_pairs={{0,1},{1,0},{2,3},{3,2},{4,5},{5,4},{6,7},{7,6},{8,9},{9,8},{10,11... | collective-permute-start | bytes 196616 | tf_op jit(solution)/shard_map/ppermute | solution.py:35
  42.0 10.2 %collective-permute-start.17 = (f32[128,512]{1,0:T(8,128)S(1)}, f32[128,512]{1,0:T(8,128)S(1)}, u32[]{:S(2)}, u32[]{:S(2)}) collective-permute-start(f32[128,512]{1,0:T(8,128)S(1)} %get-tuple-element.104.refs_0_), channel_id=1, source_target_pairs={{0,1},{1,0},{2,3},{3,2},{4,5},{5,4},{6,7},{7,6},{8,9},{9,8},{10,11... | collective-permute-start | bytes 786440 | tf_op jit(solution)/shard_map/ppermute | solution.py:35
  42.5 9.8 %collective-permute-start.18 = (f32[128,512]{1,0:T(8,128)S(1)}, f32[128,512]{1,0:T(8,128)S(1)}, u32[]{:S(2)}, u32[]{:S(2)}) collective-permute-start(f32[128,512]{1,0:T(8,128)S(1)} %get-tuple-element.105.refs_1_), channel_id=1, source_target_pairs={{0,7},{1,2},{2,1},{3,4},{4,3},{5,6},{6,5},{7,0},{8,15},{9,10},{10,... | collective-permute-start | bytes 786440 | tf_op jit(solution)/shard_map/ppermute | solution.py:35
  45.3 6.2 %collective-permute-start.16 = (f32[32,512]{1,0:T(8,128)S(1)}, f32[32,512]{1,0:T(8,128)S(1)}, u32[]{:S(2)}, u32[]{:S(2)}) collective-permute-start(f32[32,512]{1,0:T(8,128)S(1)} %get-tuple-element.98.refs_3_), channel_id=1, source_target_pairs={{0,24},{8,16},{16,8},{24,0},{1,25},{9,17},{17,9},{25,1},{2,26},{10... | collective-permute-start | bytes 196616 | tf_op jit(solution)/shard_map/ppermute | solution.py:35
  47.0 5.0 %collective-permute-start.15 = (f32[32,512]{1,0:T(8,128)S(1)}, f32[32,512]{1,0:T(8,128)S(1)}, u32[]{:S(2)}, u32[]{:S(2)}) collective-permute-start(f32[32,512]{1,0:T(8,128)S(1)} %get-tuple-element.98.refs_3_), channel_id=1, source_target_pairs={{0,8},{8,0},{16,24},{24,16},{1,9},{9,1},{17,25},{25,17},{2,10},{10... | collective-permute-start | bytes 196616 | tf_op jit(solution)/shard_map/ppermute | solution.py:35
  53.3 13.3 %collective-permute-start.20 = (f32[136,512]{1,0:T(8,128)S(1)}, f32[136,512]{1,0:T(8,128)S(1)}, u32[]{:S(2)}, u32[]{:S(2)}) collective-permute-start(f32[136,512]{1,0:T(8,128)S(1)} %get-tuple-element.107.third), channel_id=1, source_target_pairs={{0,8},{8,0},{16,24},{24,16},{1,9},{9,1},{17,25},{25,17},{2,10},{10... | collective-permute-start | bytes 835592 | tf_op jit(solution)/shard_map/ppermute | solution.py:35
  53.4 13.2 %collective-permute-start.19 = (f32[128,512]{1,0:T(8,128)S(1)}, f32[128,512]{1,0:T(8,128)S(1)}, u32[]{:S(2)}, u32[]{:S(2)}) collective-permute-start(f32[128,512]{1,0:T(8,128)S(1)} %get-tuple-element.108.fourth), channel_id=1, source_target_pairs={{0,24},{8,16},{16,8},{24,0},{1,25},{9,17},{17,9},{25,1},{2,26},{10... | collective-permute-start | bytes 786440 | tf_op jit(solution)/shard_map/ppermute | solution.py:35
  55.4 11.6 %collective-permute-start.21 = (f32[128,512]{1,0:T(8,128)S(1)}, f32[128,512]{1,0:T(8,128)S(1)}, u32[]{:S(2)}, u32[]{:S(2)}) collective-permute-start(f32[128,512]{1,0:T(8,128)S(1)} %get-tuple-element.115.refs_4_), channel_id=1, source_target_pairs={{0,1},{1,0},{2,3},{3,2},{4,5},{5,4},{6,7},{7,6},{8,9},{9,8},{10,11... | collective-permute-start | bytes 786440 | tf_op jit(solution)/shard_map/ppermute | solution.py:35
  55.4 11.7 %collective-permute-start.22 = (f32[128,512]{1,0:T(8,128)S(1)}, f32[128,512]{1,0:T(8,128)S(1)}, u32[]{:S(2)}, u32[]{:S(2)}) collective-permute-start(f32[128,512]{1,0:T(8,128)S(1)} %get-tuple-element.116.refs_5_), channel_id=1, source_target_pairs={{0,7},{1,2},{2,1},{3,4},{4,3},{5,6},{6,5},{7,0},{8,15},{9,10},{10,... | collective-permute-start | bytes 786440 | tf_op jit(solution)/shard_map/ppermute | solution.py:35
  68.5 5.3 %collective-permute-start.26 = (f32[32,512]{1,0:T(8,128)S(1)}, f32[32,512]{1,0:T(8,128)S(1)}, u32[]{:S(2)}, u32[]{:S(2)}) collective-permute-start(f32[32,512]{1,0:T(8,128)S(1)} %get-tuple-element.125.refs_0_), channel_id=1, source_target_pairs={{0,1},{1,0},{2,3},{3,2},{4,5},{5,4},{6,7},{7,6},{8,9},{9,8},{10,11... | collective-permute-start | bytes 196616 | tf_op jit(solution)/shard_map/ppermute | solution.py:35
  68.5 7.0 %collective-permute-start.25 = (f32[32,512]{1,0:T(8,128)S(1)}, f32[32,512]{1,0:T(8,128)S(1)}, u32[]{:S(2)}, u32[]{:S(2)}) collective-permute-start(f32[32,512]{1,0:T(8,128)S(1)} %get-tuple-element.125.refs_0_), channel_id=1, source_target_pairs={{0,6},{1,7},{2,4},{3,5},{4,2},{5,3},{6,0},{7,1},{8,14},{9,15},{10,... | collective-permute-start | bytes 196616 | tf_op jit(solution)/shard_map/ppermute | solution.py:35
  71.1 4.5 %collective-permute-start.24 = (f32[32,512]{1,0:T(8,128)S(1)}, f32[32,512]{1,0:T(8,128)S(1)}, u32[]{:S(2)}, u32[]{:S(2)}) collective-permute-start(f32[32,512]{1,0:T(8,128)S(1)} %get-tuple-element.125.refs_0_), channel_id=1, source_target_pairs={{0,4},{1,5},{2,6},{3,7},{4,0},{5,1},{6,2},{7,3},{8,12},{9,13},{10,... | collective-permute-start | bytes 196616 | tf_op jit(solution)/shard_map/ppermute | solution.py:35
  71.9 4.3 %collective-permute-start.23 = (f32[32,512]{1,0:T(8,128)S(1)}, f32[32,512]{1,0:T(8,128)S(1)}, u32[]{:S(2)}, u32[]{:S(2)}) collective-permute-start(f32[32,512]{1,0:T(8,128)S(1)} %get-tuple-element.125.refs_0_), channel_id=1, source_target_pairs={{0,2},{1,3},{2,0},{3,1},{4,6},{5,7},{6,4},{7,5},{8,10},{9,11},{10,... | collective-permute-start | bytes 196616 | tf_op jit(solution)/shard_map/ppermute | solution.py:35
  72.0 13.2 %collective-permute-start.30 = (f32[128,512]{1,0:T(8,128)S(1)}, f32[128,512]{1,0:T(8,128)S(1)}, u32[]{:S(2)}, u32[]{:S(2)}) collective-permute-start(f32[128,512]{1,0:T(8,128)S(1)} %get-tuple-element.127), channel_id=1, source_target_pairs={{0,7},{1,0},{2,1},{3,2},{4,3},{5,4},{6,5},{7,6},{8,15},{9,8},{10,9... | collective-permute-start | bytes 786440 | tf_op jit(solution)/shard_map/ppermute | solution.py:35
  73.8 11.5 %collective-permute-start.31 = (f32[128,512]{1,0:T(8,128)S(1)}, f32[128,512]{1,0:T(8,128)S(1)}, u32[]{:S(2)}, u32[]{:S(2)}) collective-permute-start(f32[128,512]{1,0:T(8,128)S(1)} %get-tuple-element.128), channel_id=1, source_target_pairs={{0,24},{8,0},{16,8},{24,16},{1,25},{9,1},{17,9},{25,17},{2,26},{10... | collective-permute-start | bytes 786440 | tf_op jit(solution)/shard_map/ppermute | solution.py:35
  75.5 1.3 %collective-permute-start.29 = (f32[32,512]{1,0:T(8,128)S(1)}, f32[32,512]{1,0:T(8,128)S(1)}, u32[]{:S(2)}, u32[]{:S(2)}) collective-permute-start(f32[32,512]{1,0:T(8,128)S(1)} %collective-permute-done.25.refs_3_), channel_id=1, source_target_pairs={{0,1},{1,0},{2,3},{3,2},{4,5},{5,4},{6,7},{7,6},{8,9},{9,8},{10,11... | collective-permute-start | bytes 196616 | tf_op jit(solution)/shard_map/ppermute | solution.py:35
  75.6 1.4 %collective-permute-start.28 = (f32[32,512]{1,0:T(8,128)S(1)}, f32[32,512]{1,0:T(8,128)S(1)}, u32[]{:S(2)}, u32[]{:S(2)}) collective-permute-start(f32[32,512]{1,0:T(8,128)S(1)} %collective-permute-done.24.refs_2_), channel_id=1, source_target_pairs={{0,1},{1,0},{2,3},{3,2},{4,5},{5,4},{6,7},{7,6},{8,9},{9,8},{10,11... | collective-permute-start | bytes 196616 | tf_op jit(solution)/shard_map/ppermute | solution.py:35
  76.2 1.3 %collective-permute-start.27 = (f32[32,512]{1,0:T(8,128)S(1)}, f32[32,512]{1,0:T(8,128)S(1)}, u32[]{:S(2)}, u32[]{:S(2)}) collective-permute-start(f32[32,512]{1,0:T(8,128)S(1)} %collective-permute-done.23.refs_1_), channel_id=1, source_target_pairs={{0,1},{1,0},{2,3},{3,2},{4,5},{5,4},{6,7},{7,6},{8,9},{9,8},{10,11... | collective-permute-start | bytes 196616 | tf_op jit(solution)/shard_map/ppermute | solution.py:35
  77.9 7.1 %collective-permute-start.33 = (f32[32,512]{1,0:T(8,128)S(1)}, f32[32,512]{1,0:T(8,128)S(1)}, u32[]{:S(2)}, u32[]{:S(2)}) collective-permute-start(f32[32,512]{1,0:T(8,128)S(1)} %get-tuple-element.129), channel_id=1, source_target_pairs={{0,24},{8,16},{16,8},{24,0},{1,25},{9,17},{17,9},{25,1},{2,26},{10... | collective-permute-start | bytes 196616 | tf_op jit(solution)/shard_map/ppermute | solution.py:35
  79.6 5.6 %collective-permute-start.32 = (f32[32,512]{1,0:T(8,128)S(1)}, f32[32,512]{1,0:T(8,128)S(1)}, u32[]{:S(2)}, u32[]{:S(2)}) collective-permute-start(f32[32,512]{1,0:T(8,128)S(1)} %get-tuple-element.129), channel_id=1, source_target_pairs={{0,8},{8,0},{16,24},{24,16},{1,9},{9,1},{17,25},{25,17},{2,10},{10... | collective-permute-start | bytes 196616 | tf_op jit(solution)/shard_map/ppermute | solution.py:35
  80.0 4.9 %collective-permute-start.34 = (f32[8,512]{1,0:T(8,128)S(1)}, f32[8,512]{1,0:T(8,128)S(1)}, u32[]{:S(2)}, u32[]{:S(2)}) collective-permute-start(f32[8,512]{1,0:T(8,128)S(1)} %slice.20.refs_13_), channel_id=1, source_target_pairs={{0,16},{8,24},{16,0},{24,8},{1,17},{9,25},{17,1},{25,9},{2,18},{10... | collective-permute-start | bytes 49160 | tf_op jit(solution)/shard_map/ppermute | solution.py:35

commit v6 on v5

--- a/solution.py
+++ b/solution.py
@@ -413,9 +413,9 @@
         back[...] = dense[here]
     message[:corners] = both_dots(flat, triple, triple_grp)
     message[pl.ds(corners, 8)] = jnp.zeros((8, local.shape[1]), wide)
-    message[pl.ds(corners, 2)] = 0.5 * sums
-    message[pl.ds(corners + 2, 1)] = column_sum(search_next[...], local)
-    message[pl.ds(corners + 3, 1)] = column_sum(search[...], local)
+    message[pl.ds(corners, 1)] = 0.5 * sums[:1]
+    message[pl.ds(corners + 1, 1)] = column_sum(search_next[...], local)
+    message[pl.ds(corners + 2, 1)] = 0.5 * sums[1:2]
 
 
 def owned_kernel(*refs):
@@ -439,9 +439,9 @@
         newer = newer[-8:] + near_passed[pl.ds(corners, 8)] + far_passed[pl.ds(corners, 8)]
     gamma, slope = old_total[:1], old_total[1:2]
     alpha = gamma / slope
-    gamma_next, cross, steep, cross_other = (newer[i : i + 1] for i in range(4))
+    gamma_next, steep, cross = (newer[i : i + 1] for i in range(3))
     beta = gamma_next / gamma
-    alpha_next = gamma_next / (steep + beta * (cross + cross_other + beta * slope))
+    alpha_next = gamma_next / (steep + beta * (2.0 * cross + beta * slope))
     upper = odd[1] == 1
     table = jnp.where(upper, far_table[...].astype(wide), near_table[...].astype(wide))
     put_values(values, jnp.where(upper, far_passed[...], near_passed[...]))
@@ -630,7 +630,7 @@
     every_next = gather_members(sent)
     passed, coarse = call(
         functools.partial(coarse_kernel, corners),
-        [coarse_table, *every_next, *every],
+        [coarse_table, *every_next],
         *coarse_shapes,
         flops=1_000_000_000,
         scalars=0,

time: 86.8 us -> 86.8 us (level)
  no operation moved by 1% of the time
where the time goes in v6:
time: 86.8 us; the launch traced here: 86.5 us
  starting transfers between devices  34.4 us (40%)
  waiting for transfers between devices  26.3 us (30%)
  Pallas kernels  12.5 us (14%)
  blocking collectives  9.22 us (11%)
  local copies, waits for them, and re-layouts  2.54 us (3%)
  between operations  1.57 us (2%)
    ppermute x35, starting transfers between devices, move(): lax.ppermute(array, axis, [(i, target(i) % peers) for i in range(peers)])  34.4 us
    ppermute x35, waiting for transfers between devices, move(): lax.ppermute(array, axis, [(i, target(i) % peers) for i in range(peers)])  26.3 us
    pallas_call x20, Pallas kernels, call(): pl.pallas_call(body, out_shape=[jax.ShapeDtypeStruct(shape, kind) for sha...  12.5 us
    all_gather x1, blocking collectives, per_device(): labels = lax.all_gather(label_given, 'sub', axis=0, tiled=True)  9.22 us
  transfers between devices with their start and end apart: 35, of which 15 were waited for; matrix products, arithmetic and copies ran while one was open for 0% of the time, Pallas kernels for 8%

profile of v6, /device:TPU:0, one launch (start us, length us, event | category | flops | bytes accessed | tf_op | source)
XLA Modules:
  0.0 86.5 jit_solution(11555803779177514530)
XLA Ops:
  0.6 1.2 %slice_bitcast_fusion = (f32[128,512]{1,0:T(8,128)S(1)}, f32[128,512]{1,0:T(8,128)S(1)}) fusion(f32[1,1,256,512]{3,2,1,0:T(8,128)} %param.9), kind=kLoop, calls=%fused_computation | loop fusion | bytes 1048576 | tf_op jit(solution)/shard_map/slice | solution.py:497
  1.8 3.1 %collective-permute-start.1 = (f32[128,512]{1,0:T(8,128)S(1)}, f32[128,512]{1,0:T(8,128)S(1)}, u32[]{:S(2)}, u32[]{:S(2)}) collective-permute-start(f32[128,512]{1,0:T(8,128)S(1)} %get-tuple-element.132.upper), channel_id=1, source_target_pairs={{0,8},{8,16},{16,24},{24,0},{1,9},{9,17},{17,25},{25,1},{2,10},{10... | collective-permute-start | bytes 786440 | tf_op jit(solution)/shard_map/ppermute | solution.py:35
  4.9 0.7 copy-done.1
  5.6 0.7 copy-done.2
  6.2 1.4 %shard_map.105.matrix = bf16[512,1536]{1,0:T(8,128)(2,1)S(1)} custom-call(s32[4,4]{1,0:T(4,128)S(1)} %bitcast.16, f32[512,512]{1,0:T(8,128)S(1)} %bitcast.15, s32[2,128]{1,0:T(2,128)S(1)} %bitcast.18), custom_call_target="tpu_custom_call" | custom-call | flops 536870912 | bytes 1049664 | tf_op jit(solution)/shard_map/pallas_call | solution.py:22
  7.7 1.7 %shard_map.104 = (bf16[512,1536]{1,0:T(8,128)(2,1)S(1)}, bf16[24,1536]{1,0:T(8,128)(2,1)S(1)}, bf16[512,128]{1,0:T(8,128)(2,1)S(1)}, f32[8,512]{1,0:T(8,128)S(1)...) custom-call(s32[4,4]{1,0:T(4,128)S(1)} %bitcast.17, f32[512,512]{1,0:T(8,128)S(1)} %bitcast.22, ...), custom_call_target="tpu_custom_call" | custom-call | flops 536870912 | bytes 1098816 | tf_op jit(solution)/shard_map/pallas_call | solution.py:22
  9.4 3.8 %collective-permute-done.1.from_below = f32[128,512]{1,0:T(8,128)S(1)} collective-permute-done((f32[128,512]{1,0:T(8,128)S(1)}, f32[128,512]{1,0:T(8,128)S(1)}, u32[]{:S(2)}, u32[]{:S(2)}) %collective-permute-start.1) | collective-permute-done | bytes 262176 | tf_op jit(solution)/shard_map/ppermute | solution.py:35
  13.2 1.1 %shard_map.106 = (f32[512,512]{1,0:T(8,128)S(1)}, f32[136,512]{1,0:T(8,128)S(1)}, f32[136,512]{1,0:T(8,128)S(1)}, f32[136,512]{1,0:T(8,128)S(1)}, f32[136,512]{1,0:T(8,128)S(1)}, /*index=5*/f32[8,512]{1,0:T(8,128)S(1)}) custom-call(bf16[512,1536]{1,0:T(8,128)(2,1)S(1)} %get-tuple-element.70.matrix, f32[128,512]{1,0:T(8,128)S(1)} %get-tuple-element.133.right, ...), custom_call_target="tpu_custom_call" | custom-call | flops 805306368 | bytes 2686976 | tf_op jit(solution)/shard_map/pallas_call | solution.py:22
  14.4 2.4 %collective-permute-start.3 = (f32[136,512]{1,0:T(8,128)S(1)}, f32[136,512]{1,0:T(8,128)S(1)}, u32[]{:S(2)}, u32[]{:S(2)}) collective-permute-start(f32[136,512]{1,0:T(8,128)S(1)} %get-tuple-element.81.fourth), channel_id=1, source_target_pairs={{0,24},{8,16},{16,8},{24,0},{1,25},{9,17},{17,9},{25,1},{2,26},{10... | collective-permute-start | bytes 835592 | tf_op jit(solution)/shard_map/ppermute | solution.py:35
  16.8 1.7 %collective-permute-start.5 = (f32[136,512]{1,0:T(8,128)S(1)}, f32[136,512]{1,0:T(8,128)S(1)}, u32[]{:S(2)}, u32[]{:S(2)}) collective-permute-start(f32[136,512]{1,0:T(8,128)S(1)} %get-tuple-element.84.refs_1_), channel_id=1, source_target_pairs={{0,7},{1,2},{2,1},{3,4},{4,3},{5,6},{6,5},{7,0},{8,15},{9,10},{10,... | collective-permute-start | bytes 835592 | tf_op jit(solution)/shard_map/ppermute | solution.py:35
  19.2 9.2 %all_gather.3.labels = f32[64,128]{1,0:T(8,128)S(1)} all-gather(f32[8,128]{1,0:T(8,128)S(1)} %shard_map.107), channel_id=1, replica_groups=mesh['grp'=4,'sub'=8] {'sub'}, dimensions={0}, use_global_device_ids=true | all-gather | bytes 36864 | tf_op jit(solution)/shard_map/all_gather | solution.py:526
  28.5 0.4 shard_map.108.table
  28.9 1.0 %collective-permute-done.3.far_one.refs_1_ = f32[136,512]{1,0:T(8,128)S(1)} collective-permute-done((f32[136,512]{1,0:T(8,128)S(1)}, f32[136,512]{1,0:T(8,128)S(1)}, u32[]{:S(2)}, u32[]{:S(2)}) %collective-permute-start.3) | collective-permute-done | bytes 278560 | tf_op jit(solution)/shard_map/ppermute | solution.py:35
  30.0 1.2 %shard_map.110 = (f32[512,512]{1,0:T(8,128)S(1)}, f32[128,512]{1,0:T(8,128)S(1)}, f32[128,512]{1,0:T(8,128)S(1)}, f32[128,512]{1,0:T(8,128)S(1)}, f32[128,512]{1,0:T(8,128)S(1)}, /*index=5*/f32[32,512]{1,0:T(8,128)S(1)}) custom-call(bf16[512,1536]{1,0:T(8,128)(2,1)S(1)} %shard_map.105.matrix, bf16[24,1536]{1,0:T(8,128)(2,1)S(1)} %get-tuple-element.69.flat, ...), custom_call_target="tpu_custom_call" | custom-call | flops 805306368 | bytes 4087808 | tf_op jit(solution)/shard_map/pallas_call | solution.py:22
  31.2 1.3 %collective-permute-start.13 = (f32[128,512]{1,0:T(8,128)S(1)}, f32[128,512]{1,0:T(8,128)S(1)}, u32[]{:S(2)}, u32[]{:S(2)}) collective-permute-start(f32[128,512]{1,0:T(8,128)S(1)} %get-tuple-element.95.refs_6_), channel_id=1, source_target_pairs={{0,8},{8,0},{16,24},{24,16},{1,9},{9,1},{17,25},{25,17},{2,10},{10... | collective-permute-start | bytes 786440 | tf_op jit(solution)/shard_map/ppermute | solution.py:35
  32.5 1.7 %collective-permute-start.14 = (f32[128,512]{1,0:T(8,128)S(1)}, f32[128,512]{1,0:T(8,128)S(1)}, u32[]{:S(2)}, u32[]{:S(2)}) collective-permute-start(f32[128,512]{1,0:T(8,128)S(1)} %get-tuple-element.96.refs_7_), channel_id=1, source_target_pairs={{0,24},{8,16},{16,8},{24,0},{1,25},{9,17},{17,9},{25,1},{2,26},{10... | collective-permute-start | bytes 786440 | tf_op jit(solution)/shard_map/ppermute | solution.py:35
  34.2 2.5 %collective-permute-start.8 = (f32[32,512]{1,0:T(8,128)S(1)}, f32[32,512]{1,0:T(8,128)S(1)}, u32[]{:S(2)}, u32[]{:S(2)}) collective-permute-start(f32[32,512]{1,0:T(8,128)S(1)} %get-tuple-element.88.refs_0_), channel_id=1, source_target_pairs={{0,6},{1,7},{2,4},{3,5},{4,2},{5,3},{6,0},{7,1},{8,14},{9,15},{10,... | collective-permute-start | bytes 196616 | tf_op jit(solution)/shard_map/ppermute | solution.py:35
  36.7 0.5 collective-permute-start.7
  37.2 0.5 collective-permute-start.6
  37.7 1.9 %collective-permute-done.8.refs_3_ = f32[32,512]{1,0:T(8,128)S(1)} collective-permute-done((f32[32,512]{1,0:T(8,128)S(1)}, f32[32,512]{1,0:T(8,128)S(1)}, u32[]{:S(2)}, u32[]{:S(2)}) %collective-permute-start.8) | collective-permute-done | bytes 65568 | tf_op jit(solution)/shard_map/ppermute | solution.py:35
  39.6 1.4 %collective-permute-done.7.refs_2_ = f32[32,512]{1,0:T(8,128)S(1)} collective-permute-done((f32[32,512]{1,0:T(8,128)S(1)}, f32[32,512]{1,0:T(8,128)S(1)}, u32[]{:S(2)}, u32[]{:S(2)}) %collective-permute-start.7) | collective-permute-done | bytes 65568 | tf_op jit(solution)/shard_map/ppermute | solution.py:35
  41.0 0.4 collective-permute-done.6.refs_1_
  42.0 0.5 collective-permute-start.17
  42.5 1.4 %collective-permute-start.18 = (f32[128,512]{1,0:T(8,128)S(1)}, f32[128,512]{1,0:T(8,128)S(1)}, u32[]{:S(2)}, u32[]{:S(2)}) collective-permute-start(f32[128,512]{1,0:T(8,128)S(1)} %get-tuple-element.105.refs_1_), channel_id=1, source_target_pairs={{0,7},{1,2},{2,1},{3,4},{4,3},{5,6},{6,5},{7,0},{8,15},{9,10},{10,... | collective-permute-start | bytes 786440 | tf_op jit(solution)/shard_map/ppermute | solution.py:35
  44.0 0.4 shard_map.111
  44.4 0.9 %collective-permute-done.14.refs_8_ = f32[128,512]{1,0:T(8,128)S(1)} collective-permute-done((f32[128,512]{1,0:T(8,128)S(1)}, f32[128,512]{1,0:T(8,128)S(1)}, u32[]{:S(2)}, u32[]{:S(2)}) %collective-permute-start.14) | collective-permute-done | bytes 262176 | tf_op jit(solution)/shard_map/ppermute | solution.py:35
  45.3 1.8 %collective-permute-start.16 = (f32[32,512]{1,0:T(8,128)S(1)}, f32[32,512]{1,0:T(8,128)S(1)}, u32[]{:S(2)}, u32[]{:S(2)}) collective-permute-start(f32[32,512]{1,0:T(8,128)S(1)} %get-tuple-element.98.refs_3_), channel_id=1, source_target_pairs={{0,24},{8,16},{16,8},{24,0},{1,25},{9,17},{17,9},{25,1},{2,26},{10... | collective-permute-start | bytes 196616 | tf_op jit(solution)/shard_map/ppermute | solution.py:35
  47.7 3.7 %collective-permute-done.16.refs_5_ = f32[32,512]{1,0:T(8,128)S(1)} collective-permute-done((f32[32,512]{1,0:T(8,128)S(1)}, f32[32,512]{1,0:T(8,128)S(1)}, u32[]{:S(2)}, u32[]{:S(2)}) %collective-permute-start.16) | collective-permute-done | bytes 65568 | tf_op jit(solution)/shard_map/ppermute | solution.py:35
  51.4 0.5 collective-permute-done.15.refs_4_
  52.3 1.0 %shard_map.116 = (f32[512,512]{1,0:T(8,128)S(1)}, f32[128,512]{1,0:T(8,128)S(1)}, f32[128,512]{1,0:T(8,128)S(1)}, f32[136,512]{1,0:T(8,128)S(1)}, f32[128,512]{1,0:T(8,128)S(1)}) custom-call(bf16[512,1536]{1,0:T(8,128)(2,1)S(1)} %get-tuple-element.70.matrix, f32[512,512]{1,0:T(8,128)S(1)} %shard_map.113.refs_0_.extra, ...), custom_call_target="tpu_custom_call" | custom-call | flops 805306368 | bytes 4997120 | tf_op jit(solution)/shard_map/pallas_call | solution.py:22
  53.4 2.1 %collective-permute-start.19 = (f32[128,512]{1,0:T(8,128)S(1)}, f32[128,512]{1,0:T(8,128)S(1)}, u32[]{:S(2)}, u32[]{:S(2)}) collective-permute-start(f32[128,512]{1,0:T(8,128)S(1)} %get-tuple-element.108.fourth), channel_id=1, source_target_pairs={{0,24},{8,16},{16,8},{24,0},{1,25},{9,17},{17,9},{25,1},{2,26},{10... | collective-permute-start | bytes 786440 | tf_op jit(solution)/shard_map/ppermute | solution.py:35
  55.4 2.3 %collective-permute-start.22 = (f32[128,512]{1,0:T(8,128)S(1)}, f32[128,512]{1,0:T(8,128)S(1)}, u32[]{:S(2)}, u32[]{:S(2)}) collective-permute-start(f32[128,512]{1,0:T(8,128)S(1)} %get-tuple-element.116.refs_5_), channel_id=1, source_target_pairs={{0,7},{1,2},{2,1},{3,4},{4,3},{5,6},{6,5},{7,0},{8,15},{9,10},{10,... | collective-permute-start | bytes 786440 | tf_op jit(solution)/shard_map/ppermute | solution.py:35
  57.7 8.9 %collective-permute-done.19.far_one = f32[128,512]{1,0:T(8,128)S(1)} collective-permute-done((f32[128,512]{1,0:T(8,128)S(1)}, f32[128,512]{1,0:T(8,128)S(1)}, u32[]{:S(2)}, u32[]{:S(2)}) %collective-permute-start.19) | collective-permute-done | bytes 262176 | tf_op jit(solution)/shard_map/ppermute | solution.py:35
  66.6 0.5 shard_map.117
  67.1 1.4 %shard_map.118 = (f32[512,512]{1,0:T(8,128)S(1)}, f32[512,512]{1,0:T(8,128)S(1)}, f32[128,512]{1,0:T(8,128)S(1)}, f32[128,512]{1,0:T(8,128)S(1)}, f32[512,512]{1,0:T(8,128)S(1)}, /*index=5*/f32[32,512]{1,0:T(8,128)S(1)}) custom-call(bf16[512,1536]{1,0:T(8,128)(2,1)S(1)} %shard_map.105.matrix, bf16[24,1536]{1,0:T(8,128)(2,1)S(1)} %get-tuple-element.69.flat, ...), custom_call_target="tpu_custom_call" | custom-call | flops 805306368 | bytes 7708672 | tf_op jit(solution)/shard_map/pallas_call | solution.py:22
  68.5 2.6 %collective-permute-start.25 = (f32[32,512]{1,0:T(8,128)S(1)}, f32[32,512]{1,0:T(8,128)S(1)}, u32[]{:S(2)}, u32[]{:S(2)}) collective-permute-start(f32[32,512]{1,0:T(8,128)S(1)} %get-tuple-element.125.refs_0_), channel_id=1, source_target_pairs={{0,6},{1,7},{2,4},{3,5},{4,2},{5,3},{6,0},{7,1},{8,14},{9,15},{10,... | collective-permute-start | bytes 196616 | tf_op jit(solution)/shard_map/ppermute | solution.py:35
  71.1 0.8 collective-permute-start.24
  72.1 1.7 %collective-permute-start.30 = (f32[128,512]{1,0:T(8,128)S(1)}, f32[128,512]{1,0:T(8,128)S(1)}, u32[]{:S(2)}, u32[]{:S(2)}) collective-permute-start(f32[128,512]{1,0:T(8,128)S(1)} %get-tuple-element.127), channel_id=1, source_target_pairs={{0,7},{1,0},{2,1},{3,2},{4,3},{5,4},{6,5},{7,6},{8,15},{9,8},{10,9... | collective-permute-start | bytes 786440 | tf_op jit(solution)/shard_map/ppermute | solution.py:35
  73.8 1.8 %collective-permute-start.31 = (f32[128,512]{1,0:T(8,128)S(1)}, f32[128,512]{1,0:T(8,128)S(1)}, u32[]{:S(2)}, u32[]{:S(2)}) collective-permute-start(f32[128,512]{1,0:T(8,128)S(1)} %get-tuple-element.128), channel_id=1, source_target_pairs={{0,24},{8,0},{16,8},{24,16},{1,25},{9,1},{17,9},{25,17},{2,26},{10... | collective-permute-start | bytes 786440 | tf_op jit(solution)/shard_map/ppermute | solution.py:35
  75.5 0.5 collective-permute-start.28
  76.2 0.6 collective-permute-done.29.refs_7_
  76.9 0.5 collective-permute-done.27.refs_5_
  77.4 0.4 shard_map.121
  77.8 1.8 %collective-permute-start.33 = (f32[32,512]{1,0:T(8,128)S(1)}, f32[32,512]{1,0:T(8,128)S(1)}, u32[]{:S(2)}, u32[]{:S(2)}) collective-permute-start(f32[32,512]{1,0:T(8,128)S(1)} %get-tuple-element.129), channel_id=1, source_target_pairs={{0,24},{8,16},{16,8},{24,0},{1,25},{9,17},{17,9},{25,1},{2,26},{10... | collective-permute-start | bytes 196616 | tf_op jit(solution)/shard_map/ppermute | solution.py:35
  79.6 0.4 collective-permute-start.32
  80.0 2.2 %collective-permute-start.34 = (f32[8,512]{1,0:T(8,128)S(1)}, f32[8,512]{1,0:T(8,128)S(1)}, u32[]{:S(2)}, u32[]{:S(2)}) collective-permute-start(f32[8,512]{1,0:T(8,128)S(1)} %slice.20.refs_13_), channel_id=1, source_target_pairs={{0,16},{8,24},{16,0},{24,8},{1,17},{9,25},{17,1},{25,9},{2,18},{10... | collective-permute-start | bytes 49160 | tf_op jit(solution)/shard_map/ppermute | solution.py:35
  82.8 2.1 %collective-permute-done.34.refs_14_ = f32[8,512]{1,0:T(8,128)S(1)} collective-permute-done((f32[8,512]{1,0:T(8,128)S(1)}, f32[8,512]{1,0:T(8,128)S(1)}, u32[]{:S(2)}, u32[]{:S(2)}) %collective-permute-start.34) | collective-permute-done | bytes 16416 | tf_op jit(solution)/shard_map/ppermute | solution.py:35
  85.2 1.3 %shard_map.123 = (f32[256,512]{1,0:T(8,128)}, f32[256,512]{1,0:T(8,128)}) custom-call(f32[256,512]{1,0:T(8,128)S(1)} %get-tuple-element.118.refs_0_, f32[256,512]{1,0:T(8,128)S(1)} %get-tuple-element.119.refs_1_, f32[256,512]{1,0:T(8,128)S(1)} %get-tuple-element.122.refs_2_, f32[256,512]{1,0:T(8,128)S(1)} %get-tuple-element.123.refs_3_, ...), custom_call_target="tpu_custom_call" | custom-call | bytes 4440064 | tf_op jit(solution)/shard_map/pallas_call | solution.py:22
  (59 shorter events, 3.3 us)
Async XLA Ops:
  0.6 4.2 %copy-start = (f32[1,1,512,512]{3,2,1,0:T(8,128)S(1)}, f32[1,1,512,512]{3,2,1,0:T(8,128)}, u32[]{:S(2)}) copy-start(f32[1,1,512,512]{3,2,1,0:T(8,128)} %param.10) | copy-start | bytes 3145732
  1.8 11.4 %collective-permute-start.1 = (f32[128,512]{1,0:T(8,128)S(1)}, f32[128,512]{1,0:T(8,128)S(1)}, u32[]{:S(2)}, u32[]{:S(2)}) collective-permute-start(f32[128,512]{1,0:T(8,128)S(1)} %get-tuple-element.132.upper), channel_id=1, source_target_pairs={{0,8},{8,16},{16,24},{24,0},{1,9},{9,17},{17,25},{25,1},{2,10},{10... | collective-permute-start | bytes 786440 | tf_op jit(solution)/shard_map/ppermute | solution.py:35
  4.9 8.3 %collective-permute-start = (f32[128,512]{1,0:T(8,128)S(1)}, f32[128,512]{1,0:T(8,128)S(1)}, u32[]{:S(2)}, u32[]{:S(2)}) collective-permute-start(f32[128,512]{1,0:T(8,128)S(1)} %get-tuple-element.133.right), channel_id=1, source_target_pairs={{0,1},{1,2},{2,3},{3,4},{4,5},{5,6},{6,7},{7,0},{8,9},{9,10},{10,1... | collective-permute-start | bytes 786440 | tf_op jit(solution)/shard_map/ppermute | solution.py:35
  4.9 0.7 copy-start.1
  5.6 0.7 copy-start.2
  6.2 1.4 %copy-start.5 = (f32[1,1,512,512]{3,2,1,0:T(8,128)S(1)}, f32[1,1,512,512]{3,2,1,0:T(8,128)}, u32[]{:S(2)}) copy-start(f32[1,1,512,512]{3,2,1,0:T(8,128)} %param.11) | copy-start | bytes 3145732
  6.2 1.4 %copy-start.6 = (f32[1,1,512,24]{2,3,1,0:T(8,128)S(1)}, f32[1,1,512,24]{2,3,1,0:T(8,128)}, u32[]{:S(2)}) copy-start(f32[1,1,512,24]{2,3,1,0:T(8,128)} %param.12) | copy-start | bytes 147460
  9.4 9.8 %copy-start.3 = (f32[1,1,24]{2,1,0:T(1,128)S(1)}, f32[1,1,24]{2,1,0:T(1,128)}, u32[]{:S(2)}) copy-start(f32[1,1,24]{2,1,0:T(1,128)} %param.13) | copy-start | bytes 292
  9.4 9.8 %copy-start.4 = (s32[1,1,24]{2,1,0:T(1,128)S(1)}, s32[1,1,24]{2,1,0:T(1,128)}, u32[]{:S(2)}) copy-start(s32[1,1,24]{2,1,0:T(1,128)} %param.14) | copy-start | bytes 292
  14.3 5.0 %collective-permute-start.2 = (f32[136,512]{1,0:T(8,128)S(1)}, f32[136,512]{1,0:T(8,128)S(1)}, u32[]{:S(2)}, u32[]{:S(2)}) collective-permute-start(f32[136,512]{1,0:T(8,128)S(1)} %get-tuple-element.77.refs_0_), channel_id=1, source_target_pairs={{0,1},{1,0},{2,3},{3,2},{4,5},{5,4},{6,7},{7,6},{8,9},{9,8},{10,11... | collective-permute-start | bytes 835592 | tf_op jit(solution)/shard_map/ppermute | solution.py:35
  14.3 14.6 %collective-permute-start.4 = (f32[136,512]{1,0:T(8,128)S(1)}, f32[136,512]{1,0:T(8,128)S(1)}, u32[]{:S(2)}, u32[]{:S(2)}) collective-permute-start(f32[136,512]{1,0:T(8,128)S(1)} %get-tuple-element.80.third), channel_id=1, source_target_pairs={{0,8},{8,0},{16,24},{24,16},{1,9},{9,1},{17,25},{25,17},{2,10},{10... | collective-permute-start | bytes 835592 | tf_op jit(solution)/shard_map/ppermute | solution.py:35
  14.4 15.5 %collective-permute-start.3 = (f32[136,512]{1,0:T(8,128)S(1)}, f32[136,512]{1,0:T(8,128)S(1)}, u32[]{:S(2)}, u32[]{:S(2)}) collective-permute-start(f32[136,512]{1,0:T(8,128)S(1)} %get-tuple-element.81.fourth), channel_id=1, source_target_pairs={{0,24},{8,16},{16,8},{24,0},{1,25},{9,17},{17,9},{25,1},{2,26},{10... | collective-permute-start | bytes 835592 | tf_op jit(solution)/shard_map/ppermute | solution.py:35
  16.8 13.2 %collective-permute-start.5 = (f32[136,512]{1,0:T(8,128)S(1)}, f32[136,512]{1,0:T(8,128)S(1)}, u32[]{:S(2)}, u32[]{:S(2)}) collective-permute-start(f32[136,512]{1,0:T(8,128)S(1)} %get-tuple-element.84.refs_1_), channel_id=1, source_target_pairs={{0,7},{1,2},{2,1},{3,4},{4,3},{5,6},{6,5},{7,0},{8,15},{9,10},{10,... | collective-permute-start | bytes 835592 | tf_op jit(solution)/shard_map/ppermute | solution.py:35
  31.2 13.2 %collective-permute-start.13 = (f32[128,512]{1,0:T(8,128)S(1)}, f32[128,512]{1,0:T(8,128)S(1)}, u32[]{:S(2)}, u32[]{:S(2)}) collective-permute-start(f32[128,512]{1,0:T(8,128)S(1)} %get-tuple-element.95.refs_6_), channel_id=1, source_target_pairs={{0,8},{8,0},{16,24},{24,16},{1,9},{9,1},{17,25},{25,17},{2,10},{10... | collective-permute-start | bytes 786440 | tf_op jit(solution)/shard_map/ppermute | solution.py:35
  32.5 12.8 %collective-permute-start.14 = (f32[128,512]{1,0:T(8,128)S(1)}, f32[128,512]{1,0:T(8,128)S(1)}, u32[]{:S(2)}, u32[]{:S(2)}) collective-permute-start(f32[128,512]{1,0:T(8,128)S(1)} %get-tuple-element.96.refs_7_), channel_id=1, source_target_pairs={{0,24},{8,16},{16,8},{24,0},{1,25},{9,17},{17,9},{25,1},{2,26},{10... | collective-permute-start | bytes 786440 | tf_op jit(solution)/shard_map/ppermute | solution.py:35
  34.2 3.0 %collective-permute-start.9 = (f32[32,512]{1,0:T(8,128)S(1)}, f32[32,512]{1,0:T(8,128)S(1)}, u32[]{:S(2)}, u32[]{:S(2)}) collective-permute-start(f32[32,512]{1,0:T(8,128)S(1)} %get-tuple-element.88.refs_0_), channel_id=1, source_target_pairs={{0,1},{1,0},{2,3},{3,2},{4,5},{5,4},{6,7},{7,6},{8,9},{9,8},{10,11... | collective-permute-start | bytes 196616 | tf_op jit(solution)/shard_map/ppermute | solution.py:35
  34.2 5.4 %collective-permute-start.8 = (f32[32,512]{1,0:T(8,128)S(1)}, f32[32,512]{1,0:T(8,128)S(1)}, u32[]{:S(2)}, u32[]{:S(2)}) collective-permute-start(f32[32,512]{1,0:T(8,128)S(1)} %get-tuple-element.88.refs_0_), channel_id=1, source_target_pairs={{0,6},{1,7},{2,4},{3,5},{4,2},{5,3},{6,0},{7,1},{8,14},{9,15},{10,... | collective-permute-start | bytes 196616 | tf_op jit(solution)/shard_map/ppermute | solution.py:35
  36.7 4.4 %collective-permute-start.7 = (f32[32,512]{1,0:T(8,128)S(1)}, f32[32,512]{1,0:T(8,128)S(1)}, u32[]{:S(2)}, u32[]{:S(2)}) collective-permute-start(f32[32,512]{1,0:T(8,128)S(1)} %get-tuple-element.88.refs_0_), channel_id=1, source_target_pairs={{0,4},{1,5},{2,6},{3,7},{4,0},{5,1},{6,2},{7,3},{8,12},{9,13},{10,... | collective-permute-start | bytes 196616 | tf_op jit(solution)/shard_map/ppermute | solution.py:35
  37.2 4.3 %collective-permute-start.6 = (f32[32,512]{1,0:T(8,128)S(1)}, f32[32,512]{1,0:T(8,128)S(1)}, u32[]{:S(2)}, u32[]{:S(2)}) collective-permute-start(f32[32,512]{1,0:T(8,128)S(1)} %get-tuple-element.88.refs_0_), channel_id=1, source_target_pairs={{0,2},{1,3},{2,0},{3,1},{4,6},{5,7},{6,4},{7,5},{8,10},{9,11},{10,... | collective-permute-start | bytes 196616 | tf_op jit(solution)/shard_map/ppermute | solution.py:35
  39.6 2.4 %collective-permute-start.12 = (f32[32,512]{1,0:T(8,128)S(1)}, f32[32,512]{1,0:T(8,128)S(1)}, u32[]{:S(2)}, u32[]{:S(2)}) collective-permute-start(f32[32,512]{1,0:T(8,128)S(1)} %collective-permute-done.8.refs_3_), channel_id=1, source_target_pairs={{0,1},{1,0},{2,3},{3,2},{4,5},{5,4},{6,7},{7,6},{8,9},{9,8},{10,11... | collective-permute-start | bytes 196616 | tf_op jit(solution)/shard_map/ppermute | solution.py:35
  41.0 1.5 %collective-permute-start.11 = (f32[32,512]{1,0:T(8,128)S(1)}, f32[32,512]{1,0:T(8,128)S(1)}, u32[]{:S(2)}, u32[]{:S(2)}) collective-permute-start(f32[32,512]{1,0:T(8,128)S(1)} %collective-permute-done.7.refs_2_), channel_id=1, source_target_pairs={{0,1},{1,0},{2,3},{3,2},{4,5},{5,4},{6,7},{7,6},{8,9},{9,8},{10,11... | collective-permute-start | bytes 196616 | tf_op jit(solution)/shard_map/ppermute | solution.py:35
  41.5 2.5 %collective-permute-start.10 = (f32[32,512]{1,0:T(8,128)S(1)}, f32[32,512]{1,0:T(8,128)S(1)}, u32[]{:S(2)}, u32[]{:S(2)}) collective-permute-start(f32[32,512]{1,0:T(8,128)S(1)} %collective-permute-done.6.refs_1_), channel_id=1, source_target_pairs={{0,1},{1,0},{2,3},{3,2},{4,5},{5,4},{6,7},{7,6},{8,9},{9,8},{10,11... | collective-permute-start | bytes 196616 | tf_op jit(solution)/shard_map/ppermute | solution.py:35
  42.0 10.2 %collective-permute-start.17 = (f32[128,512]{1,0:T(8,128)S(1)}, f32[128,512]{1,0:T(8,128)S(1)}, u32[]{:S(2)}, u32[]{:S(2)}) collective-permute-start(f32[128,512]{1,0:T(8,128)S(1)} %get-tuple-element.104.refs_0_), channel_id=1, source_target_pairs={{0,1},{1,0},{2,3},{3,2},{4,5},{5,4},{6,7},{7,6},{8,9},{9,8},{10,11... | collective-permute-start | bytes 786440 | tf_op jit(solution)/shard_map/ppermute | solution.py:35
  42.5 9.8 %collective-permute-start.18 = (f32[128,512]{1,0:T(8,128)S(1)}, f32[128,512]{1,0:T(8,128)S(1)}, u32[]{:S(2)}, u32[]{:S(2)}) collective-permute-start(f32[128,512]{1,0:T(8,128)S(1)} %get-tuple-element.105.refs_1_), channel_id=1, source_target_pairs={{0,7},{1,2},{2,1},{3,4},{4,3},{5,6},{6,5},{7,0},{8,15},{9,10},{10,... | collective-permute-start | bytes 786440 | tf_op jit(solution)/shard_map/ppermute | solution.py:35
  45.3 6.2 %collective-permute-start.16 = (f32[32,512]{1,0:T(8,128)S(1)}, f32[32,512]{1,0:T(8,128)S(1)}, u32[]{:S(2)}, u32[]{:S(2)}) collective-permute-start(f32[32,512]{1,0:T(8,128)S(1)} %get-tuple-element.98.refs_3_), channel_id=1, source_target_pairs={{0,24},{8,16},{16,8},{24,0},{1,25},{9,17},{17,9},{25,1},{2,26},{10... | collective-permute-start | bytes 196616 | tf_op jit(solution)/shard_map/ppermute | solution.py:35
  47.0 5.0 %collective-permute-start.15 = (f32[32,512]{1,0:T(8,128)S(1)}, f32[32,512]{1,0:T(8,128)S(1)}, u32[]{:S(2)}, u32[]{:S(2)}) collective-permute-start(f32[32,512]{1,0:T(8,128)S(1)} %get-tuple-element.98.refs_3_), channel_id=1, source_target_pairs={{0,8},{8,0},{16,24},{24,16},{1,9},{9,1},{17,25},{25,17},{2,10},{10... | collective-permute-start | bytes 196616 | tf_op jit(solution)/shard_map/ppermute | solution.py:35
  53.3 13.3 %collective-permute-start.20 = (f32[136,512]{1,0:T(8,128)S(1)}, f32[136,512]{1,0:T(8,128)S(1)}, u32[]{:S(2)}, u32[]{:S(2)}) collective-permute-start(f32[136,512]{1,0:T(8,128)S(1)} %get-tuple-element.107.third), channel_id=1, source_target_pairs={{0,8},{8,0},{16,24},{24,16},{1,9},{9,1},{17,25},{25,17},{2,10},{10... | collective-permute-start | bytes 835592 | tf_op jit(solution)/shard_map/ppermute | solution.py:35
  53.4 13.2 %collective-permute-start.19 = (f32[128,512]{1,0:T(8,128)S(1)}, f32[128,512]{1,0:T(8,128)S(1)}, u32[]{:S(2)}, u32[]{:S(2)}) collective-permute-start(f32[128,512]{1,0:T(8,128)S(1)} %get-tuple-element.108.fourth), channel_id=1, source_target_pairs={{0,24},{8,16},{16,8},{24,0},{1,25},{9,17},{17,9},{25,1},{2,26},{10... | collective-permute-start | bytes 786440 | tf_op jit(solution)/shard_map/ppermute | solution.py:35
  55.4 11.6 %collective-permute-start.21 = (f32[128,512]{1,0:T(8,128)S(1)}, f32[128,512]{1,0:T(8,128)S(1)}, u32[]{:S(2)}, u32[]{:S(2)}) collective-permute-start(f32[128,512]{1,0:T(8,128)S(1)} %get-tuple-element.115.refs_4_), channel_id=1, source_target_pairs={{0,1},{1,0},{2,3},{3,2},{4,5},{5,4},{6,7},{7,6},{8,9},{9,8},{10,11... | collective-permute-start | bytes 786440 | tf_op jit(solution)/shard_map/ppermute | solution.py:35
  55.4 11.7 %collective-permute-start.22 = (f32[128,512]{1,0:T(8,128)S(1)}, f32[128,512]{1,0:T(8,128)S(1)}, u32[]{:S(2)}, u32[]{:S(2)}) collective-permute-start(f32[128,512]{1,0:T(8,128)S(1)} %get-tuple-element.116.refs_5_), channel_id=1, source_target_pairs={{0,7},{1,2},{2,1},{3,4},{4,3},{5,6},{6,5},{7,0},{8,15},{9,10},{10,... | collective-permute-start | bytes 786440 | tf_op jit(solution)/shard_map/ppermute | solution.py:35
  68.5 5.3 %collective-permute-start.26 = (f32[32,512]{1,0:T(8,128)S(1)}, f32[32,512]{1,0:T(8,128)S(1)}, u32[]{:S(2)}, u32[]{:S(2)}) collective-permute-start(f32[32,512]{1,0:T(8,128)S(1)} %get-tuple-element.125.refs_0_), channel_id=1, source_target_pairs={{0,1},{1,0},{2,3},{3,2},{4,5},{5,4},{6,7},{7,6},{8,9},{9,8},{10,11... | collective-permute-start | bytes 196616 | tf_op jit(solution)/shard_map/ppermute | solution.py:35
  68.5 7.0 %collective-permute-start.25 = (f32[32,512]{1,0:T(8,128)S(1)}, f32[32,512]{1,0:T(8,128)S(1)}, u32[]{:S(2)}, u32[]{:S(2)}) collective-permute-start(f32[32,512]{1,0:T(8,128)S(1)} %get-tuple-element.125.refs_0_), channel_id=1, source_target_pairs={{0,6},{1,7},{2,4},{3,5},{4,2},{5,3},{6,0},{7,1},{8,14},{9,15},{10,... | collective-permute-start | bytes 196616 | tf_op jit(solution)/shard_map/ppermute | solution.py:35
  71.1 4.5 %collective-permute-start.24 = (f32[32,512]{1,0:T(8,128)S(1)}, f32[32,512]{1,0:T(8,128)S(1)}, u32[]{:S(2)}, u32[]{:S(2)}) collective-permute-start(f32[32,512]{1,0:T(8,128)S(1)} %get-tuple-element.125.refs_0_), channel_id=1, source_target_pairs={{0,4},{1,5},{2,6},{3,7},{4,0},{5,1},{6,2},{7,3},{8,12},{9,13},{10,... | collective-permute-start | bytes 196616 | tf_op jit(solution)/shard_map/ppermute | solution.py:35
  71.9 4.3 %collective-permute-start.23 = (f32[32,512]{1,0:T(8,128)S(1)}, f32[32,512]{1,0:T(8,128)S(1)}, u32[]{:S(2)}, u32[]{:S(2)}) collective-permute-start(f32[32,512]{1,0:T(8,128)S(1)} %get-tuple-element.125.refs_0_), channel_id=1, source_target_pairs={{0,2},{1,3},{2,0},{3,1},{4,6},{5,7},{6,4},{7,5},{8,10},{9,11},{10,... | collective-permute-start | bytes 196616 | tf_op jit(solution)/shard_map/ppermute | solution.py:35
  72.1 13.2 %collective-permute-start.30 = (f32[128,512]{1,0:T(8,128)S(1)}, f32[128,512]{1,0:T(8,128)S(1)}, u32[]{:S(2)}, u32[]{:S(2)}) collective-permute-start(f32[128,512]{1,0:T(8,128)S(1)} %get-tuple-element.127), channel_id=1, source_target_pairs={{0,7},{1,0},{2,1},{3,2},{4,3},{5,4},{6,5},{7,6},{8,15},{9,8},{10,9... | collective-permute-start | bytes 786440 | tf_op jit(solution)/shard_map/ppermute | solution.py:35
  73.8 11.5 %collective-permute-start.31 = (f32[128,512]{1,0:T(8,128)S(1)}, f32[128,512]{1,0:T(8,128)S(1)}, u32[]{:S(2)}, u32[]{:S(2)}) collective-permute-start(f32[128,512]{1,0:T(8,128)S(1)} %get-tuple-element.128), channel_id=1, source_target_pairs={{0,24},{8,0},{16,8},{24,16},{1,25},{9,1},{17,9},{25,17},{2,26},{10... | collective-permute-start | bytes 786440 | tf_op jit(solution)/shard_map/ppermute | solution.py:35
  75.5 1.3 %collective-permute-start.29 = (f32[32,512]{1,0:T(8,128)S(1)}, f32[32,512]{1,0:T(8,128)S(1)}, u32[]{:S(2)}, u32[]{:S(2)}) collective-permute-start(f32[32,512]{1,0:T(8,128)S(1)} %collective-permute-done.25.refs_3_), channel_id=1, source_target_pairs={{0,1},{1,0},{2,3},{3,2},{4,5},{5,4},{6,7},{7,6},{8,9},{9,8},{10,11... | collective-permute-start | bytes 196616 | tf_op jit(solution)/shard_map/ppermute | solution.py:35
  75.5 1.4 %collective-permute-start.28 = (f32[32,512]{1,0:T(8,128)S(1)}, f32[32,512]{1,0:T(8,128)S(1)}, u32[]{:S(2)}, u32[]{:S(2)}) collective-permute-start(f32[32,512]{1,0:T(8,128)S(1)} %collective-permute-done.24.refs_2_), channel_id=1, source_target_pairs={{0,1},{1,0},{2,3},{3,2},{4,5},{5,4},{6,7},{7,6},{8,9},{9,8},{10,11... | collective-permute-start | bytes 196616 | tf_op jit(solution)/shard_map/ppermute | solution.py:35
  76.2 1.3 %collective-permute-start.27 = (f32[32,512]{1,0:T(8,128)S(1)}, f32[32,512]{1,0:T(8,128)S(1)}, u32[]{:S(2)}, u32[]{:S(2)}) collective-permute-start(f32[32,512]{1,0:T(8,128)S(1)} %collective-permute-done.23.refs_1_), channel_id=1, source_target_pairs={{0,1},{1,0},{2,3},{3,2},{4,5},{5,4},{6,7},{7,6},{8,9},{9,8},{10,11... | collective-permute-start | bytes 196616 | tf_op jit(solution)/shard_map/ppermute | solution.py:35
  77.8 7.1 %collective-permute-start.33 = (f32[32,512]{1,0:T(8,128)S(1)}, f32[32,512]{1,0:T(8,128)S(1)}, u32[]{:S(2)}, u32[]{:S(2)}) collective-permute-start(f32[32,512]{1,0:T(8,128)S(1)} %get-tuple-element.129), channel_id=1, source_target_pairs={{0,24},{8,16},{16,8},{24,0},{1,25},{9,17},{17,9},{25,1},{2,26},{10... | collective-permute-start | bytes 196616 | tf_op jit(solution)/shard_map/ppermute | solution.py:35
  79.6 5.6 %collective-permute-start.32 = (f32[32,512]{1,0:T(8,128)S(1)}, f32[32,512]{1,0:T(8,128)S(1)}, u32[]{:S(2)}, u32[]{:S(2)}) collective-permute-start(f32[32,512]{1,0:T(8,128)S(1)} %get-tuple-element.129), channel_id=1, source_target_pairs={{0,8},{8,0},{16,24},{24,16},{1,9},{9,1},{17,25},{25,17},{2,10},{10... | collective-permute-start | bytes 196616 | tf_op jit(solution)/shard_map/ppermute | solution.py:35
  80.0 4.9 %collective-permute-start.34 = (f32[8,512]{1,0:T(8,128)S(1)}, f32[8,512]{1,0:T(8,128)S(1)}, u32[]{:S(2)}, u32[]{:S(2)}) collective-permute-start(f32[8,512]{1,0:T(8,128)S(1)} %slice.20.refs_13_), channel_id=1, source_target_pairs={{0,16},{8,24},{16,0},{24,8},{1,17},{9,25},{17,1},{25,9},{2,18},{10... | collective-permute-start | bytes 49160 | tf_op jit(solution)/shard_map/ppermute | solution.py:35
